TPU v7x, 128 devices: a whole 4x4x4 slice. The times are simulated.
128 devices in a mesh: dp: 32 (over y, x_hi, z), mp: 4 (over x_lo, core).
Axes of the slice: x: 4 (x_hi: 2, x_lo: 2; x = x_hi * 2 + x_lo), y: 4, z: 4, core: 2. Of those that a mesh axis runs over, the one named last changes fastest.
Arguments:
- passages: bfloat16 [256, 128, 4096], P('dp'), may hold values from -6 to 6
- lengths: int32 [256], P('dp'), may hold values from 16 to 128, as said below
- owner: int32 [256], P('dp'), may hold values from 0 to 31, as said below
- enc_gain: float32 [4096], replicated, may hold values from 0.25 to 2.5
- final_gain: float32 [4096], replicated, may hold values from 0.25 to 2.5
- enc_wq: bfloat16 [4096, 2048], P('dp', 'mp'), may hold values from -2 to 2
- enc_wk: bfloat16 [4096, 2048], P('dp', 'mp'), may hold values from -0.09375 to 0.09375
- enc_wv: bfloat16 [4096, 2048], P('dp', 'mp'), may hold values from -0.09375 to 0.09375
- enc_wo: bfloat16 [2048, 4096], P('mp', 'dp'), may hold values from -0.125 to 0.125
- dec_wk: bfloat16 [4096, 2048], P('dp', 'mp'), may hold values from -0.09375 to 0.09375
- dec_wv: bfloat16 [4096, 2048], P('dp', 'mp'), may hold values from -0.09375 to 0.09375
- dec_query: bfloat16 [32, 32, 2048], P(None, None, 'mp'), may hold values from -3 to 3
Outputs:
- encoded: bfloat16 [256, 128, 4096], P('dp')
- context: bfloat16 [32, 32, 2048], P('dp', None, 'mp')
Inputs may be any that keep to these rules, and one draw needn't show every extreme that they name: `lengths`: every device's first passage has length 128. `owner`: each question owns exactly 8 passages, spread over the devices at random.
All inputs are finite; a program needn't handle non-finite values.
Results may differ from a plain program's by a relative error of at most 0.038.
Values may be sent and summed in bfloat16 or wider, within the bound.
No kernel may reach another device: no remote copies, remote signals or barrier semaphores. Data moves between devices by JAX's collectives and lax.ppermute only.
A program may use at most 128 MiB of HBM per device.

v0:
```python
import jax
import jax.numpy as jnp
from jax import lax
from jax.sharding import PartitionSpec as P

HD = 64


EPS = 1e-06
SCALE = 0.125


def rms_norm(values, gain_vec):
    return values * lax.rsqrt(jnp.mean(values * values, axis=-1, keepdims=True) + EPS) * gain_vec


def add_slice(source, weight_part):
    return jnp.dot(source, weight_part, preferred_element_type=jnp.float32)


def shards(
    passages,
    lengths,
    owner,
    enc_gain,
    final_gain,
    enc_wq,
    enc_wk,
    enc_wv,
    enc_wo,
    dec_wk,
    dec_wv,
    dec_query,
):
    pass_count, seq_len, width = passages.shape
    tok_rows = pass_count * seq_len
    local_cols = enc_wq.shape[1]
    local_heads = local_cols // HD
    floats = passages.reshape(tok_rows, width).astype(jnp.float32)
    normed = rms_norm(floats, enc_gain).astype(jnp.bfloat16)

    def add_normed(weight_part):
        return add_slice(normed, weight_part)

    query_acc = add_normed(lax.all_gather(enc_wq, "dp", axis=0, tiled=True))
    key_acc = add_normed(lax.all_gather(enc_wk, "dp", axis=0, tiled=True))
    value_acc = add_normed(lax.all_gather(enc_wv, "dp", axis=0, tiled=True))

    def by_heads(values):
        return values.astype(jnp.bfloat16).reshape(pass_count, seq_len, local_heads, HD)

    queries = by_heads(query_acc)
    keys_enc = by_heads(key_acc)
    values_enc = by_heads(value_acc)
    visible = lax.broadcasted_iota(jnp.int32, (pass_count, seq_len), 1) < lengths[:, None]
    scores = (
        jnp.einsum("pqhd,pkhd->phqk", queries, keys_enc, preferred_element_type=jnp.float32) * SCALE
    )
    expon = jnp.where(visible[:, None, None, :], jnp.exp(scores), 0.0)
    weights = (expon / jnp.sum(expon, axis=-1, keepdims=True)).astype(jnp.bfloat16)
    attended = jnp.einsum(
        "phqk,pkhd->pqhd", weights, values_enc, preferred_element_type=jnp.float32
    )
    attended = attended.astype(jnp.bfloat16).reshape(tok_rows, local_cols)
    partial_value = jnp.dot(
        attended,
        lax.all_gather(enc_wo, "dp", axis=1, tiled=True),
        preferred_element_type=jnp.float32,
    )
    summed = lax.psum(partial_value.astype(jnp.bfloat16), "mp").astype(jnp.float32)
    encoded = (floats + summed).astype(jnp.bfloat16)
    final = rms_norm(encoded.astype(jnp.float32), final_gain).astype(jnp.bfloat16)
    dkey_acc = add_slice(final, lax.all_gather(dec_wk, "dp", axis=0, tiled=True))
    dvalue_acc = add_slice(final, lax.all_gather(dec_wv, "dp", axis=0, tiled=True))
    dkeys = by_heads(dkey_acc)
    dvalues_wide = by_heads(dvalue_acc).astype(jnp.float32)
    question_count, dec_len, _ = dec_query.shape
    member = owner[:, None] == lax.broadcasted_iota(jnp.int32, (pass_count, question_count), 1)
    selector = member.astype(jnp.bfloat16)
    member_float = member.astype(jnp.float32)
    picked = jnp.dot(
        selector,
        dec_query.reshape(question_count, dec_len * local_cols),
        preferred_element_type=jnp.float32,
    )
    picked = picked.astype(jnp.bfloat16).reshape(pass_count, dec_len, local_heads, HD)
    dec_scores = (
        jnp.einsum("pthd,plhd->pthl", picked, dkeys, preferred_element_type=jnp.float32) * SCALE
    )
    dec_expon = jnp.where(visible[:, None, None, :], jnp.exp(dec_scores), 0.0)
    passage_total = jnp.sum(dec_expon, axis=-1)
    passage_numer = jnp.einsum(
        "pthl,plhd->pthd", dec_expon, dvalues_wide, precision=lax.Precision.HIGHEST
    )
    question_numer = jnp.einsum(
        "pq,pthd->qthd", member_float, passage_numer, precision=lax.Precision.HIGHEST
    )
    question_numer = question_numer.reshape(question_count, dec_len, local_cols)
    question_total = jnp.einsum(
        "pq,pth->qth", member_float, passage_total, precision=lax.Precision.HIGHEST
    )
    dp_count = lax.axis_size("dp")
    own_count = question_count // dp_count
    full_numer, full_total = (
        lax.psum(question_numer.astype(jnp.bfloat16), "dp").astype(jnp.float32),
        lax.psum(question_total.astype(jnp.bfloat16), "dp").astype(jnp.float32),
    )
    own_start = lax.axis_index("dp") * own_count
    own_numer = lax.dynamic_slice_in_dim(full_numer, own_start, own_count, 0)
    own_total = lax.dynamic_slice_in_dim(full_total, own_start, own_count, 0)
    shaped_numer = own_numer.reshape(own_count, dec_len, local_heads, HD)
    context = (
        (shaped_numer / own_total[..., None])
        .astype(jnp.bfloat16)
        .reshape(own_count, dec_len, local_cols)
    )
    return (encoded.reshape(pass_count, seq_len, width), context)


def solution(mesh):
    return jax.shard_map(
        shards,
        mesh=mesh,
        in_specs=(
            P("dp", None, None),
            P("dp"),
            P("dp"),
            P(),
            P(),
            P("dp", "mp"),
            P("dp", "mp"),
            P("dp", "mp"),
            P("mp", "dp"),
            P("dp", "mp"),
            P("dp", "mp"),
            P(None, None, "mp"),
        ),
        out_specs=(P("dp", None, None), P("dp", None, "mp")),
        check_vma=False,
    )
```

profile of v0, /device:TPU:0, one launch (start us, length us, event | category | flops | bytes accessed | tf_op | source)
XLA Modules:
  0.0 1066.7 jit_solution(7213230854905686124)
XLA Ops:
  10.0 5.1 fusion.3
  15.2 10.5 fusion.5
  25.7 68.4 %all-gather.9.cloned.1.call-done = bf16[4096,512]{1,0:T(8,128)(2,1)} async-done(((bf16[128,512]{1,0:T(8,128)(2,1)}), bf16[4096,512]{1,0:T(8,128)(2,1)}) %all-gather.9.cloned.1.call-update) | async-done | bytes 4194320 | tf_op jit(solution)/shard_map/all_gather | solution.py:45
  94.1 9.1 convolution_convert_fusion.4
  103.2 1.3 reshape.105
  104.5 72.1 %all-gather.11.cloned.1.call-done = bf16[4096,512]{1,0:T(8,128)(2,1)} async-done(((bf16[128,512]{1,0:T(8,128)(2,1)}), bf16[4096,512]{1,0:T(8,128)(2,1)}) %all-gather.11.cloned.1.call-update) | async-done | bytes 4194320 | tf_op jit(solution)/shard_map/all_gather | solution.py:46
  176.6 9.1 convolution_convert_fusion.3
  185.7 2.1 reshape.106
  187.7 71.4 %all-gather.7.cloned.1.call-done = bf16[4096,512]{1,0:T(8,128)(2,1)} async-done(((bf16[128,512]{1,0:T(8,128)(2,1)}), bf16[4096,512]{1,0:T(8,128)(2,1)}) %all-gather.7.cloned.1.call-update) | async-done | bytes 4194320 | tf_op jit(solution)/shard_map/all_gather | solution.py:47
  259.1 9.1 convolution_convert_fusion.5
  268.2 2.1 reshape.104
  270.3 3.2 fusion.7
  273.5 1.4 fusion.31
  275.7 76.8 %all-gather.13.cloned.1.call-done = bf16[512,4096]{1,0:T(8,128)(2,1)} async-done(((bf16[512,128]{1,0:T(8,128)(2,1)}), bf16[512,4096]{1,0:T(8,128)(2,1)}) %all-gather.13.cloned.1.call-update) | async-done | bytes 4194320 | tf_op jit(solution)/shard_map/all_gather | solution.py:67
  352.5 9.0 convolution_convert_fusion.1
  364.0 1.4 reshape.100
  365.4 152.9 %all-reduce.3.cloned.1.call-done = bf16[1024,4096]{1,0:T(8,128)(2,1)} async-done(((bf16[1024,4096]{1,0:T(8,128)(2,1)}), bf16[1024,4096]{1,0:T(8,128)(2,1)}) %all-reduce.3.cloned.1.call-update) | async-done | bytes 8388624 | tf_op jit(solution)/shard_map/psum | solution.py:70
  518.3 10.4 fusion
  528.7 74.1 %all-gather.17.cloned.1.call-done = bf16[4096,512]{1,0:T(8,128)(2,1)} async-done(((bf16[128,512]{1,0:T(8,128)(2,1)}), bf16[4096,512]{1,0:T(8,128)(2,1)}) %all-gather.17.cloned.1.call-update) | async-done | bytes 4194320 | tf_op jit(solution)/shard_map/all_gather | solution.py:73
  602.8 9.1 fusion.28
  611.9 2.1 reshape.108
  614.0 71.3 %all-gather.15.cloned.1.call-done = bf16[4096,512]{1,0:T(8,128)(2,1)} async-done(((bf16[128,512]{1,0:T(8,128)(2,1)}), bf16[4096,512]{1,0:T(8,128)(2,1)}) %all-gather.15.cloned.1.call-update) | async-done | bytes 4194320 | tf_op jit(solution)/shard_map/all_gather | solution.py:74
  685.2 9.1 fusion.25
  694.4 1.4 reshape.107
  695.7 3.1 fusion.64
  698.8 1.8 fusion.34
  700.5 2.6 convolution_convert_fusion.2
  703.2 0.8 copy.48
  704.0 2.1 convert_element_type.97
  706.4 181.1 %psum.23 = bf16[32,32,8]{1,0,2:T(8,128)(2,1)S(1)} all-reduce(bf16[32,32,8]{1,0,2:T(8,128)(2,1)S(1)} %convolution_convert_fusion.6), channel_id=1, replica_groups=mesh['dp'=32,'mp'=4] {'dp'}, use_global_device_ids=true, to_apply=%region_6.7 | all-reduce | flops 8192 | bytes 32768 | tf_op jit(solution)/shard_map/psum | solution.py:106
  887.8 170.2 %all-reduce.5.cloned.1.call-done = bf16[32,32,512]{2,1,0:T(8,128)(2,1)} async-done(((bf16[32,32,512]{2,1,0:T(8,128)(2,1)}), bf16[32,32,512]{2,1,0:T(8,128)(2,1)}) %all-reduce.5.cloned.1.call-update) | async-done | bytes 1048592 | tf_op jit(solution)/shard_map/psum | solution.py:105
  1058.0 1.4 divide_convert_fusion.6
  (39 shorter events, 6.6 us)
Async XLA Ops:
  7.2 87.0 %all-gather.9.cloned.1.call-start = ((), (), s32[]{:S(2)}) async-start(), calls=%async_computation.1 | async-start | bytes 4325376 | tf_op jit(solution)/shard_map/all_gather | solution.py:45
  7.9 168.7 %all-gather.11.cloned.1.call-start = ((), (), s32[]{:S(2)}) async-start(), calls=%async_computation.2 | async-start | bytes 4325376 | tf_op jit(solution)/shard_map/all_gather | solution.py:46
  8.6 250.5 %all-gather.7.cloned.1.call-start = ((), (), s32[]{:S(2)}) async-start(), calls=%async_computation | async-start | bytes 4325376 | tf_op jit(solution)/shard_map/all_gather | solution.py:47
  9.4 343.1 %all-gather.13.cloned.1.call-start = ((), (), s32[]{:S(2)}) async-start(), calls=%async_computation.3 | async-start | bytes 4325376 | tf_op jit(solution)/shard_map/all_gather | solution.py:67
  10.0 5.2 copy-start.5
  10.0 5.2 copy-start.2
  10.0 508.3 %all-reduce.3.cloned.1.call-start = ((), (), s32[]{:S(2)}) async-start(), calls=%async_computation.4 | async-start | bytes 16777216 | tf_op jit(solution)/shard_map/psum | solution.py:70
  270.3 3.3 copy-start
  361.5 1.6 copy-start.1
  361.5 2.2 copy-start.3
  361.5 241.2 %all-gather.17.cloned.1.call-start = ((), (), s32[]{:S(2)}) async-start(), calls=%async_computation.6 | async-start | bytes 4325376 | tf_op jit(solution)/shard_map/all_gather | solution.py:73
  362.1 323.2 %all-gather.15.cloned.1.call-start = ((), (), s32[]{:S(2)}) async-start(), calls=%async_computation.5 | async-start | bytes 4325376 | tf_op jit(solution)/shard_map/all_gather | solution.py:74
  362.8 695.2 %all-reduce.5.cloned.1.call-start = ((), (), s32[]{:S(2)}) async-start(), calls=%async_computation.7 | async-start | bytes 2097152 | tf_op jit(solution)/shard_map/psum | solution.py:105
  365.4 237.4 %copy-start.4 = (f32[4096]{0:T(1024)S(1)}, f32[4096]{0:T(1024)}, u32[]{:S(2)}) copy-start(f32[4096]{0:T(1024)} %param.16) | copy-start | bytes 49156
Sparse Core Ops, SparseCore 0:
  11.2 82.9 all-gather.8
  97.3 79.2 all-gather.10
  179.8 79.2 all-gather.6
  261.7 90.6 all-gather.12
  361.6 156.5 all-reduce.2
  521.3 81.4 all-gather.16
  605.9 79.2 all-gather.14
  706.2 351.7 all-reduce.4
where the time goes:
time: 1070 us
  waiting for transfers between devices  761 us (71%)
  blocking collectives  181 us (17%)
  matrix products  67.2 us (6%)
  other arithmetic  27.5 us (3%)
  local copies, waits for them, and re-layouts  14.7 us (1%)
  between operations  14.7 us (1%)
    psum x1, blocking collectives, shards(): lax.psum(question_total.astype(jnp.bfloat16), 'dp').astype(jnp.float32)  181 us
    psum x1, waiting for transfers between devices, shards(): lax.psum(question_numer.astype(jnp.bfloat16), 'dp').astype(jnp.float32)  170 us
    psum x1, waiting for transfers between devices, shards(): lax.psum(partial_value.astype(jnp.bfloat16), 'mp').astype(jnp.float32)  153 us
    all_gather x1, waiting for transfers between devices, shards(): lax.all_gather(enc_wo, 'dp', axis=1, tiled=True)  76.8 us
    all_gather x1, waiting for transfers between devices, shards(): lax.all_gather(dec_wk, 'dp', axis=0, tiled=True)  74.1 us
    all_gather x1, waiting for transfers between devices, shards(): key_acc = add_normed(lax.all_gather(enc_wk, 'dp', axis=0, tiled=True))  72.1 us
    all_gather x1, waiting for transfers between devices, shards(): value_acc = add_normed(lax.all_gather(enc_wv, 'dp', axis=0, tiled=True))  71.4 us
    all_gather x1, waiting for transfers between devices, shards(): lax.all_gather(dec_wv, 'dp', axis=0, tiled=True)  71.3 us
  transfers between devices with their start and end apart: 8, of which 8 were waited for; matrix products, arithmetic and copies ran while one was open for 7% of the time, Pallas kernels for 0%

commit v1 on v0

v1 whole, which is shorter than its diff:
```python
import jax
import jax.numpy as jnp
from jax import lax
from jax.sharding import Mesh, PartitionSpec as P

HD = 64

EPS = 1e-06
SCALE = 0.125
AXES = ("y", "xh", "z", "xl", "c")
SIZES = (4, 2, 4, 2, 2)
DP = ("y", "xh", "z")
MP = ("xl", "c")


def swap(values, axis):
    return lax.ppermute(values, axis, [(0, 1), (1, 0)])


def in_order(mine, other, axis):
    first = lax.axis_index(axis) == 0
    return jnp.where(first, mine, other), jnp.where(first, other, mine)


def gather_rows(parts):
    count, rows, cols = parts.shape
    lo, hi = in_order(parts, swap(parts, "xh"), "xh")
    both = jnp.stack([lo, hi])
    full = lax.all_gather(both, ("y", "z"), axis=0, tiled=False)
    full = full.reshape(4, 4, 2, count, rows, cols)
    return [full[:, :, :, i].transpose(0, 2, 1, 3, 4).reshape(-1, cols) for i in range(count)]


def shards(
    passages,
    lengths,
    owner,
    enc_gain,
    final_gain,
    enc_wq,
    enc_wk,
    enc_wv,
    enc_wo,
    dec_wk,
    dec_wv,
    dec_query,
):
    pass_count, seq_len, width = passages.shape
    tok_rows = pass_count * seq_len
    local_cols = enc_wq.shape[1]
    local_heads = local_cols // HD
    floats = passages.reshape(tok_rows, width).astype(jnp.float32)

    def rms_norm(values, gain_vec):
        return values * lax.rsqrt(jnp.mean(values * values, axis=-1, keepdims=True) + EPS) * gain_vec

    def mm(a, b):
        return jnp.dot(a, b, preferred_element_type=jnp.float32)

    normed = rms_norm(floats, enc_gain).astype(jnp.bfloat16)
    wq, wk, wv = gather_rows(jnp.stack([enc_wq, enc_wk, enc_wv]))
    wo_lo, wo_hi = in_order(enc_wo, swap(enc_wo, "xl"), "xl")
    wo_both = jnp.concatenate([wo_lo, wo_hi], axis=0)
    wo_x = jnp.stack(in_order(wo_both, swap(wo_both, "xh"), "xh"))
    wo_full = lax.all_gather(wo_x, ("y", "z"), axis=0, tiled=False)
    wo_full = wo_full.reshape(4, 4, 2, 2 * local_cols, -1).transpose(3, 0, 2, 1, 4).reshape(2 * local_cols, width)
    dwk, dwv = gather_rows(jnp.stack([dec_wk, dec_wv]))

    def by_heads(values):
        return values.astype(jnp.bfloat16).reshape(pass_count, seq_len, local_heads, HD)

    queries = by_heads(mm(normed, wq))
    keys_enc = by_heads(mm(normed, wk))
    values_enc = by_heads(mm(normed, wv))
    visible = lax.broadcasted_iota(jnp.int32, (pass_count, seq_len), 1) < lengths[:, None]
    scores = jnp.einsum("pqhd,pkhd->phqk", queries, keys_enc, preferred_element_type=jnp.float32) * SCALE
    expon = jnp.where(visible[:, None, None, :], jnp.exp(scores), 0.0)
    weights = (expon / jnp.sum(expon, axis=-1, keepdims=True)).astype(jnp.bfloat16)
    attended = jnp.einsum("phqk,pkhd->pqhd", weights, values_enc, preferred_element_type=jnp.float32)
    attended = attended.astype(jnp.bfloat16).reshape(tok_rows, local_cols)
    attended = jnp.concatenate(in_order(attended, swap(attended, "xl"), "xl"), axis=1)
    partial_value = mm(attended, wo_full).astype(jnp.bfloat16)
    summed = partial_value.astype(jnp.float32) + swap(partial_value, "c").astype(jnp.float32)
    encoded = (floats + summed).astype(jnp.bfloat16)
    final = rms_norm(encoded.astype(jnp.float32), final_gain).astype(jnp.bfloat16)
    dkeys = by_heads(mm(final, dwk))
    dvalues_wide = by_heads(mm(final, dwv)).astype(jnp.float32)
    question_count, dec_len, _ = dec_query.shape
    member = owner[:, None] == lax.broadcasted_iota(jnp.int32, (pass_count, question_count), 1)
    member_float = member.astype(jnp.float32)
    picked = dec_query[owner].reshape(pass_count, dec_len, local_heads, HD)
    dec_scores = jnp.einsum("pthd,plhd->pthl", picked, dkeys, preferred_element_type=jnp.float32) * SCALE
    dec_expon = jnp.where(visible[:, None, None, :], jnp.exp(dec_scores), 0.0)
    passage_total = jnp.sum(dec_expon, axis=-1)
    passage_numer = jnp.einsum("pthl,plhd->pthd", dec_expon, dvalues_wide, precision=lax.Precision.HIGHEST)
    question_numer = jnp.einsum("pq,pthd->qthd", member_float, passage_numer, precision=lax.Precision.HIGHEST)
    question_total = jnp.einsum("pq,pth->qth", member_float, passage_total, precision=lax.Precision.HIGHEST)
    numer_out = question_numer.reshape(question_count, dec_len, local_cols).astype(jnp.bfloat16)
    total_out = question_total.reshape(question_count, 1, dec_len * local_heads).astype(jnp.bfloat16)
    total_out = jnp.pad(total_out, ((0, 0), (0, 0), (0, local_cols - dec_len * local_heads)))
    sent = jnp.concatenate([numer_out, total_out], axis=1)
    came = lax.all_to_all(sent, DP, 0, 0, tiled=True).astype(jnp.float32)
    came = jnp.sum(came, axis=0)
    own_numer = came[:dec_len].reshape(dec_len, local_heads, HD)
    own_total = came[dec_len, : dec_len * local_heads].reshape(dec_len, local_heads, 1)
    context = (own_numer / own_total).astype(jnp.bfloat16).reshape(1, dec_len, local_cols)
    return (encoded.reshape(pass_count, seq_len, width), context)


def solution(mesh):
    fine = Mesh(mesh.devices.reshape(SIZES), AXES)
    row = P(DP, MP)
    return jax.shard_map(
        shards,
        mesh=fine,
        in_specs=(
            P(DP, None, None),
            P(DP),
            P(DP),
            P(),
            P(),
            row,
            row,
            row,
            P(MP, DP),
            row,
            row,
            P(None, None, MP),
        ),
        out_specs=(P(DP, None, None), P(DP, None, MP)),
        check_vma=False,
    )
```

time: 1070 us -> 361 us (0.34)
  waiting for transfers between devices: 761 us -> 124 us
  blocking collectives: 181 us -> 29.7 us
  local copies, waits for them, and re-layouts: 14.7 us -> 74.6 us
  starting transfers between devices: 0.52 us -> 13.1 us
    all_gather x6 -> x3, waiting for transfers between devices: 434 us -> 107 us  [the longest x2 91.3 us: gather_rows(): full = lax.all_gather(both, ('y', 'z'), axis=0, tiled=False)]
    psum x2 -> x0, waiting for transfers between devices: 323 us -> none  [the longest x1 170 us: shards(): lax.psum(question_numer.astype(jnp.bfloat16), 'dp').astype(jnp.float32)]
    psum x1 -> x0, blocking collectives: 181 us -> none  [shards(): lax.psum(question_total.astype(jnp.bfloat16), 'dp').astype(jnp.float32)]
    transpose x0 -> x8, local copies, waits for them, and re-layouts: none -> 44.6 us  [the longest x1 23.3 us: shards(): wo_full.reshape(4, 4, 2, 2 * local_cols, -1).transpose(3, 0, 2, 1, 4)]
    all_to_all x0 -> x1, blocking collectives: none -> 29.7 us  [shards(): came = lax.all_to_all(sent, DP, 0, 0, tiled=True).astype(jnp.float32)]
    ppermute x0 -> x6, waiting for transfers between devices: none -> 17 us  [swap(): return lax.ppermute(values, axis, [(0, 1), (1, 0)])]
    ppermute x0 -> x6, starting transfers between devices: none -> 13 us  [swap(): return lax.ppermute(values, axis, [(0, 1), (1, 0)])]
    dot_general x7 -> x6, matrix products: 54.7 us -> 54.4 us  [mm(): return jnp.dot(a, b, preferred_element_type=jnp.float32)]
  transfers between devices with their start and end apart: 8 -> 9, of which waited for: 8 -> 6; matrix products, arithmetic and copies ran while one was open for 7% -> 34% of each run, Pallas kernels for 0% -> 0%
where the time goes in v1:
time: 361 us; the launch traced here: 354 us
  waiting for transfers between devices  124 us (34%)
  local copies, waits for them, and re-layouts  74.6 us (21%)
  matrix products  66.8 us (19%)
  other arithmetic  31.8 us (9%)
  blocking collectives  29.7 us (8%)
  between operations  14.3 us (4%)
  starting transfers between devices  13.1 us (4%)
    all_gather x2, waiting for transfers between devices, gather_rows(): full = lax.all_gather(both, ('y', 'z'), axis=0, tiled=False)  91.3 us
    dot_general x6, matrix products, mm(): return jnp.dot(a, b, preferred_element_type=jnp.float32)  54.4 us
    all_to_all x1, blocking collectives, shards(): came = lax.all_to_all(sent, DP, 0, 0, tiled=True).astype(jnp.float32)  29.7 us
    transpose x1, local copies, waits for them, and re-layouts, shards(): wo_full.reshape(4, 4, 2, 2 * local_cols, -1).transpose(3, 0, 2, 1, 4)  23.3 us
    transpose x7, local copies, waits for them, and re-layouts, gather_rows(): full[:, :, :, i].transpose(0, 2, 1, 3, 4).reshape(-1, cols)  21.3 us
    reshape x5, local copies, waits for them, and re-layouts, by_heads(): values.astype(jnp.bfloat16).reshape(pass_count, seq_len, local_heads, HD)  17.5 us
    ppermute x6, waiting for transfers between devices, swap(): return lax.ppermute(values, axis, [(0, 1), (1, 0)])  17 us
    all_gather x1, waiting for transfers between devices, shards(): wo_full = lax.all_gather(wo_x, ('y', 'z'), axis=0, tiled=False)  15.5 us
  transfers between devices with their start and end apart: 9, of which 6 were waited for; matrix products, arithmetic and copies ran while one was open for 34% of the time, Pallas kernels for 0%

profile of v1, /device:TPU:0, one launch (start us, length us, event | category | flops | bytes accessed | tf_op | source)
XLA Modules:
  0.0 354.1 jit_solution(310930018859950913)
XLA Ops:
  8.4 3.2 collective-permute-start
  11.6 9.1 %collective-permute-done = bf16[3,128,512]{2,1,0:T(8,128)(2,1)S(1)} collective-permute-done((bf16[3,128,512]{2,1,0:T(8,128)(2,1)S(1)}, bf16[3,128,512]{2,1,0:T(8,128)(2,1)S(1)}, u32[]{:S(2)}, u32[]{:S(2)}) %collective-permute-start) | collective-permute-done | bytes 393248 | tf_op jit(solution)/shard_map/ppermute | solution.py:17
  24.7 3.3 collective-permute-done.2
  28.0 3.3 collective-permute-start.3
  31.4 4.7 %collective-permute-done.3 = bf16[1024,128]{1,0:T(8,128)(2,1)S(1)} collective-permute-done((bf16[1024,128]{1,0:T(8,128)(2,1)S(1)}, bf16[1024,128]{1,0:T(8,128)(2,1)S(1)}, u32[]{:S(2)}, u32[]{:S(2)}) %collective-permute-start.3) | collective-permute-done | bytes 262176 | tf_op jit(solution)/shard_map/ppermute | solution.py:17
  37.1 3.3 collective-permute-start.5
  40.4 5.2 %multiply_reduce_fusion = f32[8,128]{1,0:T(8,128)S(1)} fusion(bf16[8,128,4096]{2,1,0:T(8,128)(2,1)} %param.12), kind=kLoop, calls=%fused_computation.9 | loop fusion | flops 12581888 | bytes 8392704 | tf_op jit(solution)/shard_map/reduce_sum | solution.py:55
  45.6 10.6 %multiply_convert_fusion = bf16[8,128,4096]{2,1,0:T(8,128)(2,1)} fusion(bf16[8,128,4096]{2,1,0:T(8,128)(2,1)} %param.12, f32[4096]{0:T(1024)S(1)} %copy-done.6, f32[8,128]{1,0:T(8,128)S(1)} %add_rsqrt_fusion.1), kind=kLoop, calls=%fused_computation.8 | loop fusion | flops 16777216 | bytes 16797696 | tf_op jit(solution)/shard_map/convert_element_type | solution.py:60
  57.2 58.6 %all-gather.7.cloned.1.call-done = bf16[32,3,128,512]{3,2,1,0:T(8,128)(2,1)} async-done(((bf16[2,3,128,512]{3,2,1,0:T(8,128)(2,1)}), bf16[32,3,128,512]{3,2,1,0:T(8,128)(2,1)}) %all-gather.7.cloned.1.call-update) | async-done | bytes 12582928 | tf_op jit(solution)/shard_map/all_gather | solution.py:29
  115.8 7.9 %slice_bitcast_fusion.4 = (bf16[4,2,4,128,512]{4,3,1,2,0:T(8,128)(2,1)}, bf16[4,2,4,128,512]{4,3,1,2,0:T(8,128)(2,1)}, bf16[4,2,4,128,512]{4,3,1,2,0:T(8,128)(2,1)S(1)}) fusion(bf16[4,4,2,3,128,512]{5,4,3,2,1,0:T(8,128)(2,1)} %bitcast.99), kind=kLoop, calls=%fused_computation.15 | loop fusion | bytes 25165824 | tf_op jit(solution)/shard_map/transpose | solution.py:31
  124.1 8.1 %convolution_convert_fusion.3 = bf16[1024,512]{1,0:T(8,128)(2,1)} fusion(bf16[1024,4096]{1,0:T(8,128)(2,1)} %bitcast.105, bf16[4096,512]{1,0:T(8,128)(2,1)S(1)} %bitcast.112), kind=kOutput, calls=%fused_computation.42 | convolution fusion | flops 4295491584 | bytes 13631488 | tf_op jit(solution)/shard_map/dot_general | solution.py:58
  132.2 2.8 reshape.178
  135.0 2.7 copy.61
  137.7 8.1 %convolution_convert_fusion.2 = bf16[1024,512]{1,0:T(8,128)(2,1)} fusion(bf16[1024,4096]{1,0:T(8,128)(2,1)} %bitcast.106, bf16[4096,512]{1,0:T(8,128)(2,1)S(1)} %bitcast.113), kind=kOutput, calls=%fused_computation.41 | convolution fusion | flops 4295491584 | bytes 13631488 | tf_op jit(solution)/shard_map/dot_general | solution.py:58
  145.7 3.9 %reshape.179 = bf16[8,128,8,64]{3,2,1,0:T(8,128)(2,1)} reshape(bf16[1024,512]{1,0:T(8,128)(2,1)} %convolution_convert_fusion.2) | data formatting | bytes 2097152 | tf_op jit(solution)/shard_map/reshape | solution.py:70
  149.6 3.3 copy.57
  153.0 8.0 %convolution_convert_fusion.4 = bf16[1024,512]{1,0:T(8,128)(2,1)} fusion(bf16[1024,4096]{1,0:T(8,128)(2,1)} %bitcast.107, bf16[4096,512]{1,0:T(8,128)(2,1)S(1)} %bitcast.111), kind=kOutput, calls=%fused_computation.43 | convolution fusion | flops 4295491584 | bytes 13631488 | tf_op jit(solution)/shard_map/dot_general | solution.py:58
  161.0 3.9 %reshape.177 = bf16[8,128,8,64]{3,2,1,0:T(8,128)(2,1)} reshape(bf16[1024,512]{1,0:T(8,128)(2,1)} %convolution_convert_fusion.4) | data formatting | bytes 2097152 | tf_op jit(solution)/shard_map/reshape | solution.py:70
  164.9 3.2 fusion.4
  172.9 15.5 %all-gather.9.cloned.1.call-done = bf16[32,1024,128]{2,1,0:T(8,128)(2,1)} async-done(((bf16[2,1024,128]{2,1,0:T(8,128)(2,1)}), bf16[32,1024,128]{2,1,0:T(8,128)(2,1)}) %all-gather.9.cloned.1.call-update) | async-done | bytes 8388624 | tf_op jit(solution)/shard_map/all_gather | solution.py:65
  188.4 23.3 %copy.68 = bf16[1024,4,2,4,128]{0,4,3,2,1:T(8,128)(2,1)} copy(bf16[1024,4,2,4,128]{4,0,2,3,1:T(8,128)(2,1)} %bitcast.103) | data formatting | bytes 16777216 | tf_op jit(solution)/shard_map/transpose | solution.py:66
  211.9 14.7 %convolution_convert_fusion = bf16[1024,4096]{1,0:T(8,128)(2,1)} fusion(bf16[1024,4096]{0,1:T(8,128)(2,1)} %bitcast.108, bf16[1024,512]{0,1:T(8,128)(2,1)S(1)} %get-tuple-element.10, bf16[1024,512]{0,1:T(8,128)(2,1)S(1)} %get-tuple-element.9), kind=kOutput, calls=%fused_computation.10 | convolution fusion | flops 8598323200 | bytes 18874368 | tf_op jit(solution)/shard_map/dot_general | solution.py:58
  228.3 32.7 %all-gather.11.cloned.1.call-done = bf16[32,2,128,512]{3,2,1,0:T(8,128)(2,1)} async-done(((bf16[2,2,128,512]{3,2,1,0:T(8,128)(2,1)}), bf16[32,2,128,512]{3,2,1,0:T(8,128)(2,1)}) %all-gather.11.cloned.1.call-update) | async-done | bytes 8388624 | tf_op jit(solution)/shard_map/all_gather | solution.py:29
  261.0 3.9 %slice_bitcast_fusion.1 = (bf16[4,2,4,128,512]{4,3,1,2,0:T(8,128)(2,1)S(1)}, bf16[4,2,4,128,512]{4,3,1,2,0:T(8,128)(2,1)S(1)}) fusion(bf16[4,4,2,2,128,512]{5,4,3,2,1,0:T(8,128)(2,1)} %bitcast.104), kind=kLoop, calls=%fused_computation.12 | loop fusion | bytes 16777216 | tf_op jit(solution)/shard_map/transpose | solution.py:31
  270.1 8.4 %fusion = (f32[1024]{0:T(1024)S(1)}, bf16[1024,4096]{1,0:T(8,128)(2,1)S(1)}) fusion(bf16[1024,4096]{1,0:T(8,128)(2,1)} %collective-permute-done.4, bf16[1024,4096]{1,0:T(8,128)(2,1)} %convolution_convert_fusion, bf16[8,128,4096]{2,1,0:T(8,128)(2,1)S(1)} %bitcast.98), kind=kLoop, calls=%fused_computation.3 | loop fusion | flops 37747712 | bytes 33558528 | tf_op jit(solution)/shard_map/reduce_sum | solution.py:55
  278.5 3.4 copy-done.1
  281.9 5.5 %fusion.26 = bf16[1024,512]{1,0:T(8,128)(2,1)} fusion(bf16[4096,512]{1,0:T(8,128)(2,1)S(1)} %bitcast.110, bf16[1024,4096]{1,0:T(8,128)(2,1)S(1)} %get-tuple-element.3, f32[4096]{0:T(1024)S(1)} %copy-done.8, f32[1024]{0:T(1024)S(1)} %add_rsqrt_fusion), kind=kOutput, calls=%fused_computation.39 | convolution fusion | flops 4312268800 | bytes 13651968 | tf_op jit(solution)/shard_map/dot_general | solution.py:58
  287.4 2.8 reshape.180
  290.2 10.1 %fusion.29 = bf16[1024,512]{1,0:T(8,128)(2,1)} fusion(bf16[4096,512]{1,0:T(8,128)(2,1)} %bitcast.109, bf16[1024,4096]{1,0:T(8,128)(2,1)} %copy-done.1, f32[4096]{0:T(1024)S(1)} %copy-done.8, f32[1024]{0:T(1024)S(1)} %add_rsqrt_fusion), kind=kOutput, calls=%fused_computation.40 | convolution fusion | flops 4312268800 | bytes 13651968 | tf_op jit(solution)/shard_map/dot_general | solution.py:58
  300.3 4.1 %reshape.181 = bf16[8,128,8,64]{3,2,1,0:T(8,128)(2,1)} reshape(bf16[1024,512]{1,0:T(8,128)(2,1)} %fusion.29) | data formatting | bytes 2097152 | tf_op jit(solution)/shard_map/reshape | solution.py:70
  304.4 3.1 fusion.64
  316.6 29.7 %all_to_all.5 = bf16[32,33,512]{2,1,0:T(8,128)(2,1)S(1)} all-to-all(bf16[32,33,512]{2,1,0:T(8,128)(2,1)S(1)} %fusion.50), channel_id=1, replica_groups=mesh['y'=4,'xh'=2,'z'=4,'xl'=2,'c'=2] {'y','xh','z'}, dimensions={0} | all-to-all | bytes 2162688 | tf_op jit(solution)/shard_map/all_to_all | solution.py:102
  (75 shorter events, 29.7 us)
Async XLA Ops:
  7.2 219.4 %copy-start = (bf16[32,32,512]{2,1,0:T(8,128)(2,1)S(1)}, bf16[32,32,512]{2,1,0:T(8,128)(2,1)}, u32[]{:S(2)}) copy-start(bf16[32,32,512]{2,1,0:T(8,128)(2,1)} %param.23) | copy-start | bytes 3145732
  7.2 15.7 %copy-start.5 = (bf16[512,128]{1,0:T(8,128)(2,1)S(1)}, bf16[512,128]{1,0:T(8,128)(2,1)}, u32[]{:S(2)}) copy-start(bf16[512,128]{1,0:T(8,128)(2,1)} %param.20) | copy-start | bytes 393220
  7.2 108.6 %all-gather.7.cloned.1.call-start = ((), (), s32[]{:S(2)}) async-start(), calls=%async_computation.1 | async-start | bytes 13369344 | tf_op jit(solution)/shard_map/all_gather | solution.py:29
  7.2 29.8 %copy-start.3 = (bf16[128,512]{1,0:T(8,128)(2,1)S(1)}, bf16[128,512]{1,0:T(8,128)(2,1)}, u32[]{:S(2)}) copy-start(bf16[128,512]{1,0:T(8,128)(2,1)} %param.22) | copy-start | bytes 393220
  7.2 29.8 %copy-start.4 = (bf16[128,512]{1,0:T(8,128)(2,1)S(1)}, bf16[128,512]{1,0:T(8,128)(2,1)}, u32[]{:S(2)}) copy-start(bf16[128,512]{1,0:T(8,128)(2,1)} %param.21) | copy-start | bytes 393220
  8.4 12.3 %collective-permute-start = (bf16[3,128,512]{2,1,0:T(8,128)(2,1)S(1)}, bf16[3,128,512]{2,1,0:T(8,128)(2,1)S(1)}, u32[]{:S(2)}, u32[]{:S(2)}) collective-permute-start(bf16[3,128,512]{2,1,0:T(8,128)(2,1)S(1)} %pad_maximum_fusion.3), channel_id=1, source_target_pairs={{0,16},{16,0},{1,17},{17,1},{2,18},{18,2},{3,19},{19,3},{4,20},{20... | collective-permute-start | bytes 1179656 | tf_op jit(solution)/shard_map/ppermute | solution.py:17
  22.9 165.5 %all-gather.9.cloned.1.call-start = ((), (), s32[]{:S(2)}) async-start(), calls=%async_computation.2 | async-start | bytes 8912896 | tf_op jit(solution)/shard_map/all_gather | solution.py:65
  22.9 5.0 %collective-permute-start.2 = (bf16[512,128]{1,0:T(8,128)(2,1)S(1)}, bf16[512,128]{1,0:T(8,128)(2,1)S(1)}, u32[]{:S(2)}, u32[]{:S(2)}) collective-permute-start(bf16[512,128]{1,0:T(8,128)(2,1)S(1)} %copy-done.5), channel_id=1, source_target_pairs={{0,2},{2,0},{1,3},{3,1},{4,6},{6,4},{5,7},{7,5},{8,10},{10,8},{9,1... | collective-permute-start | bytes 393224 | tf_op jit(solution)/shard_map/ppermute | solution.py:17
  28.0 8.0 %collective-permute-start.3 = (bf16[1024,128]{1,0:T(8,128)(2,1)S(1)}, bf16[1024,128]{1,0:T(8,128)(2,1)S(1)}, u32[]{:S(2)}, u32[]{:S(2)}) collective-permute-start(bf16[1024,128]{1,0:T(8,128)(2,1)S(1)} %pad_maximum_fusion.4), channel_id=1, source_target_pairs={{0,16},{16,0},{1,17},{17,1},{2,18},{18,2},{3,19},{19,3},{4,20},{20... | collective-permute-start | bytes 786440 | tf_op jit(solution)/shard_map/ppermute | solution.py:17
  37.0 224.0 %all-gather.11.cloned.1.call-start = ((), (), s32[]{:S(2)}) async-start(), calls=%async_computation.3 | async-start | bytes 8912896 | tf_op jit(solution)/shard_map/all_gather | solution.py:29
  37.1 8.5 %copy-start.6 = (f32[4096]{0:T(1024)S(1)}, f32[4096]{0:T(1024)}, u32[]{:S(2)}) copy-start(f32[4096]{0:T(1024)} %param.15) | copy-start | bytes 49156
  37.1 19.2 %collective-permute-start.5 = (bf16[2,128,512]{2,1,0:T(8,128)(2,1)S(1)}, bf16[2,128,512]{2,1,0:T(8,128)(2,1)S(1)}, u32[]{:S(2)}, u32[]{:S(2)}) collective-permute-start(bf16[2,128,512]{2,1,0:T(8,128)(2,1)S(1)} %pad_maximum_fusion.5), channel_id=1, source_target_pairs={{0,16},{16,0},{1,17},{17,1},{2,18},{18,2},{3,19},{19,3},{4,20},{20... | collective-permute-start | bytes 786440 | tf_op jit(solution)/shard_map/ppermute | solution.py:17
  45.6 10.6 %copy-start.9 = (s32[8]{0:T(128)S(1)}, s32[8]{0:T(128)}, u32[]{:S(2)}) copy-start(s32[8]{0:T(128)} %param.13) | copy-start | bytes 100
  164.9 3.2 copy-start.2
  171.5 40.1 %collective-permute-start.1 = (bf16[1024,512]{0,1:T(8,128)(2,1)}, bf16[1024,512]{0,1:T(8,128)(2,1)S(1)}, u32[]{:S(2)}, u32[]{:S(2)}) collective-permute-start(bf16[1024,512]{0,1:T(8,128)(2,1)} %bitcast.96), channel_id=1, source_target_pairs={{0,2},{2,0},{1,3},{3,1},{4,6},{6,4},{5,7},{7,5},{8,10},{10,8},{9,1... | collective-permute-start | bytes 3145736 | tf_op jit(solution)/shard_map/ppermute | solution.py:17
  211.8 14.7 %copy-start.7 = (s32[8]{0:T(128)S(1)}, s32[8]{0:T(128)}, u32[]{:S(2)}) copy-start(s32[8]{0:T(128)} %param.14) | copy-start | bytes 100
  226.6 41.5 %collective-permute-start.4 = (bf16[1024,4096]{1,0:T(8,128)(2,1)}, bf16[1024,4096]{1,0:T(8,128)(2,1)}, u32[]{:S(2)}, u32[]{:S(2)}) collective-permute-start(bf16[1024,4096]{1,0:T(8,128)(2,1)} %convolution_convert_fusion), channel_id=1, source_target_pairs={{0,1},{1,0},{2,3},{3,2},{4,5},{5,4},{6,7},{7,6},{8,9},{9,8},{10,11... | collective-permute-start | bytes 25165832 | tf_op jit(solution)/shard_map/ppermute | solution.py:17
  265.0 3.1 slice-start
  265.4 4.6 %slice-start.1 = ((s8[8388608]{0:T(1024)(128)(4,1)}), s8[4194304]{0:T(1024)(128)(4,1)S(1)}, s32[]{:S(2)}) async-start(s8[8388608]{0:T(1024)(128)(4,1)} %bitcast.97), calls=%async_computation.5 | async-start | bytes 8388608
  268.0 13.8 %copy-start.8 = (f32[4096]{0:T(1024)S(1)}, f32[4096]{0:T(1024)}, u32[]{:S(2)}) copy-start(f32[4096]{0:T(1024)} %param.16) | copy-start | bytes 49156
  278.5 3.4 copy-start.1
Sparse Core Ops, SparseCore 0:
  23.0 92.7 all-gather.6
  117.9 70.4 all-gather.8
  190.5 70.4 all-gather.10

commit v2 on v1

v2 whole, which is shorter than its diff:
```python
import functools

import jax
import jax.numpy as jnp
from jax import lax
from jax.experimental import pallas as pl
from jax.experimental.pallas import tpu as pltpu
from jax.sharding import Mesh, PartitionSpec as P

HD = 64
EPS = 1e-06
SCALE = 0.125
AXES = ("y", "xh", "z", "xl", "c")
NY, NXH, NZ, NXL, NC = 4, 2, 4, 2, 2
DP = ("y", "xh", "z")
MP = ("xl", "c")
SEQ = 128
PAIR = 2 * HD
HALVES = 2
VMEM = 52 * 1024 * 1024


def swap(values, axis):
    return lax.ppermute(values, axis, [(0, 1), (1, 0)])


def in_order(mine, other, axis):
    first = lax.axis_index(axis) == 0
    return jnp.where(first, mine, other), jnp.where(first, other, mine)


def anywhere():
    return pl.BlockSpec(memory_space=pl.ANY)


def in_smem():
    return pl.BlockSpec(memory_space=pltpu.SMEM)


def dp_blocks():
    for y in range(NY):
        for xh in range(NXH):
            for z in range(NZ):
                yield y, xh, z, (y * NXH + xh) * NZ + z


def project(rows_ref, weight_ref, out_ref, count, cols):
    wide = 256

    def step(i, _):
        which = i // (cols // wide)
        at = pl.multiple_of((i % (cols // wide)) * wide, wide)
        acc = jnp.dot(rows_ref[...], weight_ref[which, :, pl.ds(at, wide)], preferred_element_type=jnp.float32)
        out_ref[which, :, pl.ds(at, wide)] = acc.astype(out_ref.dtype)
        return 0

    lax.fori_loop(0, count * (cols // wide), step, 0)


def attend_kernel(half, tokens, lens_ref, normed_ref, weights_ref, out_ref, rows, weight, qkv, sem_a, sem_w):
    count, width, cols = weight.shape
    copy_rows = pltpu.make_async_copy(normed_ref.at[pl.ds(half * tokens, tokens)], rows, sem_a)
    copy_rows.start()
    for which in range(count):
        for y, xh, z, d in dp_blocks():
            pltpu.make_async_copy(
                weights_ref.at[y * NZ + z, xh, which], weight.at[which, pl.ds(d * SEQ, SEQ)], sem_w.at[which]
            ).start()
    copy_rows.wait()
    wide = 256
    for which in range(count):
        pltpu.make_async_copy(weight.at[which], weight.at[which], sem_w.at[which]).wait()

        def step(i, _, which=which):
            at = pl.multiple_of(i * wide, wide)
            acc = jnp.dot(rows[...], weight[which, :, pl.ds(at, wide)], preferred_element_type=jnp.float32)
            qkv[which, :, pl.ds(at, wide)] = acc.astype(jnp.bfloat16)
            return 0

        lax.fori_loop(0, cols // wide, step, 0)

    lane = lax.broadcasted_iota(jnp.int32, (1, PAIR), 1)
    low = (lane < HD).astype(jnp.bfloat16)
    high = (lane >= HD).astype(jnp.bfloat16)

    def one(p, _):
        at = pl.multiple_of(p * SEQ, SEQ)
        seen = lane < lens_ref[half * (tokens // SEQ) + p]
        for hp in range(cols // PAIR):
            here = slice(hp * PAIR, (hp + 1) * PAIR)
            q = qkv[0, pl.ds(at, SEQ), here]
            k = qkv[1, pl.ds(at, SEQ), here]
            v = qkv[2, pl.ds(at, SEQ), here]
            q_two = jnp.concatenate([q * low, q * high], axis=0)
            scores = lax.dot_general(q_two, k, (((1,), (1,)), ((), ())), preferred_element_type=jnp.float32) * SCALE
            expon = jnp.where(seen, jnp.exp(scores), 0.0)
            share = (expon / jnp.sum(expon, axis=-1, keepdims=True)).astype(jnp.bfloat16)
            both = jnp.dot(share, v, preferred_element_type=jnp.float32)
            out_ref[pl.ds(at, SEQ), here] = jnp.where(lane < HD, both[:SEQ], both[SEQ:]).astype(jnp.bfloat16)
        return 0

    lax.fori_loop(0, tokens // SEQ, one, 0)


def attend(half, lengths, normed, gathered):
    total, width = normed.shape
    tokens = total // HALVES
    cols = gathered.shape[-1]
    return pl.pallas_call(
        functools.partial(attend_kernel, half, tokens),
        out_shape=jax.ShapeDtypeStruct((tokens, cols), jnp.bfloat16),
        in_specs=[in_smem(), anywhere(), anywhere()],
        out_specs=pl.BlockSpec(memory_space=pltpu.VMEM),
        scratch_shapes=[
            pltpu.VMEM((tokens, width), jnp.bfloat16),
            pltpu.VMEM((3, width, cols), jnp.bfloat16),
            pltpu.VMEM((3, tokens, cols), jnp.bfloat16),
            pltpu.SemaphoreType.DMA,
            pltpu.SemaphoreType.DMA((3,)),
        ],
        compiler_params=pltpu.CompilerParams(vmem_limit_bytes=VMEM),
        cost_estimate=pl.CostEstimate(flops=2 * tokens * width * cols * 3, bytes_accessed=18 << 20, transcendentals=tokens * SEQ * 8),
    )(lengths, normed, gathered)


def output_kernel(where_ref, mine_ref, other_ref, weights_ref, out_ref, rows, weight, sem_a, sem_w):
    tokens, cols = mine_ref.shape
    xl = where_ref[0]
    mine_at = pl.multiple_of(xl * cols, cols)
    other_at = pl.multiple_of((1 - xl) * cols, cols)
    pltpu.make_async_copy(mine_ref, rows.at[:, pl.ds(mine_at, cols)], sem_a).start()
    pltpu.make_async_copy(other_ref, rows.at[:, pl.ds(other_at, cols)], sem_a).start()
    for y, xh, z, d in dp_blocks():
        pltpu.make_async_copy(
            weights_ref.at[y * NZ + z, xh], weight.at[:, pl.ds(d * SEQ, SEQ)], sem_w.at[y]
        ).start()
    pltpu.make_async_copy(rows, rows, sem_a).wait()
    part = weight.shape[1] // NY
    wide = 256
    for y in range(NY):
        quarter = weight.at[:, pl.ds(y * part, part)]
        pltpu.make_async_copy(quarter, quarter, sem_w.at[y]).wait()

        def step(i, _, y=y):
            at = pl.multiple_of(y * part + i * wide, wide)
            acc = jnp.dot(rows[...], weight[:, pl.ds(at, wide)], preferred_element_type=jnp.float32)
            out_ref[:, pl.ds(at, wide)] = acc.astype(jnp.bfloat16)
            return 0

        lax.fori_loop(0, part // wide, step, 0)


def output(where, mine, other, gathered, width):
    tokens, cols = mine.shape
    return pl.pallas_call(
        output_kernel,
        out_shape=jax.ShapeDtypeStruct((tokens, width), jnp.bfloat16),
        in_specs=[in_smem(), anywhere(), anywhere(), anywhere()],
        out_specs=pl.BlockSpec(memory_space=pltpu.VMEM),
        scratch_shapes=[
            pltpu.VMEM((tokens, 2 * cols), jnp.bfloat16),
            pltpu.VMEM((2 * cols, width), jnp.bfloat16),
            pltpu.SemaphoreType.DMA,
            pltpu.SemaphoreType.DMA((NY,)),
        ],
        compiler_params=pltpu.CompilerParams(vmem_limit_bytes=VMEM),
        cost_estimate=pl.CostEstimate(flops=4 * tokens * width * cols, bytes_accessed=13 << 20, transcendentals=0),
    )(where, mine, other, gathered)


def decode_kernel(
    half, has_prior, lens_ref, owner_ref, gain_ref, query_ref, passages_ref, mine_ref, other_ref, weights_ref, *rest
):
    if has_prior:
        rest = rest[1:]
    encoded_ref, numer_ref, final, weight, kv, sem_w = rest
    step = pl.program_id(0)
    steps = final.shape[0] // SEQ
    count, width, cols = weight.shape

    @pl.when(step == 0)
    def _():
        for which in range(count):
            for y, xh, z, d in dp_blocks():
                pltpu.make_async_copy(
                    weights_ref.at[y * NZ + z, xh, which], weight.at[which, pl.ds(d * SEQ, SEQ)], sem_w.at[which]
                ).start()

    floats = passages_ref[...].astype(jnp.float32)
    summed = mine_ref[...].astype(jnp.float32) + other_ref[...].astype(jnp.float32)
    encoded = (floats + summed).astype(jnp.bfloat16)
    encoded_ref[...] = encoded
    values = encoded.astype(jnp.float32)
    mean = jnp.mean(values * values, axis=-1, keepdims=True)
    final[pl.ds(pl.multiple_of(step * SEQ, SEQ), SEQ), :] = (
        values * lax.rsqrt(mean + EPS) * gain_ref[...]
    ).astype(jnp.bfloat16)

    @pl.when(step == steps - 1)
    def _():
        wide = 256
        for which in range(count):
            pltpu.make_async_copy(weight.at[which], weight.at[which], sem_w.at[which]).wait()

            def column(i, _, which=which):
                at = pl.multiple_of(i * wide, wide)
                acc = jnp.dot(final[...], weight[which, :, pl.ds(at, wide)], preferred_element_type=jnp.float32)
                kv[which, :, pl.ds(at, wide)] = acc.astype(jnp.bfloat16)
                return 0

            lax.fori_loop(0, cols // wide, column, 0)

        lane = lax.broadcasted_iota(jnp.int32, (1, PAIR), 1)
        low = (lane < HD).astype(jnp.bfloat16)
        high = (lane >= HD).astype(jnp.bfloat16)
        dec_len = query_ref.shape[1]

        def one(p, _):
            at = pl.multiple_of(p * SEQ, SEQ)
            seen = lane < lens_ref[half * steps + p]
            question = owner_ref[half * steps + p]
            totals = jnp.zeros((dec_len, PAIR), jnp.float32)
            for hp in range(cols // PAIR):
                here = slice(hp * PAIR, (hp + 1) * PAIR)
                q = query_ref[question, :, here]
                k = kv[0, pl.ds(at, SEQ), here]
                v = kv[1, pl.ds(at, SEQ), here]
                q_two = jnp.concatenate([q * low, q * high], axis=0)
                scores = lax.dot_general(q_two, k, (((1,), (1,)), ((), ())), preferred_element_type=jnp.float32) * SCALE
                expon = jnp.where(seen, jnp.exp(scores), 0.0)
                total = jnp.sum(expon, axis=-1, keepdims=True)
                coarse = expon.astype(jnp.bfloat16)
                fine = (expon - coarse.astype(jnp.float32)).astype(jnp.bfloat16)
                both = jnp.dot(coarse, v, preferred_element_type=jnp.float32) + jnp.dot(
                    fine, v, preferred_element_type=jnp.float32
                )
                numer_ref[p, :, here] = jnp.where(lane < HD, both[:dec_len], both[dec_len:])
                totals = jnp.where(lane == 2 * hp, total[:dec_len], totals)
                totals = jnp.where(lane == 2 * hp + 1, total[dec_len:], totals)
            numer_ref[p, :, cols : cols + PAIR] = totals
            return 0

        lax.fori_loop(0, steps, one, 0)


def decode(half, lengths, owner, gain, query, passages, mine, other, gathered, prior):
    tokens, width = mine.shape
    cols = gathered.shape[-1]
    steps = tokens // SEQ
    questions, dec_len, _ = query.shape
    block = (SEQ, width)
    in_specs = [
        in_smem(),
        in_smem(),
        pl.BlockSpec((1, width), lambda i: (0, 0)),
        pl.BlockSpec((questions, dec_len, cols), lambda i: (0, 0, 0)),
        pl.BlockSpec(block, lambda i: (half * steps + i, 0)),
        pl.BlockSpec(block, lambda i: (i, 0)),
        pl.BlockSpec(block, lambda i: (i, 0)),
        anywhere(),
    ]
    args = [lengths, owner, gain, query, passages, mine, other, gathered]
    aliases = {}
    if prior is not None:
        in_specs.append(anywhere())
        args.append(prior)
        aliases = {8: 0}
    return pl.pallas_call(
        functools.partial(decode_kernel, half, prior is not None),
        grid=(steps,),
        out_shape=(
            jax.ShapeDtypeStruct(passages.shape, jnp.bfloat16),
            jax.ShapeDtypeStruct((steps, dec_len, cols + PAIR), jnp.float32),
        ),
        in_specs=in_specs,
        out_specs=(
            pl.BlockSpec(block, lambda i: (half * steps + i, 0)),
            pl.BlockSpec((steps, dec_len, cols + PAIR), lambda i: (0, 0, 0)),
        ),
        scratch_shapes=[
            pltpu.VMEM((tokens, width), jnp.bfloat16),
            pltpu.VMEM((2, width, cols), jnp.bfloat16),
            pltpu.VMEM((2, tokens, cols), jnp.bfloat16),
            pltpu.SemaphoreType.DMA((2,)),
        ],
        input_output_aliases=aliases,
        compiler_params=pltpu.CompilerParams(vmem_limit_bytes=VMEM),
        cost_estimate=pl.CostEstimate(flops=4 * tokens * width * cols, bytes_accessed=24 << 20, transcendentals=1 << 17),
    )(*args)


def place_kernel(owner_ref, *refs):
    parts, out_ref, acc = refs[:HALVES], refs[HALVES], refs[HALVES + 1]
    acc[...] = jnp.zeros_like(acc)
    count = parts[0].shape[0]
    for half in range(HALVES):
        for p in range(count):
            question = owner_ref[half * count + p]
            acc[question] = acc[question] + parts[half][p]
    out_ref[...] = acc[...].astype(jnp.bfloat16)


def place(owner, parts, questions):
    shape = (questions,) + parts[0].shape[1:]
    return pl.pallas_call(
        place_kernel,
        out_shape=jax.ShapeDtypeStruct(shape, jnp.bfloat16),
        in_specs=[in_smem()] + [pl.BlockSpec(memory_space=pltpu.VMEM)] * HALVES,
        out_specs=pl.BlockSpec(memory_space=pltpu.VMEM),
        scratch_shapes=[pltpu.VMEM(shape, jnp.float32)],
        compiler_params=pltpu.CompilerParams(vmem_limit_bytes=VMEM),
        cost_estimate=pl.CostEstimate(flops=1 << 20, bytes_accessed=2 << 20, transcendentals=0),
    )(owner, *parts)


def gather_rows(parts):
    both = jnp.stack(in_order(parts, swap(parts, "xh"), "xh"))
    return lax.all_gather(both, ("y", "z"), axis=0, tiled=False).reshape((NY * NZ,) + both.shape)


def shards(
    passages,
    lengths,
    owner,
    enc_gain,
    final_gain,
    enc_wq,
    enc_wk,
    enc_wv,
    enc_wo,
    dec_wk,
    dec_wv,
    dec_query,
):
    pass_count, seq_len, width = passages.shape
    tok_rows = pass_count * seq_len
    local_cols = enc_wq.shape[1]
    local_heads = local_cols // HD
    question_count, dec_len, _ = dec_query.shape
    flat = passages.reshape(tok_rows, width)
    floats = flat.astype(jnp.float32)
    mean = jnp.mean(floats * floats, axis=-1, keepdims=True)
    normed = (floats * lax.rsqrt(mean + EPS) * enc_gain).astype(jnp.bfloat16)

    qkv = gather_rows(jnp.stack([enc_wq, enc_wk, enc_wv]))
    wo_both = jnp.concatenate(in_order(enc_wo, swap(enc_wo, "xl"), "xl"), axis=0)
    wo = gather_rows(wo_both)
    dkv = gather_rows(jnp.stack([dec_wk, dec_wv]))

    where = lax.axis_index("xl").astype(jnp.int32).reshape(1)
    mine = [attend(half, lengths, normed, qkv) for half in range(HALVES)]
    theirs = [swap(part, "xl") for part in mine]
    partial = [output(where, mine[half], theirs[half], wo, width) for half in range(HALVES)]
    partial_other = [swap(part, "c") for part in partial]
    encoded = None
    numers = []
    for half in range(HALVES):
        encoded, numer = decode(
            half, lengths, owner, final_gain.reshape(1, width), dec_query, flat, partial[half], partial_other[half], dkv, encoded
        )
        numers.append(numer)
    sent = place(owner, numers, question_count)
    came = lax.all_to_all(sent, DP, 0, 0, tiled=True).astype(jnp.float32)
    came = jnp.sum(came, axis=0)
    own_numer = came[:, :local_cols].reshape(dec_len, local_heads, HD)
    own_total = came[:, local_cols : local_cols + local_heads].reshape(dec_len, local_heads, 1)
    context = (own_numer / own_total).astype(jnp.bfloat16).reshape(1, dec_len, local_cols)
    return (encoded.reshape(pass_count, seq_len, width), context)


def solution(mesh):
    fine = Mesh(mesh.devices.reshape((NY, NXH, NZ, NXL, NC)), AXES)
    row = P(DP, MP)
    return jax.shard_map(
        shards,
        mesh=fine,
        in_specs=(
            P(DP, None, None),
            P(DP),
            P(DP),
            P(),
            P(),
            row,
            row,
            row,
            P(MP, DP),
            row,
            row,
            P(None, None, MP),
        ),
        out_specs=(P(DP, None, None), P(DP, None, MP)),
        check_vma=False,
    )
```

time: 361 us -> 332 us (0.920); the launches traced: 354 us -> 332 us
  Pallas kernels: 0 us -> 89.8 us
  local copies, waits for them, and re-layouts: 74.6 us -> 0.23 us
  matrix products: 66.8 us -> 0 us
  waiting for transfers between devices: 124 us -> 160 us
  other arithmetic: 31.8 us -> 23 us
    pallas_call x0 -> x7, Pallas kernels: none -> 89.8 us  [the longest x2 34.1 us: attend(): pl.pallas_call(functools.partial(attend_kernel, half, tokens), out_shape=...]
    dot_general x12 -> x0, matrix products: 66.8 us -> none  [the longest x6 54.4 us: mm(): return jnp.dot(a, b, preferred_element_type=jnp.float32)]
    transpose x8 -> x0, local copies, waits for them, and re-layouts: 44.6 us -> none  [the longest x1 23.3 us: shards(): wo_full.reshape(4, 4, 2, 2 * local_cols, -1).transpose(3, 0, 2, 1, 4)]
    all_gather x3, waiting for transfers between devices: 107 us -> 138 us  [gather_rows(): lax.all_gather(both, ('y', 'z'), axis=0, tiled=False)]
    reshape x6 -> x0, local copies, waits for them, and re-layouts: 18.6 us -> none  [the longest x5 17.5 us: by_heads(): values.astype(jnp.bfloat16).reshape(pass_count, seq_len, local_heads, HD)]
    reduce_sum x2 -> x1, other arithmetic: 13.6 us -> 5.22 us  [shards(): mean = jnp.mean(floats * floats, axis=-1, keepdims=True)]
    unnamed x26 -> x14, local copies, waits for them, and re-layouts: 6.76 us -> 0.04 us
    ppermute x6 -> x8, waiting for transfers between devices: 17 us -> 21.9 us  [swap(): return lax.ppermute(values, axis, [(0, 1), (1, 0)])]
  transfers between devices with their start and end apart: 9 -> 11, of which waited for: 6 -> 7; matrix products, arithmetic and copies ran while one was open for 34% -> 6% of each run, Pallas kernels for 0% -> 22%
where the time goes in v2:
time: 332 us
  waiting for transfers between devices  160 us (48%)
  Pallas kernels  89.8 us (27%)
  blocking collectives  29.7 us (9%)
  other arithmetic  23 us (7%)
  starting transfers between devices  14.8 us (4%)
  between operations  14 us (4%)
    all_gather x3, waiting for transfers between devices, gather_rows(): lax.all_gather(both, ('y', 'z'), axis=0, tiled=False)  138 us
    pallas_call x2, Pallas kernels, attend(): pl.pallas_call(functools.partial(attend_kernel, half, tokens), out_shape=...  34.1 us
    pallas_call x2, Pallas kernels, decode(): pl.pallas_call(functools.partial(decode_kernel, half, prior is not None),...  32.7 us
    all_to_all x1, blocking collectives, shards(): came = lax.all_to_all(sent, DP, 0, 0, tiled=True).astype(jnp.float32)  29.7 us
    pallas_call x2, Pallas kernels, output(): pl.pallas_call(output_kernel, out_shape=jax.ShapeDtypeStruct((tokens, wid...  22.1 us
    ppermute x8, waiting for transfers between devices, swap(): return lax.ppermute(values, axis, [(0, 1), (1, 0)])  21.9 us
    ppermute x8, starting transfers between devices, swap(): return lax.ppermute(values, axis, [(0, 1), (1, 0)])  14.7 us
    convert_element_type x1, other arithmetic, shards(): normed = (floats * lax.rsqrt(mean + EPS) * enc_gain).astype(jnp.bfloat16)  11 us
  transfers between devices with their start and end apart: 11, of which 7 were waited for; matrix products, arithmetic and copies ran while one was open for 6% of the time, Pallas kernels for 22%

profile of v2, /device:TPU:0, one launch (start us, length us, event | category | flops | bytes accessed | tf_op | source)
XLA Modules:
  0.0 331.8 jit_solution(8989880369305315897)
XLA Ops:
  7.2 1.1 pad_maximum_fusion.3
  8.4 3.2 collective-permute-start
  11.6 9.1 %collective-permute-done = bf16[3,128,512]{2,1,0:T(8,128)(2,1)S(1)} collective-permute-done((bf16[3,128,512]{2,1,0:T(8,128)(2,1)S(1)}, bf16[3,128,512]{2,1,0:T(8,128)(2,1)S(1)}, u32[]{:S(2)}, u32[]{:S(2)}) %collective-permute-start) | collective-permute-done | bytes 393248 | tf_op jit(solution)/shard_map/ppermute | solution.py:24
  20.7 1.1 select_bitcast_fusion.1
  21.8 1.0 pad_maximum_fusion
  22.8 1.8 collective-permute-start.2
  24.6 3.5 %collective-permute-done.2 = bf16[512,128]{1,0:T(8,128)(2,1)S(1)} collective-permute-done((bf16[512,128]{1,0:T(8,128)(2,1)}, bf16[512,128]{1,0:T(8,128)(2,1)S(1)}, u32[]{:S(2)}, u32[]{:S(2)}) %collective-permute-start.2) | collective-permute-done | bytes 131104 | tf_op jit(solution)/shard_map/ppermute | solution.py:24
  28.1 0.9 broadcast_select_fusion.1
  29.0 3.3 %collective-permute-start.3 = (bf16[1024,128]{1,0:T(8,128)(2,1)S(1)}, bf16[1024,128]{1,0:T(8,128)(2,1)S(1)}, u32[]{:S(2)}, u32[]{:S(2)}) collective-permute-start(bf16[1024,128]{1,0:T(8,128)(2,1)S(1)} %pad_maximum_fusion.4), channel_id=1, source_target_pairs={{0,16},{16,0},{1,17},{17,1},{2,18},{18,2},{3,19},{19,3},{4,20},{20... | collective-permute-start | bytes 786440 | tf_op jit(solution)/shard_map/ppermute | solution.py:24
  32.3 4.6 %collective-permute-done.3 = bf16[1024,128]{1,0:T(8,128)(2,1)S(1)} collective-permute-done((bf16[1024,128]{1,0:T(8,128)(2,1)S(1)}, bf16[1024,128]{1,0:T(8,128)(2,1)S(1)}, u32[]{:S(2)}, u32[]{:S(2)}) %collective-permute-start.3) | collective-permute-done | bytes 262176 | tf_op jit(solution)/shard_map/ppermute | solution.py:24
  37.1 0.8 pad_maximum_fusion.1
  38.0 3.3 %collective-permute-start.5 = (bf16[2,128,512]{2,1,0:T(8,128)(2,1)S(1)}, bf16[2,128,512]{2,1,0:T(8,128)(2,1)S(1)}, u32[]{:S(2)}, u32[]{:S(2)}) collective-permute-start(bf16[2,128,512]{2,1,0:T(8,128)(2,1)S(1)} %pad_maximum_fusion.5), channel_id=1, source_target_pairs={{0,16},{16,0},{1,17},{17,1},{2,18},{18,2},{3,19},{19,3},{4,20},{20... | collective-permute-start | bytes 786440 | tf_op jit(solution)/shard_map/ppermute | solution.py:24
  41.4 4.6 %collective-permute-done.5 = bf16[2,128,512]{2,1,0:T(8,128)(2,1)S(1)} collective-permute-done((bf16[2,128,512]{2,1,0:T(8,128)(2,1)S(1)}, bf16[2,128,512]{2,1,0:T(8,128)(2,1)S(1)}, u32[]{:S(2)}, u32[]{:S(2)}) %collective-permute-start.5) | collective-permute-done | bytes 262176 | tf_op jit(solution)/shard_map/ppermute | solution.py:24
  46.0 0.9 pad_maximum_fusion.2
  47.0 5.2 %multiply_reduce_fusion = f32[8,128]{1,0:T(8,128)S(1)} fusion(bf16[8,128,4096]{2,1,0:T(8,128)(2,1)} %param.12), kind=kLoop, calls=%fused_computation.1 | loop fusion | flops 12581888 | bytes 8392704 | tf_op jit(solution)/shard_map/reduce_sum | solution.py:342
  52.2 11.0 %multiply_convert_fusion.normed_ref = bf16[1024,4096]{1,0:T(8,128)(2,1)} fusion(f32[4096]{0:T(1024)S(1)} %copy-done.6, f32[1024]{0:T(1024)S(1)} %rsqrt_bitcast_fusion, bf16[8,128,4096]{2,1,0:T(8,128)(2,1)} %param.12), kind=kLoop, calls=%fused_computation | loop fusion | flops 16777216 | bytes 16797696 | tf_op jit(solution)/shard_map/convert_element_type | solution.py:343
  63.2 52.5 %all-gather.7.cloned.1.call-done = bf16[32,3,128,512]{3,2,1,0:T(8,128)(2,1)} async-done(((bf16[2,3,128,512]{3,2,1,0:T(8,128)(2,1)}), bf16[32,3,128,512]{3,2,1,0:T(8,128)(2,1)}) %all-gather.7.cloned.1.call-update) | async-done | bytes 12582928 | tf_op jit(solution)/shard_map/all_gather | solution.py:318
  115.7 17.0 %shard_map.133.mine_ref = bf16[512,512]{1,0:T(8,128)(2,1)S(1)} custom-call(s32[8]{0:T(128)S(1)} %copy-done.3, bf16[1024,4096]{1,0:T(8,128)(2,1)} %multiply_convert_fusion.normed_ref, bf16[16,2,3,128,512]{4,3,2,1,0:T(8,128)(2,1)} %bitcast.46), custom_call_target="tpu_custom_call" | custom-call | flops 6442450944 | bytes 18874368 | tf_op jit(solution)/shard_map/pallas_call | solution.py:109
  132.6 1.7 collective-permute-start.6
  134.4 17.1 %shard_map.131.mine_ref = bf16[512,512]{1,0:T(8,128)(2,1)S(1)} custom-call(s32[8]{0:T(128)S(1)} %copy-done.3, bf16[1024,4096]{1,0:T(8,128)(2,1)} %multiply_convert_fusion.normed_ref, bf16[16,2,3,128,512]{4,3,2,1,0:T(8,128)(2,1)} %bitcast.47), custom_call_target="tpu_custom_call" | custom-call | flops 6442450944 | bytes 18874368 | tf_op jit(solution)/shard_map/pallas_call | solution.py:109
  151.5 0.6 collective-permute-start.1
  152.1 36.1 %all-gather.9.cloned.1.call-done = bf16[32,1024,128]{2,1,0:T(8,128)(2,1)} async-done(((bf16[2,1024,128]{2,1,0:T(8,128)(2,1)}), bf16[32,1024,128]{2,1,0:T(8,128)(2,1)}) %all-gather.9.cloned.1.call-update) | async-done | bytes 8388624 | tf_op jit(solution)/shard_map/all_gather | solution.py:318
  188.3 10.9 %shard_map.134.mine_ref = bf16[512,4096]{1,0:T(8,128)(2,1)} custom-call(s32[1]{0:T(128)} %bitcast.2.where_ref, bf16[512,512]{1,0:T(8,128)(2,1)S(1)} %shard_map.133.mine_ref, bf16[512,512]{1,0:T(8,128)(2,1)S(1)} %collective-permute-done.6.other_ref, bf16[16,2,1024,128]{3,2,1,0:T(8,128)(2,1)} %bitcast.48), custom_call_target="tpu_custom_call" | custom-call | flops 4294967296 | bytes 13631488 | tf_op jit(solution)/shard_map/pallas_call | solution.py:155
  199.4 11.2 %shard_map.132.mine_ref = bf16[512,4096]{1,0:T(8,128)(2,1)} custom-call(s32[1]{0:T(128)} %bitcast.2.where_ref, bf16[512,512]{1,0:T(8,128)(2,1)S(1)} %shard_map.131.mine_ref, bf16[512,512]{1,0:T(8,128)(2,1)S(1)} %collective-permute-done.1.other_ref, bf16[16,2,1024,128]{3,2,1,0:T(8,128)(2,1)} %bitcast.49), custom_call_target="tpu_custom_call" | custom-call | flops 4294967296 | bytes 13631488 | tf_op jit(solution)/shard_map/pallas_call | solution.py:155
  210.6 0.6 collective-permute-start.4
  211.2 49.7 %all-gather.11.cloned.1.call-done = bf16[32,2,128,512]{3,2,1,0:T(8,128)(2,1)} async-done(((bf16[2,2,128,512]{3,2,1,0:T(8,128)(2,1)}), bf16[32,2,128,512]{3,2,1,0:T(8,128)(2,1)}) %all-gather.11.cloned.1.call-update) | async-done | bytes 8388624 | tf_op jit(solution)/shard_map/all_gather | solution.py:318
  260.9 16.3 %shard_map.135 = (bf16[1024,4096]{1,0:T(8,128)(2,1)}, f32[4,32,640]{2,1,0:T(8,128)S(1)}) custom-call(s32[8]{0:T(128)S(1)} %copy-done.3, s32[8]{0:T(128)S(1)} %copy-done.2, f32[1,4096]{1,0:T(1,128)S(1)} %bitcast.29, bf16[32,32,512]{2,1,0:T(8,128)(2,1)S(1)} %copy-done, bf16[1024,4096]{1,0:T(8,128)(2,1)} %bitcast.31, bf16[512,4096]{1,0:T(8,128)(2,1)} %shard_map.134.mine_ref, ...), custom_call_target="tpu_custom_call" | custom-call | flops 4294967296 | bytes 25165824 | tf_op jit(solution)/shard_map/pallas_call | solution.py:268
  277.3 16.3 %shard_map.136 = (bf16[1024,4096]{1,0:T(8,128)(2,1)}, f32[4,32,640]{2,1,0:T(8,128)S(1)}) custom-call(s32[8]{0:T(128)S(1)} %copy-done.3, s32[8]{0:T(128)S(1)} %copy-done.2, f32[1,4096]{1,0:T(1,128)S(1)} %bitcast.30, bf16[32,32,512]{2,1,0:T(8,128)(2,1)S(1)} %copy-done, bf16[1024,4096]{1,0:T(8,128)(2,1)} %bitcast.32, ...), custom_call_target="tpu_custom_call", output_to_operand_aliasing={{0}: (8, {})} | custom-call | flops 4294967296 | bytes 25165824 | tf_op jit(solution)/shard_map/pallas_call | solution.py:268
  293.6 0.9 shard_map.137
  294.6 29.7 %all_to_all.5 = bf16[32,32,640]{2,1,0:T(8,128)(2,1)S(1)} all-to-all(bf16[32,32,640]{2,1,0:T(8,128)(2,1)S(1)} %shard_map.137), channel_id=1, replica_groups=mesh['y'=4,'xh'=2,'z'=4,'xl'=2,'c'=2] {'y','xh','z'}, dimensions={0} | all-to-all | bytes 2621440 | tf_op jit(solution)/shard_map/all_to_all | solution.py:363
  324.2 0.2 convert_reduce_fusion
  324.6 0.6 fusion.1
  (33 shorter events, 0.7 us)
Async XLA Ops:
  7.2 30.8 %copy-start.4 = (bf16[128,512]{1,0:T(8,128)(2,1)S(1)}, bf16[128,512]{1,0:T(8,128)(2,1)}, u32[]{:S(2)}) copy-start(bf16[128,512]{1,0:T(8,128)(2,1)} %param.22) | copy-start | bytes 393220
  7.2 30.8 %copy-start.5 = (bf16[128,512]{1,0:T(8,128)(2,1)S(1)}, bf16[128,512]{1,0:T(8,128)(2,1)}, u32[]{:S(2)}) copy-start(bf16[128,512]{1,0:T(8,128)(2,1)} %param.21) | copy-start | bytes 393220
  7.2 108.5 %all-gather.7.cloned.1.call-start = ((), (), s32[]{:S(2)}) async-start(), calls=%async_computation.1 | async-start | bytes 13369344 | tf_op jit(solution)/shard_map/all_gather | solution.py:318
  8.4 12.3 %collective-permute-start = (bf16[3,128,512]{2,1,0:T(8,128)(2,1)S(1)}, bf16[3,128,512]{2,1,0:T(8,128)(2,1)S(1)}, u32[]{:S(2)}, u32[]{:S(2)}) collective-permute-start(bf16[3,128,512]{2,1,0:T(8,128)(2,1)S(1)} %pad_maximum_fusion.3), channel_id=1, source_target_pairs={{0,16},{16,0},{1,17},{17,1},{2,18},{18,2},{3,19},{19,3},{4,20},{20... | collective-permute-start | bytes 1179656 | tf_op jit(solution)/shard_map/ppermute | solution.py:24
  22.7 29.5 %copy-start.6 = (f32[4096]{0:T(1024)S(1)}, f32[4096]{0:T(1024)}, u32[]{:S(2)}) copy-start(f32[4096]{0:T(1024)} %param.15) | copy-start | bytes 49156
  22.8 165.5 %all-gather.9.cloned.1.call-start = ((), (), s32[]{:S(2)}) async-start(), calls=%async_computation.2 | async-start | bytes 8912896 | tf_op jit(solution)/shard_map/all_gather | solution.py:318
  22.8 5.3 %collective-permute-start.2 = (bf16[512,128]{1,0:T(8,128)(2,1)}, bf16[512,128]{1,0:T(8,128)(2,1)S(1)}, u32[]{:S(2)}, u32[]{:S(2)}) collective-permute-start(bf16[512,128]{1,0:T(8,128)(2,1)} %param.20), channel_id=1, source_target_pairs={{0,2},{2,0},{1,3},{3,1},{4,6},{6,4},{5,7},{7,5},{8,10},{10,8},{9,1... | collective-permute-start | bytes 393224 | tf_op jit(solution)/shard_map/ppermute | solution.py:24
  29.0 8.0 %collective-permute-start.3 = (bf16[1024,128]{1,0:T(8,128)(2,1)S(1)}, bf16[1024,128]{1,0:T(8,128)(2,1)S(1)}, u32[]{:S(2)}, u32[]{:S(2)}) collective-permute-start(bf16[1024,128]{1,0:T(8,128)(2,1)S(1)} %pad_maximum_fusion.4), channel_id=1, source_target_pairs={{0,16},{16,0},{1,17},{17,1},{2,18},{18,2},{3,19},{19,3},{4,20},{20... | collective-permute-start | bytes 786440 | tf_op jit(solution)/shard_map/ppermute | solution.py:24
  37.9 223.0 %all-gather.11.cloned.1.call-start = ((), (), s32[]{:S(2)}) async-start(), calls=%async_computation.3 | async-start | bytes 8912896 | tf_op jit(solution)/shard_map/all_gather | solution.py:318
  38.0 8.0 %collective-permute-start.5 = (bf16[2,128,512]{2,1,0:T(8,128)(2,1)S(1)}, bf16[2,128,512]{2,1,0:T(8,128)(2,1)S(1)}, u32[]{:S(2)}, u32[]{:S(2)}) collective-permute-start(bf16[2,128,512]{2,1,0:T(8,128)(2,1)S(1)} %pad_maximum_fusion.5), channel_id=1, source_target_pairs={{0,16},{16,0},{1,17},{17,1},{2,18},{18,2},{3,19},{19,3},{4,20},{20... | collective-permute-start | bytes 786440 | tf_op jit(solution)/shard_map/ppermute | solution.py:24
  52.2 63.4 %copy-start.3 = (s32[8]{0:T(128)S(1)}, s32[8]{0:T(128)}, u32[]{:S(2)}) copy-start(s32[8]{0:T(128)} %lens_ref.7) | copy-start | bytes 100
  132.6 55.7 %collective-permute-start.6 = (bf16[512,512]{1,0:T(8,128)(2,1)S(1)}, bf16[512,512]{1,0:T(8,128)(2,1)S(1)}, u32[]{:S(2)}, u32[]{:S(2)}) collective-permute-start(bf16[512,512]{1,0:T(8,128)(2,1)S(1)} %shard_map.133.mine_ref), channel_id=1, source_target_pairs={{0,2},{2,0},{1,3},{3,1},{4,6},{6,4},{5,7},{7,5},{8,10},{10,8},{9,1... | collective-permute-start | bytes 1572872 | tf_op jit(solution)/shard_map/ppermute | solution.py:24
  151.5 47.9 %collective-permute-start.1 = (bf16[512,512]{1,0:T(8,128)(2,1)S(1)}, bf16[512,512]{1,0:T(8,128)(2,1)S(1)}, u32[]{:S(2)}, u32[]{:S(2)}) collective-permute-start(bf16[512,512]{1,0:T(8,128)(2,1)S(1)} %shard_map.131.mine_ref), channel_id=1, source_target_pairs={{0,2},{2,0},{1,3},{3,1},{4,6},{6,4},{5,7},{7,5},{8,10},{10,8},{9,1... | collective-permute-start | bytes 1572872 | tf_op jit(solution)/shard_map/ppermute | solution.py:24
  199.2 61.7 %copy-start = (bf16[32,32,512]{2,1,0:T(8,128)(2,1)S(1)}, bf16[32,32,512]{2,1,0:T(8,128)(2,1)}, u32[]{:S(2)}) copy-start(bf16[32,32,512]{2,1,0:T(8,128)(2,1)} %query_ref.3) | copy-start | bytes 3145732
  199.2 61.7 %copy-start.1 = (f32[4096]{0:T(1024)S(1)}, f32[4096]{0:T(1024)}, u32[]{:S(2)}) copy-start(f32[4096]{0:T(1024)} %param.16) | copy-start | bytes 49156
  199.3 61.7 %copy-start.2 = (s32[8]{0:T(128)S(1)}, s32[8]{0:T(128)}, u32[]{:S(2)}) copy-start(s32[8]{0:T(128)} %owner_ref.5) | copy-start | bytes 100
  199.3 61.6 %collective-permute-start.7 = (bf16[512,4096]{1,0:T(8,128)(2,1)}, bf16[512,4096]{1,0:T(8,128)(2,1)}, u32[]{:S(2)}, u32[]{:S(2)}) collective-permute-start(bf16[512,4096]{1,0:T(8,128)(2,1)} %shard_map.134.mine_ref), channel_id=1, source_target_pairs={{0,1},{1,0},{2,3},{3,2},{4,5},{5,4},{6,7},{7,6},{8,9},{9,8},{10,11... | collective-permute-start | bytes 12582920 | tf_op jit(solution)/shard_map/ppermute | solution.py:24
  210.6 66.7 %collective-permute-start.4 = (bf16[512,4096]{1,0:T(8,128)(2,1)}, bf16[512,4096]{1,0:T(8,128)(2,1)}, u32[]{:S(2)}, u32[]{:S(2)}) collective-permute-start(bf16[512,4096]{1,0:T(8,128)(2,1)} %shard_map.132.mine_ref), channel_id=1, source_target_pairs={{0,1},{1,0},{2,3},{3,2},{4,5},{5,4},{6,7},{7,6},{8,9},{9,8},{10,11... | collective-permute-start | bytes 12582920 | tf_op jit(solution)/shard_map/ppermute | solution.py:24
Sparse Core Ops, SparseCore 0:
  22.9 92.7 all-gather.6
  117.8 70.4 all-gather.8
  190.4 70.4 all-gather.10

commit v3 on v2

--- a/solution.py
+++ b/solution.py
@@ -27,6 +27,31 @@
 def in_order(mine, other, axis):
     first = lax.axis_index(axis) == 0
     return jnp.where(first, mine, other), jnp.where(first, other, mine)
+
+
+RING = (0, 3, 1, 2)
+X_OFFSETS = ((0, 0), (3, 0), (1, 0), (2, 0), (2, 2))
+
+
+def shift(values, axis, by):
+    size = lax.axis_size(axis)
+    return lax.ppermute(values, axis, [(i, (i + by) % size) for i in range(size)])
+
+
+def ring_gather(values, axis):
+    return jnp.stack([values, shift(values, axis, 1), shift(values, axis, -1), shift(values, axis, 2)])
+
+
+def x_ring_pieces(values):
+    below, above = shift(values, ("xh", "xl"), 1), shift(values, ("xh", "xl"), -1)
+    half = values.shape[0] // 2
+    return [
+        values,
+        below,
+        above,
+        shift(below[:half], ("xh", "xl"), 1),
+        shift(above[half:], ("xh", "xl"), -1),
+    ]
 
 
 def anywhere():
@@ -123,26 +148,35 @@
     )(lengths, normed, gathered)
 
 
-def output_kernel(where_ref, mine_ref, other_ref, weights_ref, out_ref, rows, weight, sem_a, sem_w):
+def output_kernel(where_ref, mine_ref, other_ref, *rest):
+    pieces, (out_ref, rows, weight, sem_a, sem_w) = rest[: len(X_OFFSETS)], rest[len(X_OFFSETS) :]
     tokens, cols = mine_ref.shape
-    xl = where_ref[0]
+    y, xh, z, xl = (where_ref[i] for i in range(4))
     mine_at = pl.multiple_of(xl * cols, cols)
     other_at = pl.multiple_of((1 - xl) * cols, cols)
     pltpu.make_async_copy(mine_ref, rows.at[:, pl.ds(mine_at, cols)], sem_a).start()
     pltpu.make_async_copy(other_ref, rows.at[:, pl.ds(other_at, cols)], sem_a).start()
-    for y, xh, z, d in dp_blocks():
-        pltpu.make_async_copy(
-            weights_ref.at[y * NZ + z, xh], weight.at[:, pl.ds(d * SEQ, SEQ)], sem_w.at[y]
-        ).start()
+    for piece, (dx, first) in zip(pieces, X_OFFSETS):
+        x_from = lax.rem(xh * NXL + xl + dx, NXH * NXL)
+        row = pl.multiple_of(lax.rem(x_from, NXL) * cols, cols)
+        for i in range(piece.shape[0]):
+            z_from = lax.rem(z + RING[first + i], NZ)
+            for j in range(NY):
+                y_from = lax.rem(y + RING[j], NY)
+                block = (y_from * NXH + x_from // NXL) * NZ + z_from
+                at = pl.multiple_of(block * SEQ, SEQ)
+                pltpu.make_async_copy(
+                    piece.at[i, j], weight.at[pl.ds(row, cols), pl.ds(at, SEQ)], sem_w.at[y_from]
+                ).start()
     pltpu.make_async_copy(rows, rows, sem_a).wait()
     part = weight.shape[1] // NY
     wide = 256
-    for y in range(NY):
-        quarter = weight.at[:, pl.ds(y * part, part)]
-        pltpu.make_async_copy(quarter, quarter, sem_w.at[y]).wait()
-
-        def step(i, _, y=y):
-            at = pl.multiple_of(y * part + i * wide, wide)
+    for q in range(NY):
+        quarter = weight.at[:, pl.ds(q * part, part)]
+        pltpu.make_async_copy(quarter, quarter, sem_w.at[q]).wait()
+
+        def step(i, _, q=q):
+            at = pl.multiple_of(q * part + i * wide, wide)
             acc = jnp.dot(rows[...], weight[:, pl.ds(at, wide)], preferred_element_type=jnp.float32)
             out_ref[:, pl.ds(at, wide)] = acc.astype(jnp.bfloat16)
             return 0
@@ -150,12 +184,12 @@
         lax.fori_loop(0, part // wide, step, 0)
 
 
-def output(where, mine, other, gathered, width):
+def output(where, mine, other, pieces, width):
     tokens, cols = mine.shape
     return pl.pallas_call(
         output_kernel,
         out_shape=jax.ShapeDtypeStruct((tokens, width), jnp.bfloat16),
-        in_specs=[in_smem(), anywhere(), anywhere(), anywhere()],
+        in_specs=[in_smem()] + [anywhere()] * (2 + len(pieces)),
         out_specs=pl.BlockSpec(memory_space=pltpu.VMEM),
         scratch_shapes=[
             pltpu.VMEM((tokens, 2 * cols), jnp.bfloat16),
@@ -165,7 +199,7 @@
         ],
         compiler_params=pltpu.CompilerParams(vmem_limit_bytes=VMEM),
         cost_estimate=pl.CostEstimate(flops=4 * tokens * width * cols, bytes_accessed=13 << 20, transcendentals=0),
-    )(where, mine, other, gathered)
+    )(where, mine, other, *pieces)
 
 
 def decode_kernel(
@@ -343,11 +377,10 @@
     normed = (floats * lax.rsqrt(mean + EPS) * enc_gain).astype(jnp.bfloat16)
 
     qkv = gather_rows(jnp.stack([enc_wq, enc_wk, enc_wv]))
-    wo_both = jnp.concatenate(in_order(enc_wo, swap(enc_wo, "xl"), "xl"), axis=0)
-    wo = gather_rows(wo_both)
+    wo = x_ring_pieces(ring_gather(ring_gather(enc_wo, "y"), "z"))
     dkv = gather_rows(jnp.stack([dec_wk, dec_wv]))
 
-    where = lax.axis_index("xl").astype(jnp.int32).reshape(1)
+    where = jnp.stack([lax.axis_index(axis) for axis in AXES]).astype(jnp.int32)
     mine = [attend(half, lengths, normed, qkv) for half in range(HALVES)]
     theirs = [swap(part, "xl") for part in mine]
     partial = [output(where, mine[half], theirs[half], wo, width) for half in range(HALVES)]

time: 332 us -> 272 us (0.82)
  waiting for transfers between devices: 160 us -> 80.7 us
  starting transfers between devices: 14.8 us -> 27.7 us
  Pallas kernels: 89.8 us -> 95 us
  local copies, waits for them, and re-layouts: 0.23 us -> 3.93 us
    all_gather x3 -> x2, waiting for transfers between devices: 138 us -> 0.01 us  [gather_rows(): lax.all_gather(both, ('y', 'z'), axis=0, tiled=False)]
    ppermute x0 -> x10, waiting for transfers between devices: none -> 66.1 us  [shift(): lax.ppermute(values, axis, [(i, (i + by) % size) for i in range(size)])]
    ppermute x0 -> x10, starting transfers between devices: none -> 18.1 us  [shift(): lax.ppermute(values, axis, [(i, (i + by) % size) for i in range(size)])]
    ppermute x8 -> x6, waiting for transfers between devices: 21.9 us -> 14.6 us  [swap(): return lax.ppermute(values, axis, [(0, 1), (1, 0)])]
    ppermute x8 -> x6, starting transfers between devices: 14.7 us -> 9.59 us  [swap(): return lax.ppermute(values, axis, [(0, 1), (1, 0)])]
    pallas_call x2, Pallas kernels: 22.1 us -> 27 us  [output(): pl.pallas_call(output_kernel, out_shape=jax.ShapeDtypeStruct((tokens, wid...]
    slice x0 -> x2, local copies, waits for them, and re-layouts: none -> 3.61 us  [the longest x1 2.31 us: x_ring_pieces(): below[:half]]
  transfers between devices with their start and end apart: 11 -> 18, of which waited for: 7 -> 9; matrix products, arithmetic and copies ran while one was open for 6% -> 8% of each run, Pallas kernels for 22% -> 29%
where the time goes in v3:
time: 272 us
  Pallas kernels  95 us (35%)
  waiting for transfers between devices  80.7 us (30%)
  blocking collectives  29.2 us (11%)
  starting transfers between devices  27.7 us (10%)
  other arithmetic  21.1 us (8%)
  between operations  14.3 us (5%)
  local copies, waits for them, and re-layouts  3.93 us (1%)
    ppermute x10, waiting for transfers between devices, shift(): lax.ppermute(values, axis, [(i, (i + by) % size) for i in range(size)])  66.1 us
    pallas_call x2, Pallas kernels, attend(): pl.pallas_call(functools.partial(attend_kernel, half, tokens), out_shape=...  34.5 us
    pallas_call x2, Pallas kernels, decode(): pl.pallas_call(functools.partial(decode_kernel, half, prior is not None),...  32.7 us
    all_to_all x1, blocking collectives, shards(): came = lax.all_to_all(sent, DP, 0, 0, tiled=True).astype(jnp.float32)  29.2 us
    pallas_call x2, Pallas kernels, output(): pl.pallas_call(output_kernel, out_shape=jax.ShapeDtypeStruct((tokens, wid...  27 us
    ppermute x10, starting transfers between devices, shift(): lax.ppermute(values, axis, [(i, (i + by) % size) for i in range(size)])  18.1 us
    ppermute x6, waiting for transfers between devices, swap(): return lax.ppermute(values, axis, [(0, 1), (1, 0)])  14.6 us
    convert_element_type x1, other arithmetic, shards(): normed = (floats * lax.rsqrt(mean + EPS) * enc_gain).astype(jnp.bfloat16)  10.6 us
  transfers between devices with their start and end apart: 18, of which 9 were waited for; matrix products, arithmetic and copies ran while one was open for 8% of the time, Pallas kernels for 29%

profile of v3, /device:TPU:0, one launch (start us, length us, event | category | flops | bytes accessed | tf_op | source)
XLA Modules:
  0.0 271.9 jit_solution(12513606265924275346)
XLA Ops:
  7.2 1.2 pad_maximum_fusion.4
  8.4 3.2 %collective-permute-start = (bf16[3,128,512]{2,1,0:T(8,128)(2,1)S(1)}, bf16[3,128,512]{2,1,0:T(8,128)(2,1)S(1)}, u32[]{:S(2)}, u32[]{:S(2)}) collective-permute-start(bf16[3,128,512]{2,1,0:T(8,128)(2,1)S(1)} %pad_maximum_fusion.4), channel_id=1, source_target_pairs={{0,16},{16,0},{1,17},{17,1},{2,18},{18,2},{3,19},{19,3},{4,20},{20... | collective-permute-start | bytes 1179656 | tf_op jit(solution)/shard_map/ppermute | solution.py:24
  11.6 9.1 %collective-permute-done = bf16[3,128,512]{2,1,0:T(8,128)(2,1)S(1)} collective-permute-done((bf16[3,128,512]{2,1,0:T(8,128)(2,1)S(1)}, bf16[3,128,512]{2,1,0:T(8,128)(2,1)S(1)}, u32[]{:S(2)}, u32[]{:S(2)}) %collective-permute-start) | collective-permute-done | bytes 393248 | tf_op jit(solution)/shard_map/ppermute | solution.py:24
  20.7 1.1 select_bitcast_fusion.1
  22.9 3.3 %collective-permute-start.13 = (bf16[2,128,512]{2,1,0:T(8,128)(2,1)S(1)}, bf16[2,128,512]{2,1,0:T(8,128)(2,1)S(1)}, u32[]{:S(2)}, u32[]{:S(2)}) collective-permute-start(bf16[2,128,512]{2,1,0:T(8,128)(2,1)S(1)} %pad_maximum_fusion.5), channel_id=1, source_target_pairs={{0,16},{16,0},{1,17},{17,1},{2,18},{18,2},{3,19},{19,3},{4,20},{20... | collective-permute-start | bytes 786440 | tf_op jit(solution)/shard_map/ppermute | solution.py:24
  26.2 5.4 %collective-permute-done.13 = bf16[2,128,512]{2,1,0:T(8,128)(2,1)S(1)} collective-permute-done((bf16[2,128,512]{2,1,0:T(8,128)(2,1)S(1)}, bf16[2,128,512]{2,1,0:T(8,128)(2,1)S(1)}, u32[]{:S(2)}, u32[]{:S(2)}) %collective-permute-start.13) | collective-permute-done | bytes 262176 | tf_op jit(solution)/shard_map/ppermute | solution.py:24
  32.6 1.9 collective-permute-start.2
  34.4 2.9 %collective-permute-start.4 = (bf16[512,128]{1,0:T(8,128)(2,1)S(1)}, bf16[512,128]{1,0:T(8,128)(2,1)S(1)}, u32[]{:S(2)}, u32[]{:S(2)}) collective-permute-start(bf16[512,128]{1,0:T(8,128)(2,1)S(1)} %copy-done.7), channel_id=1, source_target_pairs={{0,64},{32,96},{64,0},{96,32},{1,65},{33,97},{65,1},{97,33},{2,66}... | collective-permute-start | bytes 393224 | tf_op jit(solution)/shard_map/ppermute | solution.py:38
  37.3 1.3 collective-permute-start.3
  38.7 2.4 collective-permute-done.2
  41.1 4.1 %collective-permute-done.4 = bf16[512,128]{1,0:T(8,128)(2,1)S(1)} collective-permute-done((bf16[512,128]{1,0:T(8,128)(2,1)S(1)}, bf16[512,128]{1,0:T(8,128)(2,1)S(1)}, u32[]{:S(2)}, u32[]{:S(2)}) %collective-permute-start.4) | collective-permute-done | bytes 131104 | tf_op jit(solution)/shard_map/ppermute | solution.py:38
  45.2 1.8 collective-permute-done.3
  47.1 4.7 %collective-permute-start.6 = (bf16[4,512,128]{2,1,0:T(8,128)(2,1)S(1)}, bf16[4,512,128]{2,1,0:T(8,128)(2,1)S(1)}, u32[]{:S(2)}, u32[]{:S(2)}) collective-permute-start(bf16[4,512,128]{2,1,0:T(8,128)(2,1)S(1)} %get-tuple-element.15), channel_id=1, source_target_pairs={{0,12},{4,0},{8,4},{12,8},{1,13},{5,1},{9,5},{13,9},{2,14},{6,2},{... | collective-permute-start | bytes 1572872 | tf_op jit(solution)/shard_map/ppermute | solution.py:38
  51.8 1.6 collective-permute-start.7
  53.4 17.1 %collective-permute-done.6 = bf16[4,512,128]{2,1,0:T(8,128)(2,1)S(1)} collective-permute-done((bf16[4,512,128]{2,1,0:T(8,128)(2,1)S(1)}, bf16[4,512,128]{2,1,0:T(8,128)(2,1)S(1)}, u32[]{:S(2)}, u32[]{:S(2)}) %collective-permute-start.6) | collective-permute-done | bytes 524320 | tf_op jit(solution)/shard_map/ppermute | solution.py:38
  70.5 3.8 %collective-permute-done.5 = bf16[4,512,128]{2,1,0:T(8,128)(2,1)S(1)} collective-permute-done((bf16[4,512,128]{2,1,0:T(8,128)(2,1)S(1)}, bf16[4,512,128]{2,1,0:T(8,128)(2,1)S(1)}, u32[]{:S(2)}, u32[]{:S(2)}) %collective-permute-start.5) | collective-permute-done | bytes 524320 | tf_op jit(solution)/shard_map/ppermute | solution.py:38
  74.2 11.0 %collective-permute-done.7 = bf16[4,512,128]{2,1,0:T(8,128)(2,1)S(1)} collective-permute-done((bf16[4,512,128]{2,1,0:T(8,128)(2,1)S(1)}, bf16[4,512,128]{2,1,0:T(8,128)(2,1)S(1)}, u32[]{:S(2)}, u32[]{:S(2)}) %collective-permute-start.7) | collective-permute-done | bytes 524320 | tf_op jit(solution)/shard_map/ppermute | solution.py:38
  85.5 2.8 %collective-permute-start.9 = (bf16[4,4,512,128]{3,2,1,0:T(8,128)(2,1)S(1)}, bf16[4,4,512,128]{3,2,1,0:T(8,128)(2,1)}, u32[]{:S(2)}, u32[]{:S(2)}) collective-permute-start(bf16[4,4,512,128]{3,2,1,0:T(8,128)(2,1)S(1)} %pad_maximum_fusion.rest_0_), channel_id=1, source_target_pairs={{0,18},{2,0},{16,2},{18,16},{1,19},{3,1},{17,3},{19,17},{4,22},{6,... | collective-permute-start | bytes 6291464 | tf_op jit(solution)/shard_map/ppermute | solution.py:38
  88.4 5.2 %multiply_reduce_fusion = f32[8,128]{1,0:T(8,128)S(1)} fusion(bf16[8,128,4096]{2,1,0:T(8,128)(2,1)} %param.12), kind=kLoop, calls=%fused_computation.1 | loop fusion | flops 12581888 | bytes 8392704 | tf_op jit(solution)/shard_map/reduce_sum | solution.py:376
  93.6 10.6 %multiply_convert_fusion.normed_ref = bf16[1024,4096]{1,0:T(8,128)(2,1)} fusion(f32[4096]{0:T(1024)S(1)} %copy-done.8, f32[1024]{0:T(1024)S(1)} %rsqrt_bitcast_fusion, bf16[8,128,4096]{2,1,0:T(8,128)(2,1)} %param.12), kind=kLoop, calls=%fused_computation | loop fusion | flops 16777216 | bytes 16797696 | tf_op jit(solution)/shard_map/convert_element_type | solution.py:377
  104.2 25.9 %collective-permute-done.9.rest_2_ = bf16[4,4,512,128]{3,2,1,0:T(8,128)(2,1)} collective-permute-done((bf16[4,4,512,128]{3,2,1,0:T(8,128)(2,1)S(1)}, bf16[4,4,512,128]{3,2,1,0:T(8,128)(2,1)}, u32[]{:S(2)}, u32[]{:S(2)}) %collective-permute-start.9) | collective-permute-done | bytes 2097184 | tf_op jit(solution)/shard_map/ppermute | solution.py:38
  130.0 1.3 slice.17
  131.3 2.8 %collective-permute-start.11 = (bf16[2,4,512,128]{3,2,1,0:T(8,128)(2,1)S(1)}, bf16[2,4,512,128]{3,2,1,0:T(8,128)(2,1)}, u32[]{:S(2)}, u32[]{:S(2)}) collective-permute-start(bf16[2,4,512,128]{3,2,1,0:T(8,128)(2,1)S(1)} %slice.17), channel_id=1, source_target_pairs={{0,18},{2,0},{16,2},{18,16},{1,19},{3,1},{17,3},{19,17},{4,22},{6,... | collective-permute-start | bytes 3145736 | tf_op jit(solution)/shard_map/ppermute | solution.py:38
  134.2 2.3 slice.16
  136.5 17.5 %shard_map.133.mine_ref = bf16[512,512]{1,0:T(8,128)(2,1)S(1)} custom-call(s32[8]{0:T(128)S(1)} %copy-done.3, bf16[1024,4096]{1,0:T(8,128)(2,1)} %multiply_convert_fusion.normed_ref, bf16[16,2,3,128,512]{4,3,2,1,0:T(8,128)(2,1)} %bitcast.61), custom_call_target="tpu_custom_call" | custom-call | flops 6442450944 | bytes 18874368 | tf_op jit(solution)/shard_map/pallas_call | solution.py:134
  154.8 17.0 %shard_map.131.mine_ref = bf16[512,512]{1,0:T(8,128)(2,1)S(1)} custom-call(s32[8]{0:T(128)S(1)} %copy-done.3, bf16[1024,4096]{1,0:T(8,128)(2,1)} %multiply_convert_fusion.normed_ref, bf16[16,2,3,128,512]{4,3,2,1,0:T(8,128)(2,1)} %bitcast.62), custom_call_target="tpu_custom_call" | custom-call | flops 6442450944 | bytes 18874368 | tf_op jit(solution)/shard_map/pallas_call | solution.py:134
  171.8 1.4 collective-permute-start.1
  173.3 13.5 %shard_map.134.mine_ref = bf16[512,4096]{1,0:T(8,128)(2,1)} custom-call(s32[5]{0:T(128)S(1)} %stack.92.where_ref, bf16[512,512]{1,0:T(8,128)(2,1)S(1)} %shard_map.133.mine_ref, bf16[512,512]{1,0:T(8,128)(2,1)S(1)} %collective-permute-done.14.other_ref, bf16[4,4,512,128]{3,2,1,0:T(8,128)(2,1)} %copy-done.4, ...), custom_call_target="tpu_custom_call" | custom-call | flops 4294967296 | bytes 13631488 | tf_op jit(solution)/shard_map/pallas_call | solution.py:189
  186.9 13.4 %shard_map.132.mine_ref = bf16[512,4096]{1,0:T(8,128)(2,1)} custom-call(s32[5]{0:T(128)S(1)} %stack.92.where_ref, bf16[512,512]{1,0:T(8,128)(2,1)S(1)} %shard_map.131.mine_ref, bf16[512,512]{1,0:T(8,128)(2,1)S(1)} %collective-permute-done.1.other_ref, bf16[4,4,512,128]{3,2,1,0:T(8,128)(2,1)} %copy-done.4, ...), custom_call_target="tpu_custom_call" | custom-call | flops 4294967296 | bytes 13631488 | tf_op jit(solution)/shard_map/pallas_call | solution.py:189
  201.2 16.3 %shard_map.135 = (bf16[1024,4096]{1,0:T(8,128)(2,1)}, f32[4,32,640]{2,1,0:T(8,128)S(1)}) custom-call(s32[8]{0:T(128)S(1)} %copy-done.3, s32[8]{0:T(128)S(1)} %copy-done.2, f32[1,4096]{1,0:T(1,128)S(1)} %bitcast.37, bf16[32,32,512]{2,1,0:T(8,128)(2,1)S(1)} %copy-done, bf16[1024,4096]{1,0:T(8,128)(2,1)} %bitcast.39, bf16[512,4096]{1,0:T(8,128)(2,1)} %shard_map.134.mine_ref, ...), custom_call_target="tpu_custom_call" | custom-call | flops 4294967296 | bytes 25165824 | tf_op jit(solution)/shard_map/pallas_call | solution.py:302
  217.6 16.3 %shard_map.136 = (bf16[1024,4096]{1,0:T(8,128)(2,1)}, f32[4,32,640]{2,1,0:T(8,128)S(1)}) custom-call(s32[8]{0:T(128)S(1)} %copy-done.3, s32[8]{0:T(128)S(1)} %copy-done.2, f32[1,4096]{1,0:T(1,128)S(1)} %bitcast.38, bf16[32,32,512]{2,1,0:T(8,128)(2,1)S(1)} %copy-done, bf16[1024,4096]{1,0:T(8,128)(2,1)} %bitcast.40, ...), custom_call_target="tpu_custom_call", output_to_operand_aliasing={{0}: (8, {})} | custom-call | flops 4294967296 | bytes 25165824 | tf_op jit(solution)/shard_map/pallas_call | solution.py:302
  234.9 29.2 %all_to_all.5 = bf16[32,32,640]{2,1,0:T(8,128)(2,1)S(1)} all-to-all(bf16[32,32,640]{2,1,0:T(8,128)(2,1)S(1)} %shard_map.137), channel_id=1, replica_groups=mesh['y'=4,'xh'=2,'z'=4,'xl'=2,'c'=2] {'y','xh','z'}, dimensions={0} | all-to-all | bytes 2621440 | tf_op jit(solution)/shard_map/all_to_all | solution.py:396
  (51 shorter events, 6.1 us)
Async XLA Ops:
  7.2 15.7 %copy-start.5 = (bf16[128,512]{1,0:T(8,128)(2,1)S(1)}, bf16[128,512]{1,0:T(8,128)(2,1)}, u32[]{:S(2)}) copy-start(bf16[128,512]{1,0:T(8,128)(2,1)} %param.22) | copy-start | bytes 393220
  7.2 15.7 %copy-start.6 = (bf16[128,512]{1,0:T(8,128)(2,1)S(1)}, bf16[128,512]{1,0:T(8,128)(2,1)}, u32[]{:S(2)}) copy-start(bf16[128,512]{1,0:T(8,128)(2,1)} %param.21) | copy-start | bytes 393220
  7.2 25.4 %copy-start.7 = (bf16[512,128]{1,0:T(8,128)(2,1)S(1)}, bf16[512,128]{1,0:T(8,128)(2,1)}, u32[]{:S(2)}) copy-start(bf16[512,128]{1,0:T(8,128)(2,1)} %param.20) | copy-start | bytes 393220
  7.2 129.3 %all-gather.5.cloned.1.call-start = ((), (), s32[]{:S(2)}) async-start(), calls=%async_computation.1 | async-start | bytes 13369344 | tf_op jit(solution)/shard_map/all_gather | solution.py:352
  8.4 12.3 %collective-permute-start = (bf16[3,128,512]{2,1,0:T(8,128)(2,1)S(1)}, bf16[3,128,512]{2,1,0:T(8,128)(2,1)S(1)}, u32[]{:S(2)}, u32[]{:S(2)}) collective-permute-start(bf16[3,128,512]{2,1,0:T(8,128)(2,1)S(1)} %pad_maximum_fusion.4), channel_id=1, source_target_pairs={{0,16},{16,0},{1,17},{17,1},{2,18},{18,2},{3,19},{19,3},{4,20},{20... | collective-permute-start | bytes 1179656 | tf_op jit(solution)/shard_map/ppermute | solution.py:24
  22.8 178.4 %all-gather.7.cloned.1.call-start = ((), (), s32[]{:S(2)}) async-start(), calls=%async_computation.2 | async-start | bytes 8912896 | tf_op jit(solution)/shard_map/all_gather | solution.py:352
  22.9 8.8 %collective-permute-start.13 = (bf16[2,128,512]{2,1,0:T(8,128)(2,1)S(1)}, bf16[2,128,512]{2,1,0:T(8,128)(2,1)S(1)}, u32[]{:S(2)}, u32[]{:S(2)}) collective-permute-start(bf16[2,128,512]{2,1,0:T(8,128)(2,1)S(1)} %pad_maximum_fusion.5), channel_id=1, source_target_pairs={{0,16},{16,0},{1,17},{17,1},{2,18},{18,2},{3,19},{19,3},{4,20},{20... | collective-permute-start | bytes 786440 | tf_op jit(solution)/shard_map/ppermute | solution.py:24
  32.6 8.5 %collective-permute-start.2 = (bf16[512,128]{1,0:T(8,128)(2,1)S(1)}, bf16[512,128]{1,0:T(8,128)(2,1)S(1)}, u32[]{:S(2)}, u32[]{:S(2)}) collective-permute-start(bf16[512,128]{1,0:T(8,128)(2,1)S(1)} %copy-done.7), channel_id=1, source_target_pairs={{0,32},{32,64},{64,96},{96,0},{1,33},{33,65},{65,97},{97,1},{2,34}... | collective-permute-start | bytes 393224 | tf_op jit(solution)/shard_map/ppermute | solution.py:38
  34.4 10.8 %collective-permute-start.4 = (bf16[512,128]{1,0:T(8,128)(2,1)S(1)}, bf16[512,128]{1,0:T(8,128)(2,1)S(1)}, u32[]{:S(2)}, u32[]{:S(2)}) collective-permute-start(bf16[512,128]{1,0:T(8,128)(2,1)S(1)} %copy-done.7), channel_id=1, source_target_pairs={{0,64},{32,96},{64,0},{96,32},{1,65},{33,97},{65,1},{97,33},{2,66}... | collective-permute-start | bytes 393224 | tf_op jit(solution)/shard_map/ppermute | solution.py:38
  37.3 9.7 %collective-permute-start.3 = (bf16[512,128]{1,0:T(8,128)(2,1)S(1)}, bf16[512,128]{1,0:T(8,128)(2,1)S(1)}, u32[]{:S(2)}, u32[]{:S(2)}) collective-permute-start(bf16[512,128]{1,0:T(8,128)(2,1)S(1)} %copy-done.7), channel_id=1, source_target_pairs={{0,96},{32,0},{64,32},{96,64},{1,97},{33,1},{65,33},{97,65},{2,98}... | collective-permute-start | bytes 393224 | tf_op jit(solution)/shard_map/ppermute | solution.py:38
  47.1 23.3 %collective-permute-start.6 = (bf16[4,512,128]{2,1,0:T(8,128)(2,1)S(1)}, bf16[4,512,128]{2,1,0:T(8,128)(2,1)S(1)}, u32[]{:S(2)}, u32[]{:S(2)}) collective-permute-start(bf16[4,512,128]{2,1,0:T(8,128)(2,1)S(1)} %get-tuple-element.15), channel_id=1, source_target_pairs={{0,12},{4,0},{8,4},{12,8},{1,13},{5,1},{9,5},{13,9},{2,14},{6,2},{... | collective-permute-start | bytes 1572872 | tf_op jit(solution)/shard_map/ppermute | solution.py:38
  51.8 22.4 %collective-permute-start.5 = (bf16[4,512,128]{2,1,0:T(8,128)(2,1)S(1)}, bf16[4,512,128]{2,1,0:T(8,128)(2,1)S(1)}, u32[]{:S(2)}, u32[]{:S(2)}) collective-permute-start(bf16[4,512,128]{2,1,0:T(8,128)(2,1)S(1)} %get-tuple-element.15), channel_id=1, source_target_pairs={{0,4},{4,8},{8,12},{12,0},{1,5},{5,9},{9,13},{13,1},{2,6},{6,10},{... | collective-permute-start | bytes 1572872 | tf_op jit(solution)/shard_map/ppermute | solution.py:38
  51.8 33.4 %collective-permute-start.7 = (bf16[4,512,128]{2,1,0:T(8,128)(2,1)S(1)}, bf16[4,512,128]{2,1,0:T(8,128)(2,1)S(1)}, u32[]{:S(2)}, u32[]{:S(2)}) collective-permute-start(bf16[4,512,128]{2,1,0:T(8,128)(2,1)S(1)} %get-tuple-element.15), channel_id=1, source_target_pairs={{0,8},{4,12},{8,0},{12,4},{1,9},{5,13},{9,1},{13,5},{2,10},{6,14},... | collective-permute-start | bytes 1572872 | tf_op jit(solution)/shard_map/ppermute | solution.py:38
  85.5 8.0 %copy-start.4 = (bf16[4,4,512,128]{3,2,1,0:T(8,128)(2,1)}, bf16[4,4,512,128]{3,2,1,0:T(8,128)(2,1)S(1)}, u32[]{:S(2)}) copy-start(bf16[4,4,512,128]{3,2,1,0:T(8,128)(2,1)S(1)} %pad_maximum_fusion.rest_0_) | copy-start | bytes 6291460
  85.5 8.1 %copy-start.8 = (f32[4096]{0:T(1024)S(1)}, f32[4096]{0:T(1024)}, u32[]{:S(2)}) copy-start(f32[4096]{0:T(1024)} %param.15) | copy-start | bytes 49156
  85.5 44.5 %collective-permute-start.9 = (bf16[4,4,512,128]{3,2,1,0:T(8,128)(2,1)S(1)}, bf16[4,4,512,128]{3,2,1,0:T(8,128)(2,1)}, u32[]{:S(2)}, u32[]{:S(2)}) collective-permute-start(bf16[4,4,512,128]{3,2,1,0:T(8,128)(2,1)S(1)} %pad_maximum_fusion.rest_0_), channel_id=1, source_target_pairs={{0,18},{2,0},{16,2},{18,16},{1,19},{3,1},{17,3},{19,17},{4,22},{6,... | collective-permute-start | bytes 6291464 | tf_op jit(solution)/shard_map/ppermute | solution.py:38
  88.4 45.8 %collective-permute-start.8 = (bf16[4,4,512,128]{3,2,1,0:T(8,128)(2,1)S(1)}, bf16[4,4,512,128]{3,2,1,0:T(8,128)(2,1)}, u32[]{:S(2)}, u32[]{:S(2)}) collective-permute-start(bf16[4,4,512,128]{3,2,1,0:T(8,128)(2,1)S(1)} %pad_maximum_fusion.rest_0_), channel_id=1, source_target_pairs={{0,2},{2,16},{16,18},{18,0},{1,3},{3,17},{17,19},{19,1},{4,6},{6,2... | collective-permute-start | bytes 6291464 | tf_op jit(solution)/shard_map/ppermute | solution.py:38
  104.2 32.3 %copy-start.3 = (s32[8]{0:T(128)S(1)}, s32[8]{0:T(128)}, u32[]{:S(2)}) copy-start(s32[8]{0:T(128)} %lens_ref.7) | copy-start | bytes 100
  131.3 41.9 %collective-permute-start.11 = (bf16[2,4,512,128]{3,2,1,0:T(8,128)(2,1)S(1)}, bf16[2,4,512,128]{3,2,1,0:T(8,128)(2,1)}, u32[]{:S(2)}, u32[]{:S(2)}) collective-permute-start(bf16[2,4,512,128]{3,2,1,0:T(8,128)(2,1)S(1)} %slice.17), channel_id=1, source_target_pairs={{0,18},{2,0},{16,2},{18,16},{1,19},{3,1},{17,3},{19,17},{4,22},{6,... | collective-permute-start | bytes 3145736 | tf_op jit(solution)/shard_map/ppermute | solution.py:38
  136.5 36.8 %collective-permute-start.10 = (bf16[2,4,512,128]{3,2,1,0:T(8,128)(2,1)}, bf16[2,4,512,128]{3,2,1,0:T(8,128)(2,1)}, u32[]{:S(2)}, u32[]{:S(2)}) collective-permute-start(bf16[2,4,512,128]{3,2,1,0:T(8,128)(2,1)} %slice.16), channel_id=1, source_target_pairs={{0,2},{2,16},{16,18},{18,0},{1,3},{3,17},{17,19},{19,1},{4,6},{6,2... | collective-permute-start | bytes 3145736 | tf_op jit(solution)/shard_map/ppermute | solution.py:38
  154.0 19.2 %collective-permute-start.14 = (bf16[512,512]{1,0:T(8,128)(2,1)S(1)}, bf16[512,512]{1,0:T(8,128)(2,1)S(1)}, u32[]{:S(2)}, u32[]{:S(2)}) collective-permute-start(bf16[512,512]{1,0:T(8,128)(2,1)S(1)} %shard_map.133.mine_ref), channel_id=1, source_target_pairs={{0,2},{2,0},{1,3},{3,1},{4,6},{6,4},{5,7},{7,5},{8,10},{10,8},{9,1... | collective-permute-start | bytes 1572872 | tf_op jit(solution)/shard_map/ppermute | solution.py:24
  171.8 15.1 %collective-permute-start.1 = (bf16[512,512]{1,0:T(8,128)(2,1)S(1)}, bf16[512,512]{1,0:T(8,128)(2,1)S(1)}, u32[]{:S(2)}, u32[]{:S(2)}) collective-permute-start(bf16[512,512]{1,0:T(8,128)(2,1)S(1)} %shard_map.131.mine_ref), channel_id=1, source_target_pairs={{0,2},{2,0},{1,3},{3,1},{4,6},{6,4},{5,7},{7,5},{8,10},{10,8},{9,1... | collective-permute-start | bytes 1572872 | tf_op jit(solution)/shard_map/ppermute | solution.py:24
  186.8 14.4 %copy-start = (bf16[32,32,512]{2,1,0:T(8,128)(2,1)S(1)}, bf16[32,32,512]{2,1,0:T(8,128)(2,1)}, u32[]{:S(2)}) copy-start(bf16[32,32,512]{2,1,0:T(8,128)(2,1)} %query_ref.3) | copy-start | bytes 3145732
  186.8 14.4 %copy-start.1 = (f32[4096]{0:T(1024)S(1)}, f32[4096]{0:T(1024)}, u32[]{:S(2)}) copy-start(f32[4096]{0:T(1024)} %param.16) | copy-start | bytes 49156
  186.8 14.4 %copy-start.2 = (s32[8]{0:T(128)S(1)}, s32[8]{0:T(128)}, u32[]{:S(2)}) copy-start(s32[8]{0:T(128)} %owner_ref.5) | copy-start | bytes 100
  186.8 14.4 %collective-permute-start.15 = (bf16[512,4096]{1,0:T(8,128)(2,1)}, bf16[512,4096]{1,0:T(8,128)(2,1)}, u32[]{:S(2)}, u32[]{:S(2)}) collective-permute-start(bf16[512,4096]{1,0:T(8,128)(2,1)} %shard_map.134.mine_ref), channel_id=1, source_target_pairs={{0,1},{1,0},{2,3},{3,2},{4,5},{5,4},{6,7},{7,6},{8,9},{9,8},{10,11... | collective-permute-start | bytes 12582920 | tf_op jit(solution)/shard_map/ppermute | solution.py:24
  200.4 17.2 %collective-permute-start.12 = (bf16[512,4096]{1,0:T(8,128)(2,1)}, bf16[512,4096]{1,0:T(8,128)(2,1)}, u32[]{:S(2)}, u32[]{:S(2)}) collective-permute-start(bf16[512,4096]{1,0:T(8,128)(2,1)} %shard_map.132.mine_ref), channel_id=1, source_target_pairs={{0,1},{1,0},{2,3},{3,2},{4,5},{5,4},{6,7},{7,6},{8,9},{9,8},{10,11... | collective-permute-start | bytes 12582920 | tf_op jit(solution)/shard_map/ppermute | solution.py:24
Sparse Core Ops, SparseCore 0:
  22.9 106.2 all-gather.4
  131.4 69.4 all-gather.6

commit v4 on v3

v4 whole, which is shorter than its diff:
```python
import functools

import jax
import jax.numpy as jnp
from jax import lax
from jax.experimental import pallas as pl
from jax.experimental.pallas import tpu as pltpu
from jax.sharding import Mesh, PartitionSpec as P

HD = 64
EPS = 1e-06
SCALE = 0.125
AXES = ("y", "xh", "z", "xl", "c")
NY, NXH, NZ, NXL, NC = 4, 2, 4, 2, 2
DP = ("y", "xh", "z")
MP = ("xl", "c")
SEQ = 128
PAIR = 2 * HD
HALVES = 2
VMEM = 52 * 1024 * 1024


def swap(values, axis):
    return lax.ppermute(values, axis, [(0, 1), (1, 0)])


RING = (0, 3, 1, 2)
X_OFFSETS = ((0, 0), (3, 0), (1, 0), (2, 0), (2, 2))


def shift(values, axis, by):
    size = lax.axis_size(axis)
    return lax.ppermute(values, axis, [(i, (i + by) % size) for i in range(size)])


def ring_gather(values, axis):
    return jnp.stack([values, shift(values, axis, 1), shift(values, axis, -1), shift(values, axis, 2)])


def x_ring_pieces(values):
    below, above = shift(values, ("xh", "xl"), 1), shift(values, ("xh", "xl"), -1)
    half = values.shape[0] // 2
    return [
        values,
        below,
        above,
        shift(below[:half], ("xh", "xl"), 1),
        shift(above[half:], ("xh", "xl"), -1),
    ]


def anywhere():
    return pl.BlockSpec(memory_space=pl.ANY)


def in_smem():
    return pl.BlockSpec(memory_space=pltpu.SMEM)


def load_weights(where_ref, gathered_ref, weight, sem_w):
    xh = where_ref[1]
    for which in range(weight.shape[0]):
        for y in range(NY):
            for j in range(NXH):
                xh_from = xh if j == 0 else 1 - xh
                pltpu.make_async_copy(
                    gathered_ref.at[pl.ds(y * NZ, NZ), j, which],
                    weight.at[which, pl.ds((y * NXH + xh_from) * NZ, NZ)],
                    sem_w.at[which],
                ).start()


def attend_kernel(half, where_ref, lens_ref, normed_ref, weights_ref, out_ref, rows, weight, qkv, sem_a, sem_w):
    count, blocks, _, cols = weight.shape
    tokens = rows.shape[0]
    copy_rows = pltpu.make_async_copy(normed_ref.at[pl.ds(half * tokens, tokens)], rows, sem_a)
    copy_rows.start()
    load_weights(where_ref, weights_ref, weight, sem_w)
    copy_rows.wait()
    wide = 512
    for which in range(count):
        pltpu.make_async_copy(weight.at[which], weight.at[which], sem_w.at[which]).wait()

        def step(i, _, which=which):
            at = pl.multiple_of(i * wide, wide)
            acc = jnp.dot(
                rows[...],
                weight[which, :, :, pl.ds(at, wide)].reshape(blocks * SEQ, wide),
                preferred_element_type=jnp.float32,
            )
            qkv[which, :, pl.ds(at, wide)] = acc.astype(jnp.bfloat16)
            return 0

        lax.fori_loop(0, cols // wide, step, 0)

    lane = lax.broadcasted_iota(jnp.int32, (1, PAIR), 1)
    low = (lane < HD).astype(jnp.bfloat16)
    high = (lane >= HD).astype(jnp.bfloat16)

    def one(p, _):
        at = pl.multiple_of(p * SEQ, SEQ)
        seen = lane < lens_ref[half * (tokens // SEQ) + p]
        for hp in range(cols // PAIR):
            here = slice(hp * PAIR, (hp + 1) * PAIR)
            q = qkv[0, pl.ds(at, SEQ), here]
            k = qkv[1, pl.ds(at, SEQ), here]
            v = qkv[2, pl.ds(at, SEQ), here]
            q_two = jnp.concatenate([q * low, q * high], axis=0)
            scores = lax.dot_general(q_two, k, (((1,), (1,)), ((), ())), preferred_element_type=jnp.float32) * SCALE
            expon = jnp.where(seen, jnp.exp(scores), 0.0)
            share = (expon / jnp.sum(expon, axis=-1, keepdims=True)).astype(jnp.bfloat16)
            both = jnp.dot(share, v, preferred_element_type=jnp.float32)
            out_ref[pl.ds(at, SEQ), here] = jnp.where(lane < HD, both[:SEQ], both[SEQ:]).astype(jnp.bfloat16)
        return 0

    lax.fori_loop(0, tokens // SEQ, one, 0)


def attend(half, where, lengths, normed, gathered):
    total, width = normed.shape
    tokens = total // HALVES
    cols = gathered.shape[-1]
    return pl.pallas_call(
        functools.partial(attend_kernel, half),
        out_shape=jax.ShapeDtypeStruct((tokens, cols), jnp.bfloat16),
        in_specs=[in_smem(), in_smem(), anywhere(), anywhere()],
        out_specs=pl.BlockSpec(memory_space=pltpu.VMEM),
        scratch_shapes=[
            pltpu.VMEM((tokens, width), jnp.bfloat16),
            pltpu.VMEM((3, width // SEQ, SEQ, cols), jnp.bfloat16),
            pltpu.VMEM((3, tokens, cols), jnp.bfloat16),
            pltpu.SemaphoreType.DMA,
            pltpu.SemaphoreType.DMA((3,)),
        ],
        compiler_params=pltpu.CompilerParams(vmem_limit_bytes=VMEM),
        cost_estimate=pl.CostEstimate(flops=2 * tokens * width * cols * 3, bytes_accessed=18 << 20, transcendentals=tokens * SEQ * 8),
    )(where, lengths, normed, gathered)


def output_kernel(where_ref, mine_ref, other_ref, *rest):
    pieces, (out_ref, rows, weight, sem_a, sem_w) = rest[: len(X_OFFSETS)], rest[len(X_OFFSETS) :]
    tokens, cols = mine_ref.shape
    y, xh, z, xl = (where_ref[i] for i in range(4))
    mine_at = pl.multiple_of(xl * cols, cols)
    other_at = pl.multiple_of((1 - xl) * cols, cols)
    pltpu.make_async_copy(mine_ref, rows.at[:, pl.ds(mine_at, cols)], sem_a).start()
    pltpu.make_async_copy(other_ref, rows.at[:, pl.ds(other_at, cols)], sem_a).start()
    for piece, (dx, first) in zip(pieces, X_OFFSETS):
        x_from = lax.rem(xh * NXL + xl + dx, NXH * NXL)
        row = pl.multiple_of(lax.rem(x_from, NXL) * cols, cols)
        for i in range(piece.shape[0]):
            z_from = lax.rem(z + RING[first + i], NZ)
            for j in range(NY):
                y_from = lax.rem(y + RING[j], NY)
                block = (y_from * NXH + x_from // NXL) * NZ + z_from
                at = pl.multiple_of(block * SEQ, SEQ)
                pltpu.make_async_copy(
                    piece.at[i, j], weight.at[pl.ds(row, cols), pl.ds(at, SEQ)], sem_w.at[y_from]
                ).start()
    pltpu.make_async_copy(rows, rows, sem_a).wait()
    part = weight.shape[1] // NY
    wide = 512
    for q in range(NY):
        quarter = weight.at[:, pl.ds(q * part, part)]
        pltpu.make_async_copy(quarter, quarter, sem_w.at[q]).wait()

        def step(i, _, q=q):
            at = pl.multiple_of(q * part + i * wide, wide)
            acc = jnp.dot(rows[...], weight[:, pl.ds(at, wide)], preferred_element_type=jnp.float32)
            out_ref[:, pl.ds(at, wide)] = acc.astype(jnp.bfloat16)
            return 0

        lax.fori_loop(0, part // wide, step, 0)


def output(where, mine, other, pieces, width):
    tokens, cols = mine.shape
    return pl.pallas_call(
        output_kernel,
        out_shape=jax.ShapeDtypeStruct((tokens, width), jnp.bfloat16),
        in_specs=[in_smem()] + [anywhere()] * (2 + len(pieces)),
        out_specs=pl.BlockSpec(memory_space=pltpu.VMEM),
        scratch_shapes=[
            pltpu.VMEM((tokens, 2 * cols), jnp.bfloat16),
            pltpu.VMEM((2 * cols, width), jnp.bfloat16),
            pltpu.SemaphoreType.DMA,
            pltpu.SemaphoreType.DMA((NY,)),
        ],
        compiler_params=pltpu.CompilerParams(vmem_limit_bytes=VMEM),
        cost_estimate=pl.CostEstimate(flops=4 * tokens * width * cols, bytes_accessed=13 << 20, transcendentals=0),
    )(where, mine, other, *pieces)


def encode_kernel(gain_ref, passages_ref, mine_ref, other_ref, *rest):
    encoded_ref, final_ref = rest[-2:]
    floats = passages_ref[...].astype(jnp.float32)
    summed = mine_ref[...].astype(jnp.float32) + other_ref[...].astype(jnp.float32)
    encoded = (floats + summed).astype(jnp.bfloat16)
    encoded_ref[...] = encoded
    values = encoded.astype(jnp.float32)
    mean = jnp.mean(values * values, axis=-1, keepdims=True)
    final_ref[...] = (values * lax.rsqrt(mean + EPS) * gain_ref[...]).astype(jnp.bfloat16)


def encode(half, gain, passages, mine, other, prior):
    tokens, width = mine.shape
    steps = tokens // SEQ
    block = (SEQ, width)
    in_specs = [
        pl.BlockSpec((1, width), lambda i: (0, 0)),
        pl.BlockSpec(block, lambda i: (half * steps + i, 0)),
        pl.BlockSpec(block, lambda i: (i, 0)),
        pl.BlockSpec(block, lambda i: (i, 0)),
    ]
    args = [gain, passages, mine, other]
    aliases = {}
    if prior is not None:
        in_specs += [anywhere()]
        args += [prior]
        aliases = {4: 0}
    return pl.pallas_call(
        encode_kernel,
        grid=(steps,),
        out_shape=(
            jax.ShapeDtypeStruct(passages.shape, jnp.bfloat16),
            jax.ShapeDtypeStruct((tokens, width), jnp.bfloat16),
        ),
        in_specs=in_specs,
        out_specs=(pl.BlockSpec(block, lambda i: (half * steps + i, 0)), pl.BlockSpec(block, lambda i: (i, 0))),
        input_output_aliases=aliases,
        compiler_params=pltpu.CompilerParams(vmem_limit_bytes=32 * 1024 * 1024),
        cost_estimate=pl.CostEstimate(flops=8 * tokens * width, bytes_accessed=20 << 20, transcendentals=0),
    )(*args)


def decode_kernel(where_ref, lens_ref, owner_ref, query_ref, *rest):
    finals, rest = rest[:HALVES], rest[HALVES:]
    weights_ref, sent_ref, final, weight, kv, numer, sem_a, sem_w = rest
    count, blocks, _, cols = weight.shape
    tokens = final.shape[1]
    for half in range(HALVES):
        pltpu.make_async_copy(finals[half], final.at[half], sem_a.at[half]).start()
    load_weights(where_ref, weights_ref, weight, sem_w)
    numer[...] = jnp.zeros_like(numer)

    lane = lax.broadcasted_iota(jnp.int32, (1, PAIR), 1)
    low = (lane < HD).astype(jnp.bfloat16)
    high = (lane >= HD).astype(jnp.bfloat16)
    dec_len = query_ref.shape[1]
    wide = 256
    for half in range(HALVES):
        pltpu.make_async_copy(final.at[half], final.at[half], sem_a.at[half]).wait()
        for which in range(count):
            if half == 0:
                pltpu.make_async_copy(weight.at[which], weight.at[which], sem_w.at[which]).wait()

            def column(i, _, which=which, half=half):
                at = pl.multiple_of(i * wide, wide)
                acc = jnp.dot(
                    final[half],
                    weight[which, :, :, pl.ds(at, wide)].reshape(blocks * SEQ, wide),
                    preferred_element_type=jnp.float32,
                )
                kv[which, :, pl.ds(at, wide)] = acc.astype(jnp.bfloat16)
                return 0

            lax.fori_loop(0, cols // wide, column, 0)

        def one(p, _, half=half):
            at = pl.multiple_of(p * SEQ, SEQ)
            seen = lane < lens_ref[half * (tokens // SEQ) + p]
            question = owner_ref[half * (tokens // SEQ) + p]
            totals = jnp.zeros((dec_len, PAIR), jnp.float32)
            for hp in range(cols // PAIR):
                here = slice(hp * PAIR, (hp + 1) * PAIR)
                q = query_ref[question, :, here]
                k = kv[0, pl.ds(at, SEQ), here]
                v = kv[1, pl.ds(at, SEQ), here]
                q_two = jnp.concatenate([q * low, q * high], axis=0)
                scores = lax.dot_general(q_two, k, (((1,), (1,)), ((), ())), preferred_element_type=jnp.float32) * SCALE
                expon = jnp.where(seen, jnp.exp(scores), 0.0)
                total = jnp.sum(expon, axis=-1, keepdims=True)
                coarse = expon.astype(jnp.bfloat16)
                fine = (expon - coarse.astype(jnp.float32)).astype(jnp.bfloat16)
                both = jnp.dot(coarse, v, preferred_element_type=jnp.float32) + jnp.dot(
                    fine, v, preferred_element_type=jnp.float32
                )
                numer[question, :, here] += jnp.where(lane < HD, both[:dec_len], both[dec_len:])
                totals = jnp.where(lane == 2 * hp, total[:dec_len], totals)
                totals = jnp.where(lane == 2 * hp + 1, total[dec_len:], totals)
            numer[question, :, cols : cols + PAIR] += totals
            return 0

        lax.fori_loop(0, tokens // SEQ, one, 0)
    sent_ref[...] = numer[...].astype(jnp.bfloat16)


def decode(where, lengths, owner, query, finals, gathered):
    tokens, width = finals[0].shape
    questions, dec_len, cols = query.shape
    shape = (questions, dec_len, cols + PAIR)
    return pl.pallas_call(
        decode_kernel,
        out_shape=jax.ShapeDtypeStruct(shape, jnp.bfloat16),
        in_specs=[in_smem()] * 3 + [pl.BlockSpec(memory_space=pltpu.VMEM)] + [anywhere()] * (HALVES + 1),
        out_specs=pl.BlockSpec(memory_space=pltpu.VMEM),
        scratch_shapes=[
            pltpu.VMEM((HALVES, tokens, width), jnp.bfloat16),
            pltpu.VMEM((2, width // SEQ, SEQ, cols), jnp.bfloat16),
            pltpu.VMEM((2, tokens, cols), jnp.bfloat16),
            pltpu.VMEM(shape, jnp.float32),
            pltpu.SemaphoreType.DMA((HALVES,)),
            pltpu.SemaphoreType.DMA((2,)),
        ],
        compiler_params=pltpu.CompilerParams(vmem_limit_bytes=VMEM),
        cost_estimate=pl.CostEstimate(
            flops=4 * HALVES * tokens * width * cols, bytes_accessed=18 << 20, transcendentals=1 << 18
        ),
    )(where, lengths, owner, query, *finals, gathered)


def gather_rows(mine, other):
    both = jnp.stack([mine, other])
    return lax.all_gather(both, ("y", "z"), axis=0, tiled=False).reshape((NY * NZ,) + both.shape)


def shards(
    passages,
    lengths,
    owner,
    enc_gain,
    final_gain,
    enc_wq,
    enc_wk,
    enc_wv,
    enc_wo,
    dec_wk,
    dec_wv,
    dec_query,
):
    pass_count, seq_len, width = passages.shape
    tok_rows = pass_count * seq_len
    local_cols = enc_wq.shape[1]
    local_heads = local_cols // HD
    dec_len = dec_query.shape[1]
    flat = passages.reshape(tok_rows, width)
    floats = flat.astype(jnp.float32)
    mean = jnp.mean(floats * floats, axis=-1, keepdims=True)
    normed = (floats * lax.rsqrt(mean + EPS) * enc_gain).astype(jnp.bfloat16)

    enc = jnp.stack([enc_wq, enc_wk, enc_wv])
    enc_other = swap(enc, "xh")
    wo = ring_gather(enc_wo, "y")
    enc, enc_other, wo = lax.optimization_barrier((enc, enc_other, wo))
    qkv = gather_rows(enc, enc_other)
    wo = ring_gather(wo, "z")
    dec, wo = lax.optimization_barrier((jnp.stack([dec_wk, dec_wv]), wo))
    dkv = gather_rows(dec, swap(dec, "xh"))
    wo = x_ring_pieces(wo)
    where = jnp.stack([lax.axis_index(axis) for axis in AXES]).astype(jnp.int32)
    mine = [attend(half, where, lengths, normed, qkv) for half in range(HALVES)]
    theirs = [swap(part, "xl") for part in mine]
    partial = [output(where, mine[half], theirs[half], wo, width) for half in range(HALVES)]
    partial_other = [swap(part, "c") for part in partial]
    encoded = None
    finals = []
    for half in range(HALVES):
        encoded, final = encode(half, final_gain.reshape(1, width), flat, partial[half], partial_other[half], encoded)
        finals.append(final)
    sent = decode(where, lengths, owner, dec_query, finals, dkv)
    came = lax.all_to_all(sent, DP, 0, 0, tiled=True).astype(jnp.float32)
    came = jnp.sum(came, axis=0)
    own_numer = came[:, :local_cols].reshape(dec_len, local_heads, HD)
    own_total = came[:, local_cols : local_cols + local_heads].reshape(dec_len, local_heads, 1)
    context = (own_numer / own_total).astype(jnp.bfloat16).reshape(1, dec_len, local_cols)
    return (encoded.reshape(pass_count, seq_len, width), context)


def solution(mesh):
    fine = Mesh(mesh.devices.reshape((NY, NXH, NZ, NXL, NC)), AXES)
    row = P(DP, MP)
    return jax.shard_map(
        shards,
        mesh=fine,
        in_specs=(
            P(DP, None, None),
            P(DP),
            P(DP),
            P(),
            P(),
            row,
            row,
            row,
            P(MP, DP),
            row,
            row,
            P(None, None, MP),
        ),
        out_specs=(P(DP, None, None), P(DP, None, MP)),
        check_vma=False,
    )
```

time: 272 us -> 262 us (0.963)
  waiting for transfers between devices: 80.7 us -> 72 us
  Pallas kernels: 95 us -> 88.4 us
  local copies, waits for them, and re-layouts: 3.93 us -> 10.1 us
    ppermute x6, waiting for transfers between devices: 14.6 us -> 6.98 us  [swap(): return lax.ppermute(values, axis, [(0, 1), (1, 0)])]
    unnamed x18 -> x28, local copies, waits for them, and re-layouts: 0.05 us -> 6.22 us
    pallas_call x5, Pallas kernels: 68.1 us -> 63.4 us  [the longest x2 32.4 us: attend(): pl.pallas_call(functools.partial(attend_kernel, half), out_shape=jax.Shap...]
  transfers between devices with their start and end apart: 18 -> 18, of which waited for: 9 -> 8; matrix products, arithmetic and copies ran while one was open for 8% -> 8% of each run, Pallas kernels for 29% -> 26%
where the time goes in v4:
time: 262 us
  Pallas kernels  88.4 us (34%)
  waiting for transfers between devices  72 us (27%)
  blocking collectives  31 us (12%)
  starting transfers between devices  25.3 us (10%)
  other arithmetic  20.6 us (8%)
  between operations  14.3 us (5%)
  local copies, waits for them, and re-layouts  10.1 us (4%)
    ppermute x10, waiting for transfers between devices, shift(): lax.ppermute(values, axis, [(i, (i + by) % size) for i in range(size)])  63.8 us
    pallas_call x2, Pallas kernels, attend(): pl.pallas_call(functools.partial(attend_kernel, half), out_shape=jax.Shap...  32.4 us
    all_to_all x1, blocking collectives, shards(): came = lax.all_to_all(sent, DP, 0, 0, tiled=True).astype(jnp.float32)  31 us
    pallas_call x2, Pallas kernels, output(): pl.pallas_call(output_kernel, out_shape=jax.ShapeDtypeStruct((tokens, wid...  25 us
    pallas_call x1, Pallas kernels, decode(): pl.pallas_call(decode_kernel, out_shape=jax.ShapeDtypeStruct(shape, jnp.b...  19.6 us
    ppermute x10, starting transfers between devices, shift(): lax.ppermute(values, axis, [(i, (i + by) % size) for i in range(size)])  17.7 us
    pallas_call x2, Pallas kernels, encode(): pl.pallas_call(encode_kernel, grid=(steps,), out_shape=(jax.ShapeDtypeStr...  11.4 us
    convert_element_type x1, other arithmetic, shards(): normed = (floats * lax.rsqrt(mean + EPS) * enc_gain).astype(jnp.bfloat16)  10.5 us
  transfers between devices with their start and end apart: 18, of which 8 were waited for; matrix products, arithmetic and copies ran while one was open for 8% of the time, Pallas kernels for 26%

profile of v4, /device:TPU:0, one launch (start us, length us, event | category | flops | bytes accessed | tf_op | source)
XLA Modules:
  0.0 261.7 jit_solution(7275708355542627493)
XLA Ops:
  7.2 1.1 pad_maximum_fusion.4
  8.4 3.2 %collective-permute-start = (bf16[3,128,512]{2,1,0:T(8,128)(2,1)S(1)}, bf16[3,128,512]{2,1,0:T(8,128)(2,1)S(1)}, u32[]{:S(2)}, u32[]{:S(2)}) collective-permute-start(bf16[3,128,512]{2,1,0:T(8,128)(2,1)S(1)} %pad_maximum_fusion.4), channel_id=1, source_target_pairs={{0,16},{16,0},{1,17},{17,1},{2,18},{18,2},{3,19},{19,3},{4,20},{20... | collective-permute-start | bytes 1179656 | tf_op jit(solution)/shard_map/ppermute | solution.py:24
  11.6 3.2 %collective-permute-start.3 = (bf16[512,128]{1,0:T(8,128)(2,1)}, bf16[512,128]{1,0:T(8,128)(2,1)S(1)}, u32[]{:S(2)}, u32[]{:S(2)}) collective-permute-start(bf16[512,128]{1,0:T(8,128)(2,1)} %param.20), channel_id=1, source_target_pairs={{0,64},{32,96},{64,0},{96,32},{1,65},{33,97},{65,1},{97,33},{2,66}... | collective-permute-start | bytes 393224 | tf_op jit(solution)/shard_map/ppermute | solution.py:33
  14.8 1.1 collective-permute-start.2
  16.8 2.2 collective-permute-done.3
  18.9 2.4 collective-permute-done.2
  24.2 4.0 %collective-permute-start.7 = (bf16[4,512,128]{2,1,0:T(8,128)(2,1)S(1)}, bf16[4,512,128]{2,1,0:T(8,128)(2,1)S(1)}, u32[]{:S(2)}, u32[]{:S(2)}) collective-permute-start(bf16[4,512,128]{2,1,0:T(8,128)(2,1)S(1)} %pad_maximum_fusion.2), channel_id=1, source_target_pairs={{0,8},{4,12},{8,0},{12,4},{1,9},{5,13},{9,1},{13,5},{2,10},{6,14},... | collective-permute-start | bytes 1572872 | tf_op jit(solution)/shard_map/ppermute | solution.py:33
  28.9 1.3 collective-permute-start.5
  30.2 15.3 %collective-permute-done.7 = bf16[4,512,128]{2,1,0:T(8,128)(2,1)S(1)} collective-permute-done((bf16[4,512,128]{2,1,0:T(8,128)(2,1)S(1)}, bf16[4,512,128]{2,1,0:T(8,128)(2,1)S(1)}, u32[]{:S(2)}, u32[]{:S(2)}) %collective-permute-start.7) | collective-permute-done | bytes 524320 | tf_op jit(solution)/shard_map/ppermute | solution.py:33
  45.5 17.6 %collective-permute-done.6 = bf16[4,512,128]{2,1,0:T(8,128)(2,1)S(1)} collective-permute-done((bf16[4,512,128]{2,1,0:T(8,128)(2,1)S(1)}, bf16[4,512,128]{2,1,0:T(8,128)(2,1)S(1)}, u32[]{:S(2)}, u32[]{:S(2)}) %collective-permute-start.6) | collective-permute-done | bytes 524320 | tf_op jit(solution)/shard_map/ppermute | solution.py:33
  63.4 1.6 collective-permute-start.15
  65.0 7.0 %collective-permute-done.15 = bf16[2,128,512]{2,1,0:T(8,128)(2,1)S(1)} collective-permute-done((bf16[2,128,512]{2,1,0:T(8,128)(2,1)S(1)}, bf16[2,128,512]{2,1,0:T(8,128)(2,1)S(1)}, u32[]{:S(2)}, u32[]{:S(2)}) %collective-permute-start.15) | collective-permute-done | bytes 262176 | tf_op jit(solution)/shard_map/ppermute | solution.py:24
  72.9 3.2 %collective-permute-start.9 = (bf16[4,4,512,128]{3,2,1,0:T(8,128)(2,1)S(1)}, bf16[4,4,512,128]{3,2,1,0:T(8,128)(2,1)}, u32[]{:S(2)}, u32[]{:S(2)}) collective-permute-start(bf16[4,4,512,128]{3,2,1,0:T(8,128)(2,1)S(1)} %pad_maximum_fusion.rest_0_), channel_id=1, source_target_pairs={{0,18},{2,0},{16,2},{18,16},{1,19},{3,1},{17,3},{19,17},{4,22},{6,... | collective-permute-start | bytes 6291464 | tf_op jit(solution)/shard_map/ppermute | solution.py:33
  76.1 5.1 %multiply_reduce_fusion = f32[8,128]{1,0:T(8,128)S(1)} fusion(bf16[8,128,4096]{2,1,0:T(8,128)(2,1)} %param.12), kind=kLoop, calls=%fused_computation.1 | loop fusion | flops 12581888 | bytes 8392704 | tf_op jit(solution)/shard_map/reduce_sum | solution.py:348
  81.3 10.5 %multiply_convert_fusion.normed_ref = bf16[1024,4096]{1,0:T(8,128)(2,1)} fusion(f32[4096]{0:T(1024)S(1)} %copy-done.11, f32[1024]{0:T(1024)S(1)} %rsqrt_bitcast_fusion, bf16[8,128,4096]{2,1,0:T(8,128)(2,1)} %param.12), kind=kLoop, calls=%fused_computation | loop fusion | flops 16777216 | bytes 16797696 | tf_op jit(solution)/shard_map/convert_element_type | solution.py:349
  91.8 25.5 %collective-permute-done.8.rest_1_ = bf16[4,4,512,128]{3,2,1,0:T(8,128)(2,1)} collective-permute-done((bf16[4,4,512,128]{3,2,1,0:T(8,128)(2,1)S(1)}, bf16[4,4,512,128]{3,2,1,0:T(8,128)(2,1)}, u32[]{:S(2)}, u32[]{:S(2)}) %collective-permute-start.8) | collective-permute-done | bytes 2097184 | tf_op jit(solution)/shard_map/ppermute | solution.py:33
  117.3 1.3 slice.16
  118.7 2.3 slice.17
  121.0 3.2 %collective-permute-start.11 = (bf16[2,4,512,128]{3,2,1,0:T(8,128)(2,1)}, bf16[2,4,512,128]{3,2,1,0:T(8,128)(2,1)}, u32[]{:S(2)}, u32[]{:S(2)}) collective-permute-start(bf16[2,4,512,128]{3,2,1,0:T(8,128)(2,1)} %slice.17), channel_id=1, source_target_pairs={{0,18},{2,0},{16,2},{18,16},{1,19},{3,1},{17,3},{19,17},{4,22},{6,... | collective-permute-start | bytes 3145736 | tf_op jit(solution)/shard_map/ppermute | solution.py:33
  124.2 1.1 all-gather.5.cloned.1.call-done
  125.4 16.1 %shard_map.133.mine_ref = bf16[512,512]{1,0:T(8,128)(2,1)S(1)} custom-call(s32[5]{0:T(128)S(1)} %stack.92.where_ref, s32[8]{0:T(128)S(1)} %copy-done.6, bf16[1024,4096]{1,0:T(8,128)(2,1)} %multiply_convert_fusion.normed_ref, bf16[16,2,3,128,512]{4,3,2,1,0:T(8,128)(2,1)} %bitcast.56), custom_call_target="tpu_custom_call" | custom-call | flops 6442450944 | bytes 18874368 | tf_op jit(solution)/shard_map/pallas_call | solution.py:123
  141.5 1.5 collective-permute-start.13
  143.1 16.3 %shard_map.131.mine_ref = bf16[512,512]{1,0:T(8,128)(2,1)S(1)} custom-call(s32[5]{0:T(128)S(1)} %stack.92.where_ref, s32[8]{0:T(128)S(1)} %copy-done.6, bf16[1024,4096]{1,0:T(8,128)(2,1)} %multiply_convert_fusion.normed_ref, bf16[16,2,3,128,512]{4,3,2,1,0:T(8,128)(2,1)} %bitcast.57), custom_call_target="tpu_custom_call" | custom-call | flops 6442450944 | bytes 18874368 | tf_op jit(solution)/shard_map/pallas_call | solution.py:123
  160.1 12.7 %shard_map.134.mine_ref = bf16[512,4096]{1,0:T(8,128)(2,1)} custom-call(s32[5]{0:T(128)S(1)} %stack.92.where_ref, bf16[512,512]{1,0:T(8,128)(2,1)S(1)} %shard_map.133.mine_ref, bf16[512,512]{1,0:T(8,128)(2,1)S(1)} %collective-permute-done.13.other_ref, bf16[4,4,512,128]{3,2,1,0:T(8,128)(2,1)} %copy-done.8, ...), custom_call_target="tpu_custom_call" | custom-call | flops 4294967296 | bytes 13631488 | tf_op jit(solution)/shard_map/pallas_call | solution.py:178
  173.1 12.3 %shard_map.132.mine_ref = bf16[512,4096]{1,0:T(8,128)(2,1)} custom-call(s32[5]{0:T(128)S(1)} %stack.92.where_ref, bf16[512,512]{1,0:T(8,128)(2,1)S(1)} %shard_map.131.mine_ref, bf16[512,512]{1,0:T(8,128)(2,1)S(1)} %collective-permute-done.4.other_ref, bf16[4,4,512,128]{3,2,1,0:T(8,128)(2,1)} %copy-done.8, ...), custom_call_target="tpu_custom_call" | custom-call | flops 4294967296 | bytes 13631488 | tf_op jit(solution)/shard_map/pallas_call | solution.py:178
  185.7 2.2 copy-done
  187.9 5.7 %shard_map.135 = (bf16[1024,4096]{1,0:T(8,128)(2,1)}, bf16[512,4096]{1,0:T(8,128)(2,1)S(1)}) custom-call(f32[1,4096]{1,0:T(1,128)S(1)} %bitcast.36, bf16[1024,4096]{1,0:T(8,128)(2,1)S(1)} %bitcast.34, bf16[512,4096]{1,0:T(8,128)(2,1)S(1)} %copy-done, bf16[512,4096]{1,0:T(8,128)(2,1)} %collective-permute-done.14.other_ref), custom_call_target="tpu_custom_call" | custom-call | flops 16777216 | bytes 20971520 | tf_op jit(solution)/shard_map/pallas_call | solution.py:221
  193.6 2.0 copy-done.3
  195.7 5.7 %shard_map.136 = (bf16[1024,4096]{1,0:T(8,128)(2,1)}, bf16[512,4096]{1,0:T(8,128)(2,1)S(1)}) custom-call(f32[1,4096]{1,0:T(1,128)S(1)} %bitcast.37, bf16[1024,4096]{1,0:T(8,128)(2,1)S(1)} %bitcast.35, bf16[512,4096]{1,0:T(8,128)(2,1)S(1)} %copy-done.1, bf16[512,4096]{1,0:T(8,128)(2,1)} %collective-permute-done.12.other_ref, ...), custom_call_target="tpu_custom_call", output_to_operand_aliasing={{0}: (4, {})} | custom-call | flops 16777216 | bytes 20971520 | tf_op jit(solution)/shard_map/pallas_call | solution.py:221
  201.3 2.0 copy-done.4
  203.3 19.6 %shard_map.137 = bf16[32,32,640]{2,1,0:T(8,128)(2,1)} custom-call(s32[5]{0:T(128)S(1)} %stack.92.where_ref, s32[8]{0:T(128)S(1)} %copy-done.6, s32[8]{0:T(128)S(1)} %copy-done.7, bf16[32,32,512]{2,1,0:T(8,128)(2,1)S(1)} %copy-done.5, bf16[512,4096]{1,0:T(8,128)(2,1)} %copy-done.3, bf16[512,4096]{1,0:T(8,128)(2,1)} %copy-done.4, ...), custom_call_target="tpu_custom_call" | custom-call | flops 8589934592 | bytes 18874368 | tf_op jit(solution)/shard_map/pallas_call | solution.py:302
  222.9 31.0 %all_to_all.5 = bf16[32,32,640]{2,1,0:T(8,128)(2,1)S(1)} all-to-all(bf16[32,32,640]{2,1,0:T(8,128)(2,1)} %shard_map.137), channel_id=1, replica_groups=mesh['y'=4,'xh'=2,'z'=4,'xl'=2,'c'=2] {'y','xh','z'}, dimensions={0} | all-to-all | bytes 2621440 | tf_op jit(solution)/shard_map/all_to_all | solution.py:371
  (60 shorter events, 8.2 us)
Async XLA Ops:
  7.2 23.0 %copy-start.9 = (bf16[128,512]{1,0:T(8,128)(2,1)S(1)}, bf16[128,512]{1,0:T(8,128)(2,1)}, u32[]{:S(2)}) copy-start(bf16[128,512]{1,0:T(8,128)(2,1)} %param.22) | copy-start | bytes 393220
  7.2 23.0 %copy-start.10 = (bf16[128,512]{1,0:T(8,128)(2,1)S(1)}, bf16[128,512]{1,0:T(8,128)(2,1)}, u32[]{:S(2)}) copy-start(bf16[128,512]{1,0:T(8,128)(2,1)} %param.21) | copy-start | bytes 393220
  7.2 118.2 %all-gather.5.cloned.1.call-start = ((), (), s32[]{:S(2)}) async-start(), calls=%async_computation.1 | async-start | bytes 13369344 | tf_op jit(solution)/shard_map/all_gather | solution.py:324
  8.4 14.8 %collective-permute-start = (bf16[3,128,512]{2,1,0:T(8,128)(2,1)S(1)}, bf16[3,128,512]{2,1,0:T(8,128)(2,1)S(1)}, u32[]{:S(2)}, u32[]{:S(2)}) collective-permute-start(bf16[3,128,512]{2,1,0:T(8,128)(2,1)S(1)} %pad_maximum_fusion.4), channel_id=1, source_target_pairs={{0,16},{16,0},{1,17},{17,1},{2,18},{18,2},{3,19},{19,3},{4,20},{20... | collective-permute-start | bytes 1179656 | tf_op jit(solution)/shard_map/ppermute | solution.py:24
  11.6 7.4 %collective-permute-start.3 = (bf16[512,128]{1,0:T(8,128)(2,1)}, bf16[512,128]{1,0:T(8,128)(2,1)S(1)}, u32[]{:S(2)}, u32[]{:S(2)}) collective-permute-start(bf16[512,128]{1,0:T(8,128)(2,1)} %param.20), channel_id=1, source_target_pairs={{0,64},{32,96},{64,0},{96,32},{1,65},{33,97},{65,1},{97,33},{2,66}... | collective-permute-start | bytes 393224 | tf_op jit(solution)/shard_map/ppermute | solution.py:33
  14.8 6.6 %collective-permute-start.2 = (bf16[512,128]{1,0:T(8,128)(2,1)}, bf16[512,128]{1,0:T(8,128)(2,1)S(1)}, u32[]{:S(2)}, u32[]{:S(2)}) collective-permute-start(bf16[512,128]{1,0:T(8,128)(2,1)} %param.20), channel_id=1, source_target_pairs={{0,96},{32,0},{64,32},{96,64},{1,97},{33,1},{65,33},{97,65},{2,98}... | collective-permute-start | bytes 393224 | tf_op jit(solution)/shard_map/ppermute | solution.py:33
  15.8 6.4 %collective-permute-start.1 = (bf16[512,128]{1,0:T(8,128)(2,1)}, bf16[512,128]{1,0:T(8,128)(2,1)S(1)}, u32[]{:S(2)}, u32[]{:S(2)}) collective-permute-start(bf16[512,128]{1,0:T(8,128)(2,1)} %param.20), channel_id=1, source_target_pairs={{0,32},{32,64},{64,96},{96,0},{1,33},{33,65},{65,97},{97,1},{2,34}... | collective-permute-start | bytes 393224 | tf_op jit(solution)/shard_map/ppermute | solution.py:33
  24.2 179.1 %all-gather.7.cloned.1.call-start = ((), (), s32[]{:S(2)}) async-start(), calls=%async_computation.2 | async-start | bytes 8912896 | tf_op jit(solution)/shard_map/all_gather | solution.py:324
  24.2 21.3 %collective-permute-start.7 = (bf16[4,512,128]{2,1,0:T(8,128)(2,1)S(1)}, bf16[4,512,128]{2,1,0:T(8,128)(2,1)S(1)}, u32[]{:S(2)}, u32[]{:S(2)}) collective-permute-start(bf16[4,512,128]{2,1,0:T(8,128)(2,1)S(1)} %pad_maximum_fusion.2), channel_id=1, source_target_pairs={{0,8},{4,12},{8,0},{12,4},{1,9},{5,13},{9,1},{13,5},{2,10},{6,14},... | collective-permute-start | bytes 1572872 | tf_op jit(solution)/shard_map/ppermute | solution.py:33
  28.2 34.9 %collective-permute-start.6 = (bf16[4,512,128]{2,1,0:T(8,128)(2,1)S(1)}, bf16[4,512,128]{2,1,0:T(8,128)(2,1)S(1)}, u32[]{:S(2)}, u32[]{:S(2)}) collective-permute-start(bf16[4,512,128]{2,1,0:T(8,128)(2,1)S(1)} %pad_maximum_fusion.2), channel_id=1, source_target_pairs={{0,12},{4,0},{8,4},{12,8},{1,13},{5,1},{9,5},{13,9},{2,14},{6,2},{... | collective-permute-start | bytes 1572872 | tf_op jit(solution)/shard_map/ppermute | solution.py:33
  28.9 34.2 %collective-permute-start.5 = (bf16[4,512,128]{2,1,0:T(8,128)(2,1)S(1)}, bf16[4,512,128]{2,1,0:T(8,128)(2,1)S(1)}, u32[]{:S(2)}, u32[]{:S(2)}) collective-permute-start(bf16[4,512,128]{2,1,0:T(8,128)(2,1)S(1)} %pad_maximum_fusion.2), channel_id=1, source_target_pairs={{0,4},{4,8},{8,12},{12,0},{1,5},{5,9},{9,13},{13,1},{2,6},{6,10},{... | collective-permute-start | bytes 1572872 | tf_op jit(solution)/shard_map/ppermute | solution.py:33
  63.4 17.8 %copy-start.8 = (bf16[4,4,512,128]{3,2,1,0:T(8,128)(2,1)}, bf16[4,4,512,128]{3,2,1,0:T(8,128)(2,1)S(1)}, u32[]{:S(2)}) copy-start(bf16[4,4,512,128]{3,2,1,0:T(8,128)(2,1)S(1)} %pad_maximum_fusion.rest_0_) | copy-start | bytes 6291460
  63.4 8.5 %collective-permute-start.15 = (bf16[2,128,512]{2,1,0:T(8,128)(2,1)S(1)}, bf16[2,128,512]{2,1,0:T(8,128)(2,1)S(1)}, u32[]{:S(2)}, u32[]{:S(2)}) collective-permute-start(bf16[2,128,512]{2,1,0:T(8,128)(2,1)S(1)} %pad_maximum_fusion.5), channel_id=1, source_target_pairs={{0,16},{16,0},{1,17},{17,1},{2,18},{18,2},{3,19},{19,3},{4,20},{20... | collective-permute-start | bytes 786440 | tf_op jit(solution)/shard_map/ppermute | solution.py:24
  72.9 8.3 %copy-start.11 = (f32[4096]{0:T(1024)S(1)}, f32[4096]{0:T(1024)}, u32[]{:S(2)}) copy-start(f32[4096]{0:T(1024)} %param.15) | copy-start | bytes 49156
  72.9 44.4 %collective-permute-start.8 = (bf16[4,4,512,128]{3,2,1,0:T(8,128)(2,1)S(1)}, bf16[4,4,512,128]{3,2,1,0:T(8,128)(2,1)}, u32[]{:S(2)}, u32[]{:S(2)}) collective-permute-start(bf16[4,4,512,128]{3,2,1,0:T(8,128)(2,1)S(1)} %pad_maximum_fusion.rest_0_), channel_id=1, source_target_pairs={{0,2},{2,16},{16,18},{18,0},{1,3},{3,17},{17,19},{19,1},{4,6},{6,2... | collective-permute-start | bytes 6291464 | tf_op jit(solution)/shard_map/ppermute | solution.py:33
  72.9 45.8 %collective-permute-start.9 = (bf16[4,4,512,128]{3,2,1,0:T(8,128)(2,1)S(1)}, bf16[4,4,512,128]{3,2,1,0:T(8,128)(2,1)}, u32[]{:S(2)}, u32[]{:S(2)}) collective-permute-start(bf16[4,4,512,128]{3,2,1,0:T(8,128)(2,1)S(1)} %pad_maximum_fusion.rest_0_), channel_id=1, source_target_pairs={{0,18},{2,0},{16,2},{18,16},{1,19},{3,1},{17,3},{19,17},{4,22},{6,... | collective-permute-start | bytes 6291464 | tf_op jit(solution)/shard_map/ppermute | solution.py:33
  91.8 33.6 %copy-start.6 = (s32[8]{0:T(128)S(1)}, s32[8]{0:T(128)}, u32[]{:S(2)}) copy-start(s32[8]{0:T(128)} %lens_ref.5) | copy-start | bytes 100
  118.6 41.4 %collective-permute-start.10 = (bf16[2,4,512,128]{3,2,1,0:T(8,128)(2,1)S(1)}, bf16[2,4,512,128]{3,2,1,0:T(8,128)(2,1)}, u32[]{:S(2)}, u32[]{:S(2)}) collective-permute-start(bf16[2,4,512,128]{3,2,1,0:T(8,128)(2,1)S(1)} %slice.16), channel_id=1, source_target_pairs={{0,2},{2,16},{16,18},{18,0},{1,3},{3,17},{17,19},{19,1},{4,6},{6,2... | collective-permute-start | bytes 3145736 | tf_op jit(solution)/shard_map/ppermute | solution.py:33
  121.0 39.0 %collective-permute-start.11 = (bf16[2,4,512,128]{3,2,1,0:T(8,128)(2,1)}, bf16[2,4,512,128]{3,2,1,0:T(8,128)(2,1)}, u32[]{:S(2)}, u32[]{:S(2)}) collective-permute-start(bf16[2,4,512,128]{3,2,1,0:T(8,128)(2,1)} %slice.17), channel_id=1, source_target_pairs={{0,18},{2,0},{16,2},{18,16},{1,19},{3,1},{17,3},{19,17},{4,22},{6,... | collective-permute-start | bytes 3145736 | tf_op jit(solution)/shard_map/ppermute | solution.py:33
  141.5 18.5 %collective-permute-start.13 = (bf16[512,512]{1,0:T(8,128)(2,1)S(1)}, bf16[512,512]{1,0:T(8,128)(2,1)S(1)}, u32[]{:S(2)}, u32[]{:S(2)}) collective-permute-start(bf16[512,512]{1,0:T(8,128)(2,1)S(1)} %shard_map.133.mine_ref), channel_id=1, source_target_pairs={{0,2},{2,0},{1,3},{3,1},{4,6},{6,4},{5,7},{7,5},{8,10},{10,8},{9,1... | collective-permute-start | bytes 1572872 | tf_op jit(solution)/shard_map/ppermute | solution.py:24
  159.4 13.7 %collective-permute-start.4 = (bf16[512,512]{1,0:T(8,128)(2,1)S(1)}, bf16[512,512]{1,0:T(8,128)(2,1)S(1)}, u32[]{:S(2)}, u32[]{:S(2)}) collective-permute-start(bf16[512,512]{1,0:T(8,128)(2,1)S(1)} %shard_map.131.mine_ref), channel_id=1, source_target_pairs={{0,2},{2,0},{1,3},{3,1},{4,6},{6,4},{5,7},{7,5},{8,10},{10,8},{9,1... | collective-permute-start | bytes 1572872 | tf_op jit(solution)/shard_map/ppermute | solution.py:24
  160.1 25.6 %slice-start = ((s8[8388608]{0:T(1024)(128)(4,1)}), s8[4194304]{0:T(1024)(128)(4,1)S(1)}, s32[]{:S(2)}) async-start(s8[8388608]{0:T(1024)(128)(4,1)} %bitcast.32), calls=%async_computation.3 | async-start | bytes 8388608
  172.8 12.9 %slice-start.1 = ((s8[8388608]{0:T(1024)(128)(4,1)}), s8[4194304]{0:T(1024)(128)(4,1)S(1)}, s32[]{:S(2)}) async-start(s8[8388608]{0:T(1024)(128)(4,1)} %bitcast.32), calls=%async_computation.4 | async-start | bytes 8388608
  172.8 12.9 %copy-start.2 = (f32[4096]{0:T(1024)S(1)}, f32[4096]{0:T(1024)}, u32[]{:S(2)}) copy-start(f32[4096]{0:T(1024)} %param.16) | copy-start | bytes 49156
  172.8 12.9 %collective-permute-start.14 = (bf16[512,4096]{1,0:T(8,128)(2,1)}, bf16[512,4096]{1,0:T(8,128)(2,1)}, u32[]{:S(2)}, u32[]{:S(2)}) collective-permute-start(bf16[512,4096]{1,0:T(8,128)(2,1)} %shard_map.134.mine_ref), channel_id=1, source_target_pairs={{0,1},{1,0},{2,3},{3,2},{4,5},{5,4},{6,7},{7,6},{8,9},{9,8},{10,11... | collective-permute-start | bytes 12582920 | tf_op jit(solution)/shard_map/ppermute | solution.py:24
  185.4 10.2 %collective-permute-start.12 = (bf16[512,4096]{1,0:T(8,128)(2,1)}, bf16[512,4096]{1,0:T(8,128)(2,1)}, u32[]{:S(2)}, u32[]{:S(2)}) collective-permute-start(bf16[512,4096]{1,0:T(8,128)(2,1)} %shard_map.132.mine_ref), channel_id=1, source_target_pairs={{0,1},{1,0},{2,3},{3,2},{4,5},{5,4},{6,7},{7,6},{8,9},{9,8},{10,11... | collective-permute-start | bytes 12582920 | tf_op jit(solution)/shard_map/ppermute | solution.py:24
  185.7 2.2 copy-start
  187.9 7.8 %copy-start.1 = (bf16[512,4096]{1,0:T(8,128)(2,1)S(1)}, bf16[512,4096]{1,0:T(8,128)(2,1)}, u32[]{:S(2)}) copy-start(bf16[512,4096]{1,0:T(8,128)(2,1)} %shard_map.132.mine_ref) | copy-start | bytes 12582916
  193.6 2.0 copy-start.3
  195.7 7.6 %copy-start.5 = (bf16[32,32,512]{2,1,0:T(8,128)(2,1)S(1)}, bf16[32,32,512]{2,1,0:T(8,128)(2,1)}, u32[]{:S(2)}) copy-start(bf16[32,32,512]{2,1,0:T(8,128)(2,1)} %query_ref.1) | copy-start | bytes 3145732
  195.7 7.6 %copy-start.7 = (s32[8]{0:T(128)S(1)}, s32[8]{0:T(128)}, u32[]{:S(2)}) copy-start(s32[8]{0:T(128)} %owner_ref.1) | copy-start | bytes 100
  201.3 2.0 copy-start.4
Sparse Core Ops, SparseCore 0:
  24.3 101.0 all-gather.4
  127.5 70.4 all-gather.6

commit v5 on v4

--- a/solution.py
+++ b/solution.py
@@ -25,7 +25,7 @@
 
 
 RING = (0, 3, 1, 2)
-X_OFFSETS = ((0, 0), (3, 0), (1, 0), (2, 0), (2, 2))
+OFFSETS = ((0, 0), (3, 0), (1, 0), (2, 0), (2, 2))
 
 
 def shift(values, axis, by):
@@ -37,16 +37,10 @@
     return jnp.stack([values, shift(values, axis, 1), shift(values, axis, -1), shift(values, axis, 2)])
 
 
-def x_ring_pieces(values):
-    below, above = shift(values, ("xh", "xl"), 1), shift(values, ("xh", "xl"), -1)
+def ring_pieces(values, axis):
+    below, above = shift(values, axis, 1), shift(values, axis, -1)
     half = values.shape[0] // 2
-    return [
-        values,
-        below,
-        above,
-        shift(below[:half], ("xh", "xl"), 1),
-        shift(above[half:], ("xh", "xl"), -1),
-    ]
+    return [values, below, above, shift(below[:half], axis, 1), shift(above[half:], axis, -1)]
 
 
 def anywhere():
@@ -57,17 +51,16 @@
     return pl.BlockSpec(memory_space=pltpu.SMEM)
 
 
-def load_weights(where_ref, gathered_ref, weight, sem_w):
+def load_weights(which, where_ref, gathered_ref, weight, sem_w):
     xh = where_ref[1]
-    for which in range(weight.shape[0]):
-        for y in range(NY):
-            for j in range(NXH):
-                xh_from = xh if j == 0 else 1 - xh
-                pltpu.make_async_copy(
-                    gathered_ref.at[pl.ds(y * NZ, NZ), j, which],
-                    weight.at[which, pl.ds((y * NXH + xh_from) * NZ, NZ)],
-                    sem_w.at[which],
-                ).start()
+    for y in range(NY):
+        for j in range(NXH):
+            xh_from = xh if j == 0 else 1 - xh
+            pltpu.make_async_copy(
+                gathered_ref.at[pl.ds(y * NZ, NZ), j, which],
+                weight.at[which, pl.ds((y * NXH + xh_from) * NZ, NZ)],
+                sem_w.at[which],
+            ).start()
 
 
 def attend_kernel(half, where_ref, lens_ref, normed_ref, weights_ref, out_ref, rows, weight, qkv, sem_a, sem_w):
@@ -75,11 +68,13 @@
     tokens = rows.shape[0]
     copy_rows = pltpu.make_async_copy(normed_ref.at[pl.ds(half * tokens, tokens)], rows, sem_a)
     copy_rows.start()
-    load_weights(where_ref, weights_ref, weight, sem_w)
+    load_weights(0, where_ref, weights_ref, weight, sem_w)
     copy_rows.wait()
     wide = 512
     for which in range(count):
         pltpu.make_async_copy(weight.at[which], weight.at[which], sem_w.at[which]).wait()
+        if which + 1 < count:
+            load_weights(which + 1, where_ref, weights_ref, weight, sem_w)
 
         def step(i, _, which=which):
             at = pl.multiple_of(i * wide, wide)
@@ -138,39 +133,51 @@
 
 
 def output_kernel(where_ref, mine_ref, other_ref, *rest):
-    pieces, (out_ref, rows, weight, sem_a, sem_w) = rest[: len(X_OFFSETS)], rest[len(X_OFFSETS) :]
+    pieces, (out_ref, rows, weight, result, sem_a, sem_w, sem_o) = rest[: len(OFFSETS)], rest[len(OFFSETS) :]
     tokens, cols = mine_ref.shape
     y, xh, z, xl = (where_ref[i] for i in range(4))
     mine_at = pl.multiple_of(xl * cols, cols)
     other_at = pl.multiple_of((1 - xl) * cols, cols)
     pltpu.make_async_copy(mine_ref, rows.at[:, pl.ds(mine_at, cols)], sem_a).start()
     pltpu.make_async_copy(other_ref, rows.at[:, pl.ds(other_at, cols)], sem_a).start()
-    for piece, (dx, first) in zip(pieces, X_OFFSETS):
-        x_from = lax.rem(xh * NXL + xl + dx, NXH * NXL)
-        row = pl.multiple_of(lax.rem(x_from, NXL) * cols, cols)
-        for i in range(piece.shape[0]):
-            z_from = lax.rem(z + RING[first + i], NZ)
-            for j in range(NY):
-                y_from = lax.rem(y + RING[j], NY)
-                block = (y_from * NXH + x_from // NXL) * NZ + z_from
-                at = pl.multiple_of(block * SEQ, SEQ)
+    part = weight.shape[2]
+
+    def load_quarter(j):
+        for piece, (dx, first) in zip(pieces, OFFSETS):
+            x_from = lax.rem(xh * NXL + xl + dx, NXH * NXL)
+            row = pl.multiple_of(lax.rem(x_from, NXL) * cols, cols)
+            for i in range(piece.shape[0]):
+                z_from = lax.rem(z + RING[first + i], NZ)
+                at = pl.multiple_of(((x_from // NXL) * NZ + z_from) * SEQ, SEQ)
                 pltpu.make_async_copy(
-                    piece.at[i, j], weight.at[pl.ds(row, cols), pl.ds(at, SEQ)], sem_w.at[y_from]
+                    piece.at[i, j], weight.at[j, pl.ds(row, cols), pl.ds(at, SEQ)], sem_w.at[j]
                 ).start()
+
+    def store_quarter(j):
+        y_from = lax.rem(y + RING[j], NY)
+        return pltpu.make_async_copy(
+            result.at[j], out_ref.at[:, pl.ds(pl.multiple_of(y_from * part, part), part)], sem_o.at[j]
+        )
+
+    load_quarter(0)
+    load_quarter(1)
     pltpu.make_async_copy(rows, rows, sem_a).wait()
-    part = weight.shape[1] // NY
     wide = 512
-    for q in range(NY):
-        quarter = weight.at[:, pl.ds(q * part, part)]
-        pltpu.make_async_copy(quarter, quarter, sem_w.at[q]).wait()
-
-        def step(i, _, q=q):
-            at = pl.multiple_of(q * part + i * wide, wide)
-            acc = jnp.dot(rows[...], weight[:, pl.ds(at, wide)], preferred_element_type=jnp.float32)
-            out_ref[:, pl.ds(at, wide)] = acc.astype(jnp.bfloat16)
+    for j in range(NY):
+        pltpu.make_async_copy(weight.at[j], weight.at[j], sem_w.at[j]).wait()
+        if j + 2 < NY:
+            load_quarter(j + 2)
+
+        def step(i, _, j=j):
+            at = pl.multiple_of(i * wide, wide)
+            acc = jnp.dot(rows[...], weight[j, :, pl.ds(at, wide)], preferred_element_type=jnp.float32)
+            result[j, :, pl.ds(at, wide)] = acc.astype(jnp.bfloat16)
             return 0
 
         lax.fori_loop(0, part // wide, step, 0)
+        store_quarter(j).start()
+    for j in range(NY):
+        store_quarter(j).wait()
 
 
 def output(where, mine, other, pieces, width):
@@ -179,11 +186,13 @@
         output_kernel,
         out_shape=jax.ShapeDtypeStruct((tokens, width), jnp.bfloat16),
         in_specs=[in_smem()] + [anywhere()] * (2 + len(pieces)),
-        out_specs=pl.BlockSpec(memory_space=pltpu.VMEM),
+        out_specs=anywhere(),
         scratch_shapes=[
             pltpu.VMEM((tokens, 2 * cols), jnp.bfloat16),
-            pltpu.VMEM((2 * cols, width), jnp.bfloat16),
+            pltpu.VMEM((NY, 2 * cols, width // NY), jnp.bfloat16),
+            pltpu.VMEM((NY, tokens, width // NY), jnp.bfloat16),
             pltpu.SemaphoreType.DMA,
+            pltpu.SemaphoreType.DMA((NY,)),
             pltpu.SemaphoreType.DMA((NY,)),
         ],
         compiler_params=pltpu.CompilerParams(vmem_limit_bytes=VMEM),
@@ -238,21 +247,24 @@
     weights_ref, sent_ref, final, weight, kv, numer, sem_a, sem_w = rest
     count, blocks, _, cols = weight.shape
     tokens = final.shape[1]
-    for half in range(HALVES):
-        pltpu.make_async_copy(finals[half], final.at[half], sem_a.at[half]).start()
-    load_weights(where_ref, weights_ref, weight, sem_w)
+    pltpu.make_async_copy(finals[0], final.at[0], sem_a.at[0]).start()
+    load_weights(0, where_ref, weights_ref, weight, sem_w)
     numer[...] = jnp.zeros_like(numer)
 
     lane = lax.broadcasted_iota(jnp.int32, (1, PAIR), 1)
     low = (lane < HD).astype(jnp.bfloat16)
     high = (lane >= HD).astype(jnp.bfloat16)
     dec_len = query_ref.shape[1]
-    wide = 256
+    wide = 512
     for half in range(HALVES):
         pltpu.make_async_copy(final.at[half], final.at[half], sem_a.at[half]).wait()
         for which in range(count):
             if half == 0:
                 pltpu.make_async_copy(weight.at[which], weight.at[which], sem_w.at[which]).wait()
+                if which == 0:
+                    load_weights(1, where_ref, weights_ref, weight, sem_w)
+                else:
+                    pltpu.make_async_copy(finals[1], final.at[1], sem_a.at[1]).start()
 
             def column(i, _, which=which, half=half):
                 at = pl.multiple_of(i * wide, wide)
@@ -285,10 +297,14 @@
                 both = jnp.dot(coarse, v, preferred_element_type=jnp.float32) + jnp.dot(
                     fine, v, preferred_element_type=jnp.float32
                 )
-                numer[question, :, here] += jnp.where(lane < HD, both[:dec_len], both[dec_len:])
+                rows = slice(hp * dec_len, (hp + 1) * dec_len)
+                numer[question, rows, :] += jnp.where(lane < HD, both[:dec_len], both[dec_len:])
                 totals = jnp.where(lane == 2 * hp, total[:dec_len], totals)
                 totals = jnp.where(lane == 2 * hp + 1, total[dec_len:], totals)
-            numer[question, :, cols : cols + PAIR] += totals
+            packed = totals[:8]
+            for group in range(1, dec_len // 8):
+                packed += pltpu.roll(totals[8 * group : 8 * (group + 1)], 8 * group, 1)
+            numer[question, cols // PAIR * dec_len : cols // PAIR * dec_len + 8, :] += packed
             return 0
 
         lax.fori_loop(0, tokens // SEQ, one, 0)
@@ -298,7 +314,7 @@
 def decode(where, lengths, owner, query, finals, gathered):
     tokens, width = finals[0].shape
     questions, dec_len, cols = query.shape
-    shape = (questions, dec_len, cols + PAIR)
+    shape = (questions, cols // PAIR * dec_len + 16, PAIR)
     return pl.pallas_call(
         decode_kernel,
         out_shape=jax.ShapeDtypeStruct(shape, jnp.bfloat16),
@@ -353,10 +369,11 @@
     wo = ring_gather(enc_wo, "y")
     enc, enc_other, wo = lax.optimization_barrier((enc, enc_other, wo))
     qkv = gather_rows(enc, enc_other)
-    wo = ring_gather(wo, "z")
+    *wo, low, high = ring_pieces(wo, "z")
+    wo = jnp.stack([*wo, jnp.concatenate([low, high])])
     dec, wo = lax.optimization_barrier((jnp.stack([dec_wk, dec_wv]), wo))
     dkv = gather_rows(dec, swap(dec, "xh"))
-    wo = x_ring_pieces(wo)
+    wo = ring_pieces(wo, ("xh", "xl"))
     where = jnp.stack([lax.axis_index(axis) for axis in AXES]).astype(jnp.int32)
     mine = [attend(half, where, lengths, normed, qkv) for half in range(HALVES)]
     theirs = [swap(part, "xl") for part in mine]
@@ -370,8 +387,10 @@
     sent = decode(where, lengths, owner, dec_query, finals, dkv)
     came = lax.all_to_all(sent, DP, 0, 0, tiled=True).astype(jnp.float32)
     came = jnp.sum(came, axis=0)
-    own_numer = came[:, :local_cols].reshape(dec_len, local_heads, HD)
-    own_total = came[:, local_cols : local_cols + local_heads].reshape(dec_len, local_heads, 1)
+    pairs = local_heads // 2
+    own_numer = came[: pairs * dec_len].reshape(pairs, dec_len, 2, HD).transpose(1, 0, 2, 3)
+    own_total = came[pairs * dec_len : pairs * dec_len + 8, : dec_len // 8 * local_heads]
+    own_total = own_total.reshape(8, dec_len // 8, local_heads).transpose(1, 0, 2).reshape(dec_len, pairs, 2, 1)
     context = (own_numer / own_total).astype(jnp.bfloat16).reshape(1, dec_len, local_cols)
     return (encoded.reshape(pass_count, seq_len, width), context)
 

time: 262 us -> 248 us (0.947)
  Pallas kernels: 88.4 us -> 75.5 us
    pallas_call x2, Pallas kernels: 25 us -> 18.6 us  [output(): pl.pallas_call(output_kernel, out_shape=jax.ShapeDtypeStruct((tokens, wid...]
    ppermute x10 -> x11, waiting for transfers between devices: 63.8 us -> 57.6 us  [shift(): lax.ppermute(values, axis, [(i, (i + by) % size) for i in range(size)])]
    pallas_call x2, Pallas kernels: 32.4 us -> 27.7 us  [attend(): pl.pallas_call(functools.partial(attend_kernel, half), out_shape=jax.Shap...]
    ppermute x6, waiting for transfers between devices: 6.98 us -> 11.3 us  [swap(): return lax.ppermute(values, axis, [(0, 1), (1, 0)])]
    ppermute x10 -> x11, starting transfers between devices: 17.7 us -> 19.7 us  [shift(): lax.ppermute(values, axis, [(i, (i + by) % size) for i in range(size)])]
  transfers between devices with their start and end apart: 18 -> 19, of which waited for: 8 -> 10; matrix products, arithmetic and copies ran while one was open for 8% -> 9% of each run, Pallas kernels for 26% -> 23%
where the time goes in v5:
time: 248 us; the launch traced here: 247 us
  Pallas kernels  75.5 us (30%)
  waiting for transfers between devices  71.6 us (29%)
  blocking collectives  28.7 us (12%)
  starting transfers between devices  25.6 us (10%)
  other arithmetic  20.3 us (8%)
  between operations  14.4 us (6%)
  local copies, waits for them, and re-layouts  11.1 us (4%)
    ppermute x11, waiting for transfers between devices, shift(): lax.ppermute(values, axis, [(i, (i + by) % size) for i in range(size)])  57.6 us
    all_to_all x1, blocking collectives, shards(): came = lax.all_to_all(sent, DP, 0, 0, tiled=True).astype(jnp.float32)  28.7 us
    pallas_call x2, Pallas kernels, attend(): pl.pallas_call(functools.partial(attend_kernel, half), out_shape=jax.Shap...  27.7 us
    ppermute x11, starting transfers between devices, shift(): lax.ppermute(values, axis, [(i, (i + by) % size) for i in range(size)])  19.7 us
    pallas_call x2, Pallas kernels, output(): pl.pallas_call(output_kernel, out_shape=jax.ShapeDtypeStruct((tokens, wid...  18.6 us
    pallas_call x1, Pallas kernels, decode(): pl.pallas_call(decode_kernel, out_shape=jax.ShapeDtypeStruct(shape, jnp.b...  17.5 us
    pallas_call x2, Pallas kernels, encode(): pl.pallas_call(encode_kernel, grid=(steps,), out_shape=(jax.ShapeDtypeStr...  11.6 us
    ppermute x6, waiting for transfers between devices, swap(): return lax.ppermute(values, axis, [(0, 1), (1, 0)])  11.3 us
  transfers between devices with their start and end apart: 19, of which 10 were waited for; matrix products, arithmetic and copies ran while one was open for 9% of the time, Pallas kernels for 23%

profile of v5, /device:TPU:0, one launch (start us, length us, event | category | flops | bytes accessed | tf_op | source)
XLA Modules:
  0.0 247.2 jit_solution(11899617001882908904)
XLA Ops:
  7.2 1.1 pad_maximum_fusion.4
  8.4 3.2 %collective-permute-start = (bf16[3,128,512]{2,1,0:T(8,128)(2,1)S(1)}, bf16[3,128,512]{2,1,0:T(8,128)(2,1)S(1)}, u32[]{:S(2)}, u32[]{:S(2)}) collective-permute-start(bf16[3,128,512]{2,1,0:T(8,128)(2,1)S(1)} %pad_maximum_fusion.4), channel_id=1, source_target_pairs={{0,16},{16,0},{1,17},{17,1},{2,18},{18,2},{3,19},{19,3},{4,20},{20... | collective-permute-start | bytes 1179656 | tf_op jit(solution)/shard_map/ppermute | solution.py:24
  11.6 3.2 %collective-permute-start.3 = (bf16[512,128]{1,0:T(8,128)(2,1)}, bf16[512,128]{1,0:T(8,128)(2,1)S(1)}, u32[]{:S(2)}, u32[]{:S(2)}) collective-permute-start(bf16[512,128]{1,0:T(8,128)(2,1)} %param.20), channel_id=1, source_target_pairs={{0,64},{32,96},{64,0},{96,32},{1,65},{33,97},{65,1},{97,33},{2,66}... | collective-permute-start | bytes 393224 | tf_op jit(solution)/shard_map/ppermute | solution.py:33
  14.8 1.1 collective-permute-start.2
  16.8 2.2 collective-permute-done.3
  18.9 2.4 collective-permute-done.2
  24.2 4.1 %collective-permute-start.6 = (bf16[4,512,128]{2,1,0:T(8,128)(2,1)S(1)}, bf16[4,512,128]{2,1,0:T(8,128)(2,1)S(1)}, u32[]{:S(2)}, u32[]{:S(2)}) collective-permute-start(bf16[4,512,128]{2,1,0:T(8,128)(2,1)S(1)} %pad_maximum_fusion.2), channel_id=1, source_target_pairs={{0,12},{4,0},{8,4},{12,8},{1,13},{5,1},{9,5},{13,9},{2,14},{6,2},{... | collective-permute-start | bytes 1572872 | tf_op jit(solution)/shard_map/ppermute | solution.py:33
  28.3 14.6 %collective-permute-done.6 = bf16[4,512,128]{2,1,0:T(8,128)(2,1)S(1)} collective-permute-done((bf16[4,512,128]{2,1,0:T(8,128)(2,1)S(1)}, bf16[4,512,128]{2,1,0:T(8,128)(2,1)S(1)}, u32[]{:S(2)}, u32[]{:S(2)}) %collective-permute-start.6) | collective-permute-done | bytes 524320 | tf_op jit(solution)/shard_map/ppermute | solution.py:33
  43.0 3.8 %collective-permute-start.8 = (bf16[2,512,128]{2,1,0:T(8,128)(2,1)S(1)}, bf16[2,512,128]{2,1,0:T(8,128)(2,1)S(1)}, u32[]{:S(2)}, u32[]{:S(2)}) collective-permute-start(bf16[2,512,128]{2,1,0:T(8,128)(2,1)S(1)} %slice.25), channel_id=1, source_target_pairs={{0,12},{4,0},{8,4},{12,8},{1,13},{5,1},{9,5},{13,9},{2,14},{6,2},{... | collective-permute-start | bytes 786440 | tf_op jit(solution)/shard_map/ppermute | solution.py:33
  46.9 9.2 %collective-permute-done.8 = bf16[2,512,128]{2,1,0:T(8,128)(2,1)S(1)} collective-permute-done((bf16[2,512,128]{2,1,0:T(8,128)(2,1)S(1)}, bf16[2,512,128]{2,1,0:T(8,128)(2,1)S(1)}, u32[]{:S(2)}, u32[]{:S(2)}) %collective-permute-start.8) | collective-permute-done | bytes 262176 | tf_op jit(solution)/shard_map/ppermute | solution.py:33
  56.1 3.4 %collective-permute-done.7 = bf16[2,512,128]{2,1,0:T(8,128)(2,1)S(1)} collective-permute-done((bf16[2,512,128]{2,1,0:T(8,128)(2,1)S(1)}, bf16[2,512,128]{2,1,0:T(8,128)(2,1)S(1)}, u32[]{:S(2)}, u32[]{:S(2)}) %collective-permute-start.7) | collective-permute-done | bytes 262176 | tf_op jit(solution)/shard_map/ppermute | solution.py:33
  60.0 10.7 %collective-permute-done.16 = bf16[2,128,512]{2,1,0:T(8,128)(2,1)S(1)} collective-permute-done((bf16[2,128,512]{2,1,0:T(8,128)(2,1)S(1)}, bf16[2,128,512]{2,1,0:T(8,128)(2,1)S(1)}, u32[]{:S(2)}, u32[]{:S(2)}) %collective-permute-start.16) | collective-permute-done | bytes 262176 | tf_op jit(solution)/shard_map/ppermute | solution.py:24
  71.6 3.2 %collective-permute-start.10 = (bf16[4,4,512,128]{3,2,1,0:T(8,128)(2,1)S(1)}, bf16[4,4,512,128]{3,2,1,0:T(8,128)(2,1)}, u32[]{:S(2)}, u32[]{:S(2)}) collective-permute-start(bf16[4,4,512,128]{3,2,1,0:T(8,128)(2,1)S(1)} %pad_maximum_fusion.rest_0_), channel_id=1, source_target_pairs={{0,18},{2,0},{16,2},{18,16},{1,19},{3,1},{17,3},{19,17},{4,22},{6,... | collective-permute-start | bytes 6291464 | tf_op jit(solution)/shard_map/ppermute | solution.py:33
  74.8 5.2 %multiply_reduce_fusion = f32[8,128]{1,0:T(8,128)S(1)} fusion(bf16[8,128,4096]{2,1,0:T(8,128)(2,1)} %param.12), kind=kLoop, calls=%fused_computation.1 | loop fusion | flops 12581888 | bytes 8392704 | tf_op jit(solution)/shard_map/reduce_sum | solution.py:364
  80.1 10.6 %multiply_convert_fusion.normed_ref = bf16[1024,4096]{1,0:T(8,128)(2,1)} fusion(f32[4096]{0:T(1024)S(1)} %copy-done.11, f32[1024]{0:T(1024)S(1)} %rsqrt_bitcast_fusion, bf16[8,128,4096]{2,1,0:T(8,128)(2,1)} %param.12), kind=kLoop, calls=%fused_computation | loop fusion | flops 16777216 | bytes 16797696 | tf_op jit(solution)/shard_map/convert_element_type | solution.py:365
  90.6 24.9 %collective-permute-done.9.rest_1_ = bf16[4,4,512,128]{3,2,1,0:T(8,128)(2,1)} collective-permute-done((bf16[4,4,512,128]{3,2,1,0:T(8,128)(2,1)S(1)}, bf16[4,4,512,128]{3,2,1,0:T(8,128)(2,1)}, u32[]{:S(2)}, u32[]{:S(2)}) %collective-permute-start.9) | collective-permute-done | bytes 2097184 | tf_op jit(solution)/shard_map/ppermute | solution.py:33
  115.6 1.3 slice.26
  117.0 2.3 slice.27
  119.3 3.2 %collective-permute-start.12 = (bf16[2,4,512,128]{3,2,1,0:T(8,128)(2,1)}, bf16[2,4,512,128]{3,2,1,0:T(8,128)(2,1)}, u32[]{:S(2)}, u32[]{:S(2)}) collective-permute-start(bf16[2,4,512,128]{3,2,1,0:T(8,128)(2,1)} %slice.27), channel_id=1, source_target_pairs={{0,18},{2,0},{16,2},{18,16},{1,19},{3,1},{17,3},{19,17},{4,22},{6,... | collective-permute-start | bytes 3145736 | tf_op jit(solution)/shard_map/ppermute | solution.py:33
  122.5 13.8 %shard_map.133.mine_ref = bf16[512,512]{1,0:T(8,128)(2,1)S(1)} custom-call(s32[5]{0:T(128)S(1)} %stack.92.where_ref, s32[8]{0:T(128)S(1)} %copy-done.6, bf16[1024,4096]{1,0:T(8,128)(2,1)} %multiply_convert_fusion.normed_ref, bf16[16,2,3,128,512]{4,3,2,1,0:T(8,128)(2,1)} %bitcast.62), custom_call_target="tpu_custom_call" | custom-call | flops 6442450944 | bytes 18874368 | tf_op jit(solution)/shard_map/pallas_call | solution.py:118
  136.3 13.9 %shard_map.131.mine_ref = bf16[512,512]{1,0:T(8,128)(2,1)S(1)} custom-call(s32[5]{0:T(128)S(1)} %stack.92.where_ref, s32[8]{0:T(128)S(1)} %copy-done.6, bf16[1024,4096]{1,0:T(8,128)(2,1)} %multiply_convert_fusion.normed_ref, bf16[16,2,3,128,512]{4,3,2,1,0:T(8,128)(2,1)} %bitcast.63), custom_call_target="tpu_custom_call" | custom-call | flops 6442450944 | bytes 18874368 | tf_op jit(solution)/shard_map/pallas_call | solution.py:118
  150.2 2.1 collective-permute-start.4
  152.4 9.5 %shard_map.134.mine_ref = bf16[512,4096]{1,0:T(8,128)(2,1)} custom-call(s32[5]{0:T(128)S(1)} %stack.92.where_ref, bf16[512,512]{1,0:T(8,128)(2,1)S(1)} %shard_map.133.mine_ref, bf16[512,512]{1,0:T(8,128)(2,1)S(1)} %collective-permute-done.14.other_ref, bf16[4,4,512,128]{3,2,1,0:T(8,128)(2,1)} %copy-done.8, ...), custom_call_target="tpu_custom_call" | custom-call | flops 4294967296 | bytes 13631488 | tf_op jit(solution)/shard_map/pallas_call | solution.py:185
  162.5 9.2 %shard_map.132.mine_ref = bf16[512,4096]{1,0:T(8,128)(2,1)} custom-call(s32[5]{0:T(128)S(1)} %stack.92.where_ref, bf16[512,512]{1,0:T(8,128)(2,1)S(1)} %shard_map.131.mine_ref, bf16[512,512]{1,0:T(8,128)(2,1)S(1)} %collective-permute-done.4.other_ref, bf16[4,4,512,128]{3,2,1,0:T(8,128)(2,1)} %copy-done.8, ...), custom_call_target="tpu_custom_call" | custom-call | flops 4294967296 | bytes 13631488 | tf_op jit(solution)/shard_map/pallas_call | solution.py:185
  172.1 2.2 copy-done
  174.3 5.9 %shard_map.135 = (bf16[1024,4096]{1,0:T(8,128)(2,1)}, bf16[512,4096]{1,0:T(8,128)(2,1)S(1)}) custom-call(f32[1,4096]{1,0:T(1,128)S(1)} %bitcast.42, bf16[1024,4096]{1,0:T(8,128)(2,1)S(1)} %bitcast.40, bf16[512,4096]{1,0:T(8,128)(2,1)S(1)} %copy-done, bf16[512,4096]{1,0:T(8,128)(2,1)} %collective-permute-done.15.other_ref), custom_call_target="tpu_custom_call" | custom-call | flops 16777216 | bytes 20971520 | tf_op jit(solution)/shard_map/pallas_call | solution.py:230
  180.3 2.0 copy-done.3
  182.3 5.7 %shard_map.136 = (bf16[1024,4096]{1,0:T(8,128)(2,1)}, bf16[512,4096]{1,0:T(8,128)(2,1)S(1)}) custom-call(f32[1,4096]{1,0:T(1,128)S(1)} %bitcast.43, bf16[1024,4096]{1,0:T(8,128)(2,1)S(1)} %bitcast.41, bf16[512,4096]{1,0:T(8,128)(2,1)S(1)} %copy-done.1, bf16[512,4096]{1,0:T(8,128)(2,1)} %collective-permute-done.13.other_ref, ...), custom_call_target="tpu_custom_call", output_to_operand_aliasing={{0}: (4, {})} | custom-call | flops 16777216 | bytes 20971520 | tf_op jit(solution)/shard_map/pallas_call | solution.py:230
  188.0 2.0 copy-done.4
  190.0 2.6 %all-gather.7.cloned.1.call-done = bf16[32,2,128,512]{3,2,1,0:T(8,128)(2,1)} async-done(((bf16[2,2,128,512]{3,2,1,0:T(8,128)(2,1)}), bf16[32,2,128,512]{3,2,1,0:T(8,128)(2,1)}) %all-gather.7.cloned.1.call-update) | async-done | bytes 8388624 | tf_op jit(solution)/shard_map/all_gather | solution.py:340
  192.6 17.5 %shard_map.137 = bf16[32,144,128]{2,1,0:T(8,128)(2,1)} custom-call(s32[5]{0:T(128)S(1)} %stack.92.where_ref, s32[8]{0:T(128)S(1)} %copy-done.6, s32[8]{0:T(128)S(1)} %copy-done.7, bf16[32,32,512]{2,1,0:T(8,128)(2,1)S(1)} %copy-done.5, bf16[512,4096]{1,0:T(8,128)(2,1)} %copy-done.3, bf16[512,4096]{1,0:T(8,128)(2,1)} %copy-done.4, ...), custom_call_target="tpu_custom_call" | custom-call | flops 8589934592 | bytes 18874368 | tf_op jit(solution)/shard_map/pallas_call | solution.py:318
  210.1 28.7 %all_to_all.5 = bf16[32,144,128]{2,1,0:T(8,128)(2,1)S(1)} all-to-all(bf16[32,144,128]{2,1,0:T(8,128)(2,1)} %shard_map.137), channel_id=1, replica_groups=mesh['y'=4,'xh'=2,'z'=4,'xl'=2,'c'=2] {'y','xh','z'}, dimensions={0} | all-to-all | bytes 2359296 | tf_op jit(solution)/shard_map/all_to_all | solution.py:388
  (70 shorter events, 8.0 us)
Async XLA Ops:
  7.2 39.7 %copy-start.9 = (bf16[128,512]{1,0:T(8,128)(2,1)S(1)}, bf16[128,512]{1,0:T(8,128)(2,1)}, u32[]{:S(2)}) copy-start(bf16[128,512]{1,0:T(8,128)(2,1)} %param.22) | copy-start | bytes 393220
  7.2 39.7 %copy-start.10 = (bf16[128,512]{1,0:T(8,128)(2,1)S(1)}, bf16[128,512]{1,0:T(8,128)(2,1)}, u32[]{:S(2)}) copy-start(bf16[128,512]{1,0:T(8,128)(2,1)} %param.21) | copy-start | bytes 393220
  7.2 115.3 %all-gather.5.cloned.1.call-start = ((), (), s32[]{:S(2)}) async-start(), calls=%async_computation.1 | async-start | bytes 13369344 | tf_op jit(solution)/shard_map/all_gather | solution.py:340
  8.4 14.8 %collective-permute-start = (bf16[3,128,512]{2,1,0:T(8,128)(2,1)S(1)}, bf16[3,128,512]{2,1,0:T(8,128)(2,1)S(1)}, u32[]{:S(2)}, u32[]{:S(2)}) collective-permute-start(bf16[3,128,512]{2,1,0:T(8,128)(2,1)S(1)} %pad_maximum_fusion.4), channel_id=1, source_target_pairs={{0,16},{16,0},{1,17},{17,1},{2,18},{18,2},{3,19},{19,3},{4,20},{20... | collective-permute-start | bytes 1179656 | tf_op jit(solution)/shard_map/ppermute | solution.py:24
  11.6 7.4 %collective-permute-start.3 = (bf16[512,128]{1,0:T(8,128)(2,1)}, bf16[512,128]{1,0:T(8,128)(2,1)S(1)}, u32[]{:S(2)}, u32[]{:S(2)}) collective-permute-start(bf16[512,128]{1,0:T(8,128)(2,1)} %param.20), channel_id=1, source_target_pairs={{0,64},{32,96},{64,0},{96,32},{1,65},{33,97},{65,1},{97,33},{2,66}... | collective-permute-start | bytes 393224 | tf_op jit(solution)/shard_map/ppermute | solution.py:33
  14.8 6.6 %collective-permute-start.2 = (bf16[512,128]{1,0:T(8,128)(2,1)}, bf16[512,128]{1,0:T(8,128)(2,1)S(1)}, u32[]{:S(2)}, u32[]{:S(2)}) collective-permute-start(bf16[512,128]{1,0:T(8,128)(2,1)} %param.20), channel_id=1, source_target_pairs={{0,96},{32,0},{64,32},{96,64},{1,97},{33,1},{65,33},{97,65},{2,98}... | collective-permute-start | bytes 393224 | tf_op jit(solution)/shard_map/ppermute | solution.py:33
  15.8 6.4 %collective-permute-start.1 = (bf16[512,128]{1,0:T(8,128)(2,1)}, bf16[512,128]{1,0:T(8,128)(2,1)S(1)}, u32[]{:S(2)}, u32[]{:S(2)}) collective-permute-start(bf16[512,128]{1,0:T(8,128)(2,1)} %param.20), channel_id=1, source_target_pairs={{0,32},{32,64},{64,96},{96,0},{1,33},{33,65},{65,97},{97,1},{2,34}... | collective-permute-start | bytes 393224 | tf_op jit(solution)/shard_map/ppermute | solution.py:33
  24.2 168.4 %all-gather.7.cloned.1.call-start = ((), (), s32[]{:S(2)}) async-start(), calls=%async_computation.2 | async-start | bytes 8912896 | tf_op jit(solution)/shard_map/all_gather | solution.py:340
  24.2 18.7 %collective-permute-start.6 = (bf16[4,512,128]{2,1,0:T(8,128)(2,1)S(1)}, bf16[4,512,128]{2,1,0:T(8,128)(2,1)S(1)}, u32[]{:S(2)}, u32[]{:S(2)}) collective-permute-start(bf16[4,512,128]{2,1,0:T(8,128)(2,1)S(1)} %pad_maximum_fusion.2), channel_id=1, source_target_pairs={{0,12},{4,0},{8,4},{12,8},{1,13},{5,1},{9,5},{13,9},{2,14},{6,2},{... | collective-permute-start | bytes 1572872 | tf_op jit(solution)/shard_map/ppermute | solution.py:33
  28.3 18.4 %collective-permute-start.5 = (bf16[4,512,128]{2,1,0:T(8,128)(2,1)S(1)}, bf16[4,512,128]{2,1,0:T(8,128)(2,1)S(1)}, u32[]{:S(2)}, u32[]{:S(2)}) collective-permute-start(bf16[4,512,128]{2,1,0:T(8,128)(2,1)S(1)} %pad_maximum_fusion.2), channel_id=1, source_target_pairs={{0,4},{4,8},{8,12},{12,0},{1,5},{5,9},{9,13},{13,1},{2,6},{6,10},{... | collective-permute-start | bytes 1572872 | tf_op jit(solution)/shard_map/ppermute | solution.py:33
  43.0 13.2 %collective-permute-start.8 = (bf16[2,512,128]{2,1,0:T(8,128)(2,1)S(1)}, bf16[2,512,128]{2,1,0:T(8,128)(2,1)S(1)}, u32[]{:S(2)}, u32[]{:S(2)}) collective-permute-start(bf16[2,512,128]{2,1,0:T(8,128)(2,1)S(1)} %slice.25), channel_id=1, source_target_pairs={{0,12},{4,0},{8,4},{12,8},{1,13},{5,1},{9,5},{13,9},{2,14},{6,2},{... | collective-permute-start | bytes 786440 | tf_op jit(solution)/shard_map/ppermute | solution.py:33
  46.7 12.8 %collective-permute-start.7 = (bf16[2,512,128]{2,1,0:T(8,128)(2,1)S(1)}, bf16[2,512,128]{2,1,0:T(8,128)(2,1)S(1)}, u32[]{:S(2)}, u32[]{:S(2)}) collective-permute-start(bf16[2,512,128]{2,1,0:T(8,128)(2,1)S(1)} %slice.24), channel_id=1, source_target_pairs={{0,4},{4,8},{8,12},{12,0},{1,5},{5,9},{9,13},{13,1},{2,6},{6,10},{... | collective-permute-start | bytes 786440 | tf_op jit(solution)/shard_map/ppermute | solution.py:33
  59.8 20.2 %copy-start.8 = (bf16[4,4,512,128]{3,2,1,0:T(8,128)(2,1)}, bf16[4,4,512,128]{3,2,1,0:T(8,128)(2,1)S(1)}, u32[]{:S(2)}) copy-start(bf16[4,4,512,128]{3,2,1,0:T(8,128)(2,1)S(1)} %pad_maximum_fusion.rest_0_) | copy-start | bytes 6291460
  59.9 10.8 %collective-permute-start.16 = (bf16[2,128,512]{2,1,0:T(8,128)(2,1)S(1)}, bf16[2,128,512]{2,1,0:T(8,128)(2,1)S(1)}, u32[]{:S(2)}, u32[]{:S(2)}) collective-permute-start(bf16[2,128,512]{2,1,0:T(8,128)(2,1)S(1)} %pad_maximum_fusion.5), channel_id=1, source_target_pairs={{0,16},{16,0},{1,17},{17,1},{2,18},{18,2},{3,19},{19,3},{4,20},{20... | collective-permute-start | bytes 786440 | tf_op jit(solution)/shard_map/ppermute | solution.py:24
  71.6 8.5 %copy-start.11 = (f32[4096]{0:T(1024)S(1)}, f32[4096]{0:T(1024)}, u32[]{:S(2)}) copy-start(f32[4096]{0:T(1024)} %param.15) | copy-start | bytes 49156
  71.6 44.0 %collective-permute-start.9 = (bf16[4,4,512,128]{3,2,1,0:T(8,128)(2,1)S(1)}, bf16[4,4,512,128]{3,2,1,0:T(8,128)(2,1)}, u32[]{:S(2)}, u32[]{:S(2)}) collective-permute-start(bf16[4,4,512,128]{3,2,1,0:T(8,128)(2,1)S(1)} %pad_maximum_fusion.rest_0_), channel_id=1, source_target_pairs={{0,2},{2,16},{16,18},{18,0},{1,3},{3,17},{17,19},{19,1},{4,6},{6,2... | collective-permute-start | bytes 6291464 | tf_op jit(solution)/shard_map/ppermute | solution.py:33
  71.6 45.3 %collective-permute-start.10 = (bf16[4,4,512,128]{3,2,1,0:T(8,128)(2,1)S(1)}, bf16[4,4,512,128]{3,2,1,0:T(8,128)(2,1)}, u32[]{:S(2)}, u32[]{:S(2)}) collective-permute-start(bf16[4,4,512,128]{3,2,1,0:T(8,128)(2,1)S(1)} %pad_maximum_fusion.rest_0_), channel_id=1, source_target_pairs={{0,18},{2,0},{16,2},{18,16},{1,19},{3,1},{17,3},{19,17},{4,22},{6,... | collective-permute-start | bytes 6291464 | tf_op jit(solution)/shard_map/ppermute | solution.py:33
  90.6 31.8 %copy-start.6 = (s32[8]{0:T(128)S(1)}, s32[8]{0:T(128)}, u32[]{:S(2)}) copy-start(s32[8]{0:T(128)} %lens_ref.5) | copy-start | bytes 100
  116.9 35.5 %collective-permute-start.11 = (bf16[2,4,512,128]{3,2,1,0:T(8,128)(2,1)S(1)}, bf16[2,4,512,128]{3,2,1,0:T(8,128)(2,1)}, u32[]{:S(2)}, u32[]{:S(2)}) collective-permute-start(bf16[2,4,512,128]{3,2,1,0:T(8,128)(2,1)S(1)} %slice.26), channel_id=1, source_target_pairs={{0,2},{2,16},{16,18},{18,0},{1,3},{3,17},{17,19},{19,1},{4,6},{6,2... | collective-permute-start | bytes 3145736 | tf_op jit(solution)/shard_map/ppermute | solution.py:33
  119.3 33.1 %collective-permute-start.12 = (bf16[2,4,512,128]{3,2,1,0:T(8,128)(2,1)}, bf16[2,4,512,128]{3,2,1,0:T(8,128)(2,1)}, u32[]{:S(2)}, u32[]{:S(2)}) collective-permute-start(bf16[2,4,512,128]{3,2,1,0:T(8,128)(2,1)} %slice.27), channel_id=1, source_target_pairs={{0,18},{2,0},{16,2},{18,16},{1,19},{3,1},{17,3},{19,17},{4,22},{6,... | collective-permute-start | bytes 3145736 | tf_op jit(solution)/shard_map/ppermute | solution.py:33
  136.2 16.1 %collective-permute-start.14 = (bf16[512,512]{1,0:T(8,128)(2,1)S(1)}, bf16[512,512]{1,0:T(8,128)(2,1)S(1)}, u32[]{:S(2)}, u32[]{:S(2)}) collective-permute-start(bf16[512,512]{1,0:T(8,128)(2,1)S(1)} %shard_map.133.mine_ref), channel_id=1, source_target_pairs={{0,2},{2,0},{1,3},{3,1},{4,6},{6,4},{5,7},{7,5},{8,10},{10,8},{9,1... | collective-permute-start | bytes 1572872 | tf_op jit(solution)/shard_map/ppermute | solution.py:24
  150.2 12.3 %collective-permute-start.4 = (bf16[512,512]{1,0:T(8,128)(2,1)S(1)}, bf16[512,512]{1,0:T(8,128)(2,1)S(1)}, u32[]{:S(2)}, u32[]{:S(2)}) collective-permute-start(bf16[512,512]{1,0:T(8,128)(2,1)S(1)} %shard_map.131.mine_ref), channel_id=1, source_target_pairs={{0,2},{2,0},{1,3},{3,1},{4,6},{6,4},{5,7},{7,5},{8,10},{10,8},{9,1... | collective-permute-start | bytes 1572872 | tf_op jit(solution)/shard_map/ppermute | solution.py:24
  152.3 19.7 %slice-start = ((s8[8388608]{0:T(1024)(128)(4,1)}), s8[4194304]{0:T(1024)(128)(4,1)S(1)}, s32[]{:S(2)}) async-start(s8[8388608]{0:T(1024)(128)(4,1)} %bitcast.38), calls=%async_computation.3 | async-start | bytes 8388608
  161.8 10.3 %slice-start.1 = ((s8[8388608]{0:T(1024)(128)(4,1)}), s8[4194304]{0:T(1024)(128)(4,1)S(1)}, s32[]{:S(2)}) async-start(s8[8388608]{0:T(1024)(128)(4,1)} %bitcast.38), calls=%async_computation.4 | async-start | bytes 8388608
  161.8 10.2 %copy-start.2 = (f32[4096]{0:T(1024)S(1)}, f32[4096]{0:T(1024)}, u32[]{:S(2)}) copy-start(f32[4096]{0:T(1024)} %param.16) | copy-start | bytes 49156
  161.8 10.2 %collective-permute-start.15 = (bf16[512,4096]{1,0:T(8,128)(2,1)}, bf16[512,4096]{1,0:T(8,128)(2,1)}, u32[]{:S(2)}, u32[]{:S(2)}) collective-permute-start(bf16[512,4096]{1,0:T(8,128)(2,1)} %shard_map.134.mine_ref), channel_id=1, source_target_pairs={{0,1},{1,0},{2,3},{3,2},{4,5},{5,4},{6,7},{7,6},{8,9},{9,8},{10,11... | collective-permute-start | bytes 12582920 | tf_op jit(solution)/shard_map/ppermute | solution.py:24
  171.7 10.6 %collective-permute-start.13 = (bf16[512,4096]{1,0:T(8,128)(2,1)}, bf16[512,4096]{1,0:T(8,128)(2,1)}, u32[]{:S(2)}, u32[]{:S(2)}) collective-permute-start(bf16[512,4096]{1,0:T(8,128)(2,1)} %shard_map.132.mine_ref), channel_id=1, source_target_pairs={{0,1},{1,0},{2,3},{3,2},{4,5},{5,4},{6,7},{7,6},{8,9},{9,8},{10,11... | collective-permute-start | bytes 12582920 | tf_op jit(solution)/shard_map/ppermute | solution.py:24
  172.1 2.2 copy-start
  174.3 8.0 %copy-start.1 = (bf16[512,4096]{1,0:T(8,128)(2,1)S(1)}, bf16[512,4096]{1,0:T(8,128)(2,1)}, u32[]{:S(2)}) copy-start(bf16[512,4096]{1,0:T(8,128)(2,1)} %shard_map.132.mine_ref) | copy-start | bytes 12582916
  180.3 2.0 copy-start.3
  182.3 10.3 %copy-start.5 = (bf16[32,32,512]{2,1,0:T(8,128)(2,1)S(1)}, bf16[32,32,512]{2,1,0:T(8,128)(2,1)}, u32[]{:S(2)}) copy-start(bf16[32,32,512]{2,1,0:T(8,128)(2,1)} %query_ref.1) | copy-start | bytes 3145732
  182.3 10.3 %copy-start.7 = (s32[8]{0:T(128)S(1)}, s32[8]{0:T(128)}, u32[]{:S(2)}) copy-start(s32[8]{0:T(128)} %owner_ref.1) | copy-start | bytes 100
  (1 other events, 2.0 us)
Sparse Core Ops, SparseCore 0:
  24.3 95.6 all-gather.4
  122.1 70.4 all-gather.6

commit v6 on v5

--- a/solution.py
+++ b/solution.py
@@ -294,9 +294,8 @@
                 total = jnp.sum(expon, axis=-1, keepdims=True)
                 coarse = expon.astype(jnp.bfloat16)
                 fine = (expon - coarse.astype(jnp.float32)).astype(jnp.bfloat16)
-                both = jnp.dot(coarse, v, preferred_element_type=jnp.float32) + jnp.dot(
-                    fine, v, preferred_element_type=jnp.float32
-                )
+                both = jnp.dot(jnp.concatenate([coarse, fine], axis=0), v, preferred_element_type=jnp.float32)
+                both = both[: 2 * dec_len] + both[2 * dec_len :]
                 rows = slice(hp * dec_len, (hp + 1) * dec_len)
                 numer[question, rows, :] += jnp.where(lane < HD, both[:dec_len], both[dec_len:])
                 totals = jnp.where(lane == 2 * hp, total[:dec_len], totals)

time: 248 us -> 251 us (1.012)
  Pallas kernels: 75.5 us -> 78.5 us
    pallas_call x1, Pallas kernels: 17.5 us -> 20.5 us  [decode(): pl.pallas_call(decode_kernel, out_shape=jax.ShapeDtypeStruct(shape, jnp.b...]
where the time goes in v6:
time: 251 us; the launch traced here: 250 us
  Pallas kernels  78.5 us (31%)
  waiting for transfers between devices  71.6 us (29%)
  blocking collectives  28.7 us (11%)
  starting transfers between devices  25.6 us (10%)
  other arithmetic  20.3 us (8%)
  between operations  14.4 us (6%)
  local copies, waits for them, and re-layouts  11.1 us (4%)
    ppermute x11, waiting for transfers between devices, shift(): lax.ppermute(values, axis, [(i, (i + by) % size) for i in range(size)])  57.6 us
    all_to_all x1, blocking collectives, shards(): came = lax.all_to_all(sent, DP, 0, 0, tiled=True).astype(jnp.float32)  28.7 us
    pallas_call x2, Pallas kernels, attend(): pl.pallas_call(functools.partial(attend_kernel, half), out_shape=jax.Shap...  27.7 us
    pallas_call x1, Pallas kernels, decode(): pl.pallas_call(decode_kernel, out_shape=jax.ShapeDtypeStruct(shape, jnp.b...  20.5 us
    ppermute x11, starting transfers between devices, shift(): lax.ppermute(values, axis, [(i, (i + by) % size) for i in range(size)])  19.7 us
    pallas_call x2, Pallas kernels, output(): pl.pallas_call(output_kernel, out_shape=jax.ShapeDtypeStruct((tokens, wid...  18.6 us
    pallas_call x2, Pallas kernels, encode(): pl.pallas_call(encode_kernel, grid=(steps,), out_shape=(jax.ShapeDtypeStr...  11.6 us
    ppermute x6, waiting for transfers between devices, swap(): return lax.ppermute(values, axis, [(0, 1), (1, 0)])  11.3 us
  transfers between devices with their start and end apart: 19, of which 10 were waited for; matrix products, arithmetic and copies ran while one was open for 9% of the time, Pallas kernels for 23%

profile of v6, /device:TPU:0, one launch (start us, length us, event | category | flops | bytes accessed | tf_op | source)
XLA Modules:
  0.0 250.2 jit_solution(7305046787863008726)
XLA Ops:
  7.2 1.1 pad_maximum_fusion.4
  8.4 3.2 %collective-permute-start = (bf16[3,128,512]{2,1,0:T(8,128)(2,1)S(1)}, bf16[3,128,512]{2,1,0:T(8,128)(2,1)S(1)}, u32[]{:S(2)}, u32[]{:S(2)}) collective-permute-start(bf16[3,128,512]{2,1,0:T(8,128)(2,1)S(1)} %pad_maximum_fusion.4), channel_id=1, source_target_pairs={{0,16},{16,0},{1,17},{17,1},{2,18},{18,2},{3,19},{19,3},{4,20},{20... | collective-permute-start | bytes 1179656 | tf_op jit(solution)/shard_map/ppermute | solution.py:24
  11.6 3.2 %collective-permute-start.3 = (bf16[512,128]{1,0:T(8,128)(2,1)}, bf16[512,128]{1,0:T(8,128)(2,1)S(1)}, u32[]{:S(2)}, u32[]{:S(2)}) collective-permute-start(bf16[512,128]{1,0:T(8,128)(2,1)} %param.20), channel_id=1, source_target_pairs={{0,64},{32,96},{64,0},{96,32},{1,65},{33,97},{65,1},{97,33},{2,66}... | collective-permute-start | bytes 393224 | tf_op jit(solution)/shard_map/ppermute | solution.py:33
  14.8 1.1 collective-permute-start.2
  16.8 2.2 collective-permute-done.3
  18.9 2.4 collective-permute-done.2
  24.2 4.1 %collective-permute-start.6 = (bf16[4,512,128]{2,1,0:T(8,128)(2,1)S(1)}, bf16[4,512,128]{2,1,0:T(8,128)(2,1)S(1)}, u32[]{:S(2)}, u32[]{:S(2)}) collective-permute-start(bf16[4,512,128]{2,1,0:T(8,128)(2,1)S(1)} %pad_maximum_fusion.2), channel_id=1, source_target_pairs={{0,12},{4,0},{8,4},{12,8},{1,13},{5,1},{9,5},{13,9},{2,14},{6,2},{... | collective-permute-start | bytes 1572872 | tf_op jit(solution)/shard_map/ppermute | solution.py:33
  28.3 14.6 %collective-permute-done.6 = bf16[4,512,128]{2,1,0:T(8,128)(2,1)S(1)} collective-permute-done((bf16[4,512,128]{2,1,0:T(8,128)(2,1)S(1)}, bf16[4,512,128]{2,1,0:T(8,128)(2,1)S(1)}, u32[]{:S(2)}, u32[]{:S(2)}) %collective-permute-start.6) | collective-permute-done | bytes 524320 | tf_op jit(solution)/shard_map/ppermute | solution.py:33
  43.0 3.8 %collective-permute-start.8 = (bf16[2,512,128]{2,1,0:T(8,128)(2,1)S(1)}, bf16[2,512,128]{2,1,0:T(8,128)(2,1)S(1)}, u32[]{:S(2)}, u32[]{:S(2)}) collective-permute-start(bf16[2,512,128]{2,1,0:T(8,128)(2,1)S(1)} %slice.25), channel_id=1, source_target_pairs={{0,12},{4,0},{8,4},{12,8},{1,13},{5,1},{9,5},{13,9},{2,14},{6,2},{... | collective-permute-start | bytes 786440 | tf_op jit(solution)/shard_map/ppermute | solution.py:33
  46.9 9.2 %collective-permute-done.8 = bf16[2,512,128]{2,1,0:T(8,128)(2,1)S(1)} collective-permute-done((bf16[2,512,128]{2,1,0:T(8,128)(2,1)S(1)}, bf16[2,512,128]{2,1,0:T(8,128)(2,1)S(1)}, u32[]{:S(2)}, u32[]{:S(2)}) %collective-permute-start.8) | collective-permute-done | bytes 262176 | tf_op jit(solution)/shard_map/ppermute | solution.py:33
  56.1 3.4 %collective-permute-done.7 = bf16[2,512,128]{2,1,0:T(8,128)(2,1)S(1)} collective-permute-done((bf16[2,512,128]{2,1,0:T(8,128)(2,1)S(1)}, bf16[2,512,128]{2,1,0:T(8,128)(2,1)S(1)}, u32[]{:S(2)}, u32[]{:S(2)}) %collective-permute-start.7) | collective-permute-done | bytes 262176 | tf_op jit(solution)/shard_map/ppermute | solution.py:33
  60.0 10.7 %collective-permute-done.16 = bf16[2,128,512]{2,1,0:T(8,128)(2,1)S(1)} collective-permute-done((bf16[2,128,512]{2,1,0:T(8,128)(2,1)S(1)}, bf16[2,128,512]{2,1,0:T(8,128)(2,1)S(1)}, u32[]{:S(2)}, u32[]{:S(2)}) %collective-permute-start.16) | collective-permute-done | bytes 262176 | tf_op jit(solution)/shard_map/ppermute | solution.py:24
  71.6 3.2 %collective-permute-start.10 = (bf16[4,4,512,128]{3,2,1,0:T(8,128)(2,1)S(1)}, bf16[4,4,512,128]{3,2,1,0:T(8,128)(2,1)}, u32[]{:S(2)}, u32[]{:S(2)}) collective-permute-start(bf16[4,4,512,128]{3,2,1,0:T(8,128)(2,1)S(1)} %pad_maximum_fusion.rest_0_), channel_id=1, source_target_pairs={{0,18},{2,0},{16,2},{18,16},{1,19},{3,1},{17,3},{19,17},{4,22},{6,... | collective-permute-start | bytes 6291464 | tf_op jit(solution)/shard_map/ppermute | solution.py:33
  74.8 5.2 %multiply_reduce_fusion = f32[8,128]{1,0:T(8,128)S(1)} fusion(bf16[8,128,4096]{2,1,0:T(8,128)(2,1)} %param.12), kind=kLoop, calls=%fused_computation.1 | loop fusion | flops 12581888 | bytes 8392704 | tf_op jit(solution)/shard_map/reduce_sum | solution.py:363
  80.1 10.6 %multiply_convert_fusion.normed_ref = bf16[1024,4096]{1,0:T(8,128)(2,1)} fusion(f32[4096]{0:T(1024)S(1)} %copy-done.11, f32[1024]{0:T(1024)S(1)} %rsqrt_bitcast_fusion, bf16[8,128,4096]{2,1,0:T(8,128)(2,1)} %param.12), kind=kLoop, calls=%fused_computation | loop fusion | flops 16777216 | bytes 16797696 | tf_op jit(solution)/shard_map/convert_element_type | solution.py:364
  90.6 24.9 %collective-permute-done.9.rest_1_ = bf16[4,4,512,128]{3,2,1,0:T(8,128)(2,1)} collective-permute-done((bf16[4,4,512,128]{3,2,1,0:T(8,128)(2,1)S(1)}, bf16[4,4,512,128]{3,2,1,0:T(8,128)(2,1)}, u32[]{:S(2)}, u32[]{:S(2)}) %collective-permute-start.9) | collective-permute-done | bytes 2097184 | tf_op jit(solution)/shard_map/ppermute | solution.py:33
  115.6 1.3 slice.26
  117.0 2.3 slice.27
  119.3 3.2 %collective-permute-start.12 = (bf16[2,4,512,128]{3,2,1,0:T(8,128)(2,1)}, bf16[2,4,512,128]{3,2,1,0:T(8,128)(2,1)}, u32[]{:S(2)}, u32[]{:S(2)}) collective-permute-start(bf16[2,4,512,128]{3,2,1,0:T(8,128)(2,1)} %slice.27), channel_id=1, source_target_pairs={{0,18},{2,0},{16,2},{18,16},{1,19},{3,1},{17,3},{19,17},{4,22},{6,... | collective-permute-start | bytes 3145736 | tf_op jit(solution)/shard_map/ppermute | solution.py:33
  122.5 13.8 %shard_map.133.mine_ref = bf16[512,512]{1,0:T(8,128)(2,1)S(1)} custom-call(s32[5]{0:T(128)S(1)} %stack.92.where_ref, s32[8]{0:T(128)S(1)} %copy-done.6, bf16[1024,4096]{1,0:T(8,128)(2,1)} %multiply_convert_fusion.normed_ref, bf16[16,2,3,128,512]{4,3,2,1,0:T(8,128)(2,1)} %bitcast.62), custom_call_target="tpu_custom_call" | custom-call | flops 6442450944 | bytes 18874368 | tf_op jit(solution)/shard_map/pallas_call | solution.py:118
  136.3 13.9 %shard_map.131.mine_ref = bf16[512,512]{1,0:T(8,128)(2,1)S(1)} custom-call(s32[5]{0:T(128)S(1)} %stack.92.where_ref, s32[8]{0:T(128)S(1)} %copy-done.6, bf16[1024,4096]{1,0:T(8,128)(2,1)} %multiply_convert_fusion.normed_ref, bf16[16,2,3,128,512]{4,3,2,1,0:T(8,128)(2,1)} %bitcast.63), custom_call_target="tpu_custom_call" | custom-call | flops 6442450944 | bytes 18874368 | tf_op jit(solution)/shard_map/pallas_call | solution.py:118
  150.2 2.1 collective-permute-start.4
  152.4 9.5 %shard_map.134.mine_ref = bf16[512,4096]{1,0:T(8,128)(2,1)} custom-call(s32[5]{0:T(128)S(1)} %stack.92.where_ref, bf16[512,512]{1,0:T(8,128)(2,1)S(1)} %shard_map.133.mine_ref, bf16[512,512]{1,0:T(8,128)(2,1)S(1)} %collective-permute-done.14.other_ref, bf16[4,4,512,128]{3,2,1,0:T(8,128)(2,1)} %copy-done.8, ...), custom_call_target="tpu_custom_call" | custom-call | flops 4294967296 | bytes 13631488 | tf_op jit(solution)/shard_map/pallas_call | solution.py:185
  162.5 9.2 %shard_map.132.mine_ref = bf16[512,4096]{1,0:T(8,128)(2,1)} custom-call(s32[5]{0:T(128)S(1)} %stack.92.where_ref, bf16[512,512]{1,0:T(8,128)(2,1)S(1)} %shard_map.131.mine_ref, bf16[512,512]{1,0:T(8,128)(2,1)S(1)} %collective-permute-done.4.other_ref, bf16[4,4,512,128]{3,2,1,0:T(8,128)(2,1)} %copy-done.8, ...), custom_call_target="tpu_custom_call" | custom-call | flops 4294967296 | bytes 13631488 | tf_op jit(solution)/shard_map/pallas_call | solution.py:185
  172.1 2.2 copy-done
  174.3 5.9 %shard_map.135 = (bf16[1024,4096]{1,0:T(8,128)(2,1)}, bf16[512,4096]{1,0:T(8,128)(2,1)S(1)}) custom-call(f32[1,4096]{1,0:T(1,128)S(1)} %bitcast.42, bf16[1024,4096]{1,0:T(8,128)(2,1)S(1)} %bitcast.40, bf16[512,4096]{1,0:T(8,128)(2,1)S(1)} %copy-done, bf16[512,4096]{1,0:T(8,128)(2,1)} %collective-permute-done.15.other_ref), custom_call_target="tpu_custom_call" | custom-call | flops 16777216 | bytes 20971520 | tf_op jit(solution)/shard_map/pallas_call | solution.py:230
  180.3 2.0 copy-done.3
  182.3 5.7 %shard_map.136 = (bf16[1024,4096]{1,0:T(8,128)(2,1)}, bf16[512,4096]{1,0:T(8,128)(2,1)S(1)}) custom-call(f32[1,4096]{1,0:T(1,128)S(1)} %bitcast.43, bf16[1024,4096]{1,0:T(8,128)(2,1)S(1)} %bitcast.41, bf16[512,4096]{1,0:T(8,128)(2,1)S(1)} %copy-done.1, bf16[512,4096]{1,0:T(8,128)(2,1)} %collective-permute-done.13.other_ref, ...), custom_call_target="tpu_custom_call", output_to_operand_aliasing={{0}: (4, {})} | custom-call | flops 16777216 | bytes 20971520 | tf_op jit(solution)/shard_map/pallas_call | solution.py:230
  188.0 2.0 copy-done.4
  190.0 2.6 %all-gather.7.cloned.1.call-done = bf16[32,2,128,512]{3,2,1,0:T(8,128)(2,1)} async-done(((bf16[2,2,128,512]{3,2,1,0:T(8,128)(2,1)}), bf16[32,2,128,512]{3,2,1,0:T(8,128)(2,1)}) %all-gather.7.cloned.1.call-update) | async-done | bytes 8388624 | tf_op jit(solution)/shard_map/all_gather | solution.py:339
  192.6 20.5 %shard_map.137 = bf16[32,144,128]{2,1,0:T(8,128)(2,1)} custom-call(s32[5]{0:T(128)S(1)} %stack.92.where_ref, s32[8]{0:T(128)S(1)} %copy-done.6, s32[8]{0:T(128)S(1)} %copy-done.7, bf16[32,32,512]{2,1,0:T(8,128)(2,1)S(1)} %copy-done.5, bf16[512,4096]{1,0:T(8,128)(2,1)} %copy-done.3, bf16[512,4096]{1,0:T(8,128)(2,1)} %copy-done.4, ...), custom_call_target="tpu_custom_call" | custom-call | flops 8589934592 | bytes 18874368 | tf_op jit(solution)/shard_map/pallas_call | solution.py:317
  213.1 28.7 %all_to_all.5 = bf16[32,144,128]{2,1,0:T(8,128)(2,1)S(1)} all-to-all(bf16[32,144,128]{2,1,0:T(8,128)(2,1)} %shard_map.137), channel_id=1, replica_groups=mesh['y'=4,'xh'=2,'z'=4,'xl'=2,'c'=2] {'y','xh','z'}, dimensions={0} | all-to-all | bytes 2359296 | tf_op jit(solution)/shard_map/all_to_all | solution.py:387
  (70 shorter events, 8.0 us)
Async XLA Ops:
  7.2 39.7 %copy-start.9 = (bf16[128,512]{1,0:T(8,128)(2,1)S(1)}, bf16[128,512]{1,0:T(8,128)(2,1)}, u32[]{:S(2)}) copy-start(bf16[128,512]{1,0:T(8,128)(2,1)} %param.22) | copy-start | bytes 393220
  7.2 39.7 %copy-start.10 = (bf16[128,512]{1,0:T(8,128)(2,1)S(1)}, bf16[128,512]{1,0:T(8,128)(2,1)}, u32[]{:S(2)}) copy-start(bf16[128,512]{1,0:T(8,128)(2,1)} %param.21) | copy-start | bytes 393220
  7.2 115.3 %all-gather.5.cloned.1.call-start = ((), (), s32[]{:S(2)}) async-start(), calls=%async_computation.1 | async-start | bytes 13369344 | tf_op jit(solution)/shard_map/all_gather | solution.py:339
  8.4 14.8 %collective-permute-start = (bf16[3,128,512]{2,1,0:T(8,128)(2,1)S(1)}, bf16[3,128,512]{2,1,0:T(8,128)(2,1)S(1)}, u32[]{:S(2)}, u32[]{:S(2)}) collective-permute-start(bf16[3,128,512]{2,1,0:T(8,128)(2,1)S(1)} %pad_maximum_fusion.4), channel_id=1, source_target_pairs={{0,16},{16,0},{1,17},{17,1},{2,18},{18,2},{3,19},{19,3},{4,20},{20... | collective-permute-start | bytes 1179656 | tf_op jit(solution)/shard_map/ppermute | solution.py:24
  11.6 7.4 %collective-permute-start.3 = (bf16[512,128]{1,0:T(8,128)(2,1)}, bf16[512,128]{1,0:T(8,128)(2,1)S(1)}, u32[]{:S(2)}, u32[]{:S(2)}) collective-permute-start(bf16[512,128]{1,0:T(8,128)(2,1)} %param.20), channel_id=1, source_target_pairs={{0,64},{32,96},{64,0},{96,32},{1,65},{33,97},{65,1},{97,33},{2,66}... | collective-permute-start | bytes 393224 | tf_op jit(solution)/shard_map/ppermute | solution.py:33
  14.8 6.6 %collective-permute-start.2 = (bf16[512,128]{1,0:T(8,128)(2,1)}, bf16[512,128]{1,0:T(8,128)(2,1)S(1)}, u32[]{:S(2)}, u32[]{:S(2)}) collective-permute-start(bf16[512,128]{1,0:T(8,128)(2,1)} %param.20), channel_id=1, source_target_pairs={{0,96},{32,0},{64,32},{96,64},{1,97},{33,1},{65,33},{97,65},{2,98}... | collective-permute-start | bytes 393224 | tf_op jit(solution)/shard_map/ppermute | solution.py:33
  15.8 6.4 %collective-permute-start.1 = (bf16[512,128]{1,0:T(8,128)(2,1)}, bf16[512,128]{1,0:T(8,128)(2,1)S(1)}, u32[]{:S(2)}, u32[]{:S(2)}) collective-permute-start(bf16[512,128]{1,0:T(8,128)(2,1)} %param.20), channel_id=1, source_target_pairs={{0,32},{32,64},{64,96},{96,0},{1,33},{33,65},{65,97},{97,1},{2,34}... | collective-permute-start | bytes 393224 | tf_op jit(solution)/shard_map/ppermute | solution.py:33
  24.2 168.4 %all-gather.7.cloned.1.call-start = ((), (), s32[]{:S(2)}) async-start(), calls=%async_computation.2 | async-start | bytes 8912896 | tf_op jit(solution)/shard_map/all_gather | solution.py:339
  24.2 18.7 %collective-permute-start.6 = (bf16[4,512,128]{2,1,0:T(8,128)(2,1)S(1)}, bf16[4,512,128]{2,1,0:T(8,128)(2,1)S(1)}, u32[]{:S(2)}, u32[]{:S(2)}) collective-permute-start(bf16[4,512,128]{2,1,0:T(8,128)(2,1)S(1)} %pad_maximum_fusion.2), channel_id=1, source_target_pairs={{0,12},{4,0},{8,4},{12,8},{1,13},{5,1},{9,5},{13,9},{2,14},{6,2},{... | collective-permute-start | bytes 1572872 | tf_op jit(solution)/shard_map/ppermute | solution.py:33
  28.3 18.4 %collective-permute-start.5 = (bf16[4,512,128]{2,1,0:T(8,128)(2,1)S(1)}, bf16[4,512,128]{2,1,0:T(8,128)(2,1)S(1)}, u32[]{:S(2)}, u32[]{:S(2)}) collective-permute-start(bf16[4,512,128]{2,1,0:T(8,128)(2,1)S(1)} %pad_maximum_fusion.2), channel_id=1, source_target_pairs={{0,4},{4,8},{8,12},{12,0},{1,5},{5,9},{9,13},{13,1},{2,6},{6,10},{... | collective-permute-start | bytes 1572872 | tf_op jit(solution)/shard_map/ppermute | solution.py:33
  43.0 13.2 %collective-permute-start.8 = (bf16[2,512,128]{2,1,0:T(8,128)(2,1)S(1)}, bf16[2,512,128]{2,1,0:T(8,128)(2,1)S(1)}, u32[]{:S(2)}, u32[]{:S(2)}) collective-permute-start(bf16[2,512,128]{2,1,0:T(8,128)(2,1)S(1)} %slice.25), channel_id=1, source_target_pairs={{0,12},{4,0},{8,4},{12,8},{1,13},{5,1},{9,5},{13,9},{2,14},{6,2},{... | collective-permute-start | bytes 786440 | tf_op jit(solution)/shard_map/ppermute | solution.py:33
  46.7 12.8 %collective-permute-start.7 = (bf16[2,512,128]{2,1,0:T(8,128)(2,1)S(1)}, bf16[2,512,128]{2,1,0:T(8,128)(2,1)S(1)}, u32[]{:S(2)}, u32[]{:S(2)}) collective-permute-start(bf16[2,512,128]{2,1,0:T(8,128)(2,1)S(1)} %slice.24), channel_id=1, source_target_pairs={{0,4},{4,8},{8,12},{12,0},{1,5},{5,9},{9,13},{13,1},{2,6},{6,10},{... | collective-permute-start | bytes 786440 | tf_op jit(solution)/shard_map/ppermute | solution.py:33
  59.8 20.2 %copy-start.8 = (bf16[4,4,512,128]{3,2,1,0:T(8,128)(2,1)}, bf16[4,4,512,128]{3,2,1,0:T(8,128)(2,1)S(1)}, u32[]{:S(2)}) copy-start(bf16[4,4,512,128]{3,2,1,0:T(8,128)(2,1)S(1)} %pad_maximum_fusion.rest_0_) | copy-start | bytes 6291460
  59.9 10.8 %collective-permute-start.16 = (bf16[2,128,512]{2,1,0:T(8,128)(2,1)S(1)}, bf16[2,128,512]{2,1,0:T(8,128)(2,1)S(1)}, u32[]{:S(2)}, u32[]{:S(2)}) collective-permute-start(bf16[2,128,512]{2,1,0:T(8,128)(2,1)S(1)} %pad_maximum_fusion.5), channel_id=1, source_target_pairs={{0,16},{16,0},{1,17},{17,1},{2,18},{18,2},{3,19},{19,3},{4,20},{20... | collective-permute-start | bytes 786440 | tf_op jit(solution)/shard_map/ppermute | solution.py:24
  71.6 8.5 %copy-start.11 = (f32[4096]{0:T(1024)S(1)}, f32[4096]{0:T(1024)}, u32[]{:S(2)}) copy-start(f32[4096]{0:T(1024)} %param.15) | copy-start | bytes 49156
  71.6 44.0 %collective-permute-start.9 = (bf16[4,4,512,128]{3,2,1,0:T(8,128)(2,1)S(1)}, bf16[4,4,512,128]{3,2,1,0:T(8,128)(2,1)}, u32[]{:S(2)}, u32[]{:S(2)}) collective-permute-start(bf16[4,4,512,128]{3,2,1,0:T(8,128)(2,1)S(1)} %pad_maximum_fusion.rest_0_), channel_id=1, source_target_pairs={{0,2},{2,16},{16,18},{18,0},{1,3},{3,17},{17,19},{19,1},{4,6},{6,2... | collective-permute-start | bytes 6291464 | tf_op jit(solution)/shard_map/ppermute | solution.py:33
  71.6 45.3 %collective-permute-start.10 = (bf16[4,4,512,128]{3,2,1,0:T(8,128)(2,1)S(1)}, bf16[4,4,512,128]{3,2,1,0:T(8,128)(2,1)}, u32[]{:S(2)}, u32[]{:S(2)}) collective-permute-start(bf16[4,4,512,128]{3,2,1,0:T(8,128)(2,1)S(1)} %pad_maximum_fusion.rest_0_), channel_id=1, source_target_pairs={{0,18},{2,0},{16,2},{18,16},{1,19},{3,1},{17,3},{19,17},{4,22},{6,... | collective-permute-start | bytes 6291464 | tf_op jit(solution)/shard_map/ppermute | solution.py:33
  90.6 31.8 %copy-start.6 = (s32[8]{0:T(128)S(1)}, s32[8]{0:T(128)}, u32[]{:S(2)}) copy-start(s32[8]{0:T(128)} %lens_ref.5) | copy-start | bytes 100
  116.9 35.5 %collective-permute-start.11 = (bf16[2,4,512,128]{3,2,1,0:T(8,128)(2,1)S(1)}, bf16[2,4,512,128]{3,2,1,0:T(8,128)(2,1)}, u32[]{:S(2)}, u32[]{:S(2)}) collective-permute-start(bf16[2,4,512,128]{3,2,1,0:T(8,128)(2,1)S(1)} %slice.26), channel_id=1, source_target_pairs={{0,2},{2,16},{16,18},{18,0},{1,3},{3,17},{17,19},{19,1},{4,6},{6,2... | collective-permute-start | bytes 3145736 | tf_op jit(solution)/shard_map/ppermute | solution.py:33
  119.3 33.1 %collective-permute-start.12 = (bf16[2,4,512,128]{3,2,1,0:T(8,128)(2,1)}, bf16[2,4,512,128]{3,2,1,0:T(8,128)(2,1)}, u32[]{:S(2)}, u32[]{:S(2)}) collective-permute-start(bf16[2,4,512,128]{3,2,1,0:T(8,128)(2,1)} %slice.27), channel_id=1, source_target_pairs={{0,18},{2,0},{16,2},{18,16},{1,19},{3,1},{17,3},{19,17},{4,22},{6,... | collective-permute-start | bytes 3145736 | tf_op jit(solution)/shard_map/ppermute | solution.py:33
  136.2 16.1 %collective-permute-start.14 = (bf16[512,512]{1,0:T(8,128)(2,1)S(1)}, bf16[512,512]{1,0:T(8,128)(2,1)S(1)}, u32[]{:S(2)}, u32[]{:S(2)}) collective-permute-start(bf16[512,512]{1,0:T(8,128)(2,1)S(1)} %shard_map.133.mine_ref), channel_id=1, source_target_pairs={{0,2},{2,0},{1,3},{3,1},{4,6},{6,4},{5,7},{7,5},{8,10},{10,8},{9,1... | collective-permute-start | bytes 1572872 | tf_op jit(solution)/shard_map/ppermute | solution.py:24
  150.2 12.3 %collective-permute-start.4 = (bf16[512,512]{1,0:T(8,128)(2,1)S(1)}, bf16[512,512]{1,0:T(8,128)(2,1)S(1)}, u32[]{:S(2)}, u32[]{:S(2)}) collective-permute-start(bf16[512,512]{1,0:T(8,128)(2,1)S(1)} %shard_map.131.mine_ref), channel_id=1, source_target_pairs={{0,2},{2,0},{1,3},{3,1},{4,6},{6,4},{5,7},{7,5},{8,10},{10,8},{9,1... | collective-permute-start | bytes 1572872 | tf_op jit(solution)/shard_map/ppermute | solution.py:24
  152.3 19.7 %slice-start = ((s8[8388608]{0:T(1024)(128)(4,1)}), s8[4194304]{0:T(1024)(128)(4,1)S(1)}, s32[]{:S(2)}) async-start(s8[8388608]{0:T(1024)(128)(4,1)} %bitcast.38), calls=%async_computation.3 | async-start | bytes 8388608
  161.8 10.3 %slice-start.1 = ((s8[8388608]{0:T(1024)(128)(4,1)}), s8[4194304]{0:T(1024)(128)(4,1)S(1)}, s32[]{:S(2)}) async-start(s8[8388608]{0:T(1024)(128)(4,1)} %bitcast.38), calls=%async_computation.4 | async-start | bytes 8388608
  161.8 10.2 %copy-start.2 = (f32[4096]{0:T(1024)S(1)}, f32[4096]{0:T(1024)}, u32[]{:S(2)}) copy-start(f32[4096]{0:T(1024)} %param.16) | copy-start | bytes 49156
  161.8 10.2 %collective-permute-start.15 = (bf16[512,4096]{1,0:T(8,128)(2,1)}, bf16[512,4096]{1,0:T(8,128)(2,1)}, u32[]{:S(2)}, u32[]{:S(2)}) collective-permute-start(bf16[512,4096]{1,0:T(8,128)(2,1)} %shard_map.134.mine_ref), channel_id=1, source_target_pairs={{0,1},{1,0},{2,3},{3,2},{4,5},{5,4},{6,7},{7,6},{8,9},{9,8},{10,11... | collective-permute-start | bytes 12582920 | tf_op jit(solution)/shard_map/ppermute | solution.py:24
  171.7 10.6 %collective-permute-start.13 = (bf16[512,4096]{1,0:T(8,128)(2,1)}, bf16[512,4096]{1,0:T(8,128)(2,1)}, u32[]{:S(2)}, u32[]{:S(2)}) collective-permute-start(bf16[512,4096]{1,0:T(8,128)(2,1)} %shard_map.132.mine_ref), channel_id=1, source_target_pairs={{0,1},{1,0},{2,3},{3,2},{4,5},{5,4},{6,7},{7,6},{8,9},{9,8},{10,11... | collective-permute-start | bytes 12582920 | tf_op jit(solution)/shard_map/ppermute | solution.py:24
  172.1 2.2 copy-start
  174.3 8.0 %copy-start.1 = (bf16[512,4096]{1,0:T(8,128)(2,1)S(1)}, bf16[512,4096]{1,0:T(8,128)(2,1)}, u32[]{:S(2)}) copy-start(bf16[512,4096]{1,0:T(8,128)(2,1)} %shard_map.132.mine_ref) | copy-start | bytes 12582916
  180.3 2.0 copy-start.3
  182.3 10.3 %copy-start.5 = (bf16[32,32,512]{2,1,0:T(8,128)(2,1)S(1)}, bf16[32,32,512]{2,1,0:T(8,128)(2,1)}, u32[]{:S(2)}) copy-start(bf16[32,32,512]{2,1,0:T(8,128)(2,1)} %query_ref.1) | copy-start | bytes 3145732
  182.3 10.3 %copy-start.7 = (s32[8]{0:T(128)S(1)}, s32[8]{0:T(128)}, u32[]{:S(2)}) copy-start(s32[8]{0:T(128)} %owner_ref.1) | copy-start | bytes 100
  (1 other events, 2.0 us)
Sparse Core Ops, SparseCore 0:
  24.3 95.6 all-gather.4
  122.1 70.4 all-gather.6
